TPU v7x, 32 devices: a whole 2x2x4 slice. The times are simulated.
32 devices in a mesh: rep: 2 (over core), dom: 16 (over z, y, x).
Axes of the slice: x: 2, y: 2, z: 4, core: 2. Of those that a mesh axis runs over, the one named last changes fastest.
Arguments:
- features: bfloat16 [2048, 512], P('dom'), may hold values from -6 to 6
- tiles: bfloat16 [2048, 128, 128], P(('rep', 'dom')), may hold values from -0.359375 to 0.359375
- tile_dest: int32 [2048, 1], P(('rep', 'dom')), may hold values from 0 to 15; in each aligned block of 64 rows (0 to 63, 64 to 127, ...) at most 8 rows name the same one
- tile_count: int32 [2048], P(('rep', 'dom')), may hold values from 16 to 128
- weight: bfloat16 [512, 512], replicated, may hold values from -0.25 to 0.25
- bias: float32 [512], replicated, may hold values from -3 to 3
- cotangent: bfloat16 [2048, 512], P('dom'), may hold values from -6 to 6
Outputs:
- activated: bfloat16 [2048, 512], P('dom', 'rep')
- weight_grad: float32 [512, 512], P(None, 'rep')
- feature_grad: bfloat16 [2048, 512], P('dom', 'rep')
Inputs may be any that keep to these rules, and one draw needn't show every extreme that they name: `tile_dest`: among the tiles of one device no block is named more than 8 times, and some block is named exactly 8 times.
All inputs are finite; a program needn't handle non-finite values.
Results may differ from a plain program's by a relative error of at most 0.02.
Values may be sent and summed in bfloat16 or wider, within the bound.
No kernel may reach another device: no remote copies, remote signals or barrier semaphores. Data moves between devices by JAX's collectives and lax.ppermute only.
A program may use at most 128 MiB of HBM per device.

v0:
```python
import jax
import jax.numpy as jnp
from jax import lax
from jax.sharding import PartitionSpec as P


def per_device(features, tiles, tile_dest, tile_count, weight, bias, cotangent):
    domains = lax.axis_size("dom")
    rep_index = lax.axis_index("rep")
    block = features.shape[0]
    width = features.shape[1]
    half = width // 2
    count_tiles = tiles.shape[0]
    slots = max(2, 2 * count_tiles // domains)
    dest = tile_dest[:, 0]
    scale = lax.rsqrt(tile_count.astype(jnp.float32))
    order = jnp.arange(count_tiles, dtype=jnp.int32)
    earlier = (dest[:, None] == dest[None, :]) & (order[None, :] < order[:, None])
    rank = jnp.sum(earlier.astype(jnp.int32), axis=1)
    slot_index = dest * slots + rank
    terms = (
        jnp.einsum("tij,jf->tif", tiles, features, preferred_element_type=jnp.float32)
        * scale[:, None, None]
    )
    send_buf = (
        jnp.zeros((domains * slots, block, width), jnp.bfloat16)
        .at[slot_index]
        .set(terms.astype(jnp.bfloat16))
    )
    received = lax.all_to_all(
        send_buf.reshape(domains, slots, block, width),
        "dom",
        split_axis=0,
        concat_axis=0,
        tiled=True,
    )
    partial_rows = jnp.sum(received, axis=(0, 1), dtype=jnp.float32)
    aggregated = lax.psum(partial_rows.astype(jnp.bfloat16), "rep")
    pre = jnp.dot(aggregated, weight, preferred_element_type=jnp.float32) + bias
    sig = jax.nn.sigmoid(pre)
    activated = lax.dynamic_slice_in_dim(pre * sig, rep_index * half, half, 1).astype(jnp.bfloat16)
    pre_grad = (cotangent.astype(jnp.float32) * sig * (1.0 + pre * (1.0 - sig))).astype(
        jnp.bfloat16
    )
    grad_half = lax.dynamic_slice_in_dim(pre_grad, rep_index * half, half, 1)
    weight_part = jnp.dot(aggregated.T, grad_half, preferred_element_type=jnp.float32)
    weight_grad = lax.psum(weight_part, "dom") / jnp.sqrt(jnp.float32(domains * block))
    row_grad = jnp.dot(pre_grad, weight.T, preferred_element_type=jnp.float32).astype(jnp.bfloat16)
    every_grad = lax.all_gather(row_grad, "dom", axis=0, tiled=True).reshape(domains, block, width)
    picked = every_grad[dest]
    back_terms = (
        jnp.einsum("tij,tif->tjf", tiles, picked, preferred_element_type=jnp.float32)
        * scale[:, None, None]
    )
    back_rows = jnp.sum(back_terms, axis=0)
    feature_grad = lax.psum_scatter(
        back_rows.astype(jnp.bfloat16), "rep", scatter_dimension=1, tiled=True
    )
    return (activated, weight_grad, feature_grad)


def solution(mesh):
    in_specs = (
        P("dom", None),
        P(("rep", "dom"), None, None),
        P(("rep", "dom"), None),
        P(("rep", "dom")),
        P(),
        P(),
        P("dom", None),
    )
    out_specs = (P("dom", "rep"), P(None, "rep"), P("dom", "rep"))
    return jax.shard_map(
        per_device, mesh=mesh, in_specs=in_specs, out_specs=out_specs, check_vma=False
    )
```

profile of v0, /device:TPU:0, one launch (start us, length us, event | category | flops | bytes accessed | tf_op | source)
XLA Modules:
  0.0 636.1 jit_solution(13985763096994442492)
XLA Ops:
  7.2 0.0 copy-start
  7.2 0.0 all-reduce.3.cloned.1.call-start
  7.2 1.0 convert_reduce_fusion
  8.2 0.7 fusion.7
  8.9 0.7 convert_rsqrt_fusion
  9.5 0.0 copy-done
  9.5 6.5 %multiply_convert_fusion = bf16[64,128,512]{2,1,0:T(8,128)(2,1)} fusion(bf16[64,128,128]{2,1,0:T(8,128)(2,1)S(1)} %copy-done, f32[64]{0:T(128)S(1)} %convert_rsqrt_fusion, bf16[128,512]{1,0:T(8,128)(2,1)} %param.7), kind=kOutput, calls=%fused_computation.3 | convolution fusion | flops 1082130432 | bytes 10617088 | tf_op jit(solution)/shard_map/tij,jf->tif/dot_general | solution.py:22
  16.0 5.9 broadcast_in_dim.2
  21.9 22.1 %scatter_fusion = bf16[128,128,512]{2,1,0:T(8,128)(2,1)} fusion(bf16[128,128,512]{2,1,0:T(8,128)(2,1)} %broadcast_in_dim.2, s32[64]{0:T(128)S(1)} %get-tuple-element.12, bf16[64,128,512]{2,1,0:T(8,128)(2,1)} %multiply_convert_fusion), kind=kCustom, calls=%fused_computation.1 | custom fusion | bytes 25166080 | tf_op jit(solution)/shard_map/scatter | solution.py:28
  44.0 371.9 %all_to_all.5 = bf16[16,8,128,512]{3,2,1,0:T(8,128)(2,1)} all-to-all(bf16[16,8,128,512]{3,2,1,0:T(8,128)(2,1)} %bitcast.25), channel_id=1, replica_groups=mesh['rep'=2,'dom'=16] {'dom'}, dimensions={0} | all-to-all | bytes 33554432 | tf_op jit(solution)/shard_map/all_to_all | solution.py:30
  415.9 0.0 copy-start.1
  415.9 0.0 copy-start.2
  415.9 0.0 copy-start.3
  415.9 9.7 %reduce_sum.34 = bf16[128,512]{1,0:T(8,128)(2,1)} reduce(bf16[16,8,128,512]{3,2,1,0:T(8,128)(2,1)} %all_to_all.5, bf16[]{:T(256)} %constant.12.clone.1), dimensions={0,1}, to_apply=%region_2.0 | reduce | flops 8323072 | bytes 16908290 | tf_op jit(solution)/shard_map/reduce_sum | solution.py:37
  425.6 0.0 all-reduce.3.cloned.1.call-update
  425.6 0.0 all-gather.2.cloned.1.call-start
  425.7 16.3 %all-reduce.3.cloned.1.call-done = bf16[128,512]{1,0:T(8,128)(2,1)} async-done(((bf16[128,512]{1,0:T(8,128)(2,1)}), bf16[128,512]{1,0:T(8,128)(2,1)}) %all-reduce.3.cloned.1.call-update) | async-done | bytes 131088 | tf_op jit(solution)/shard_map/psum | solution.py:38
  442.0 0.0 copy-done.1
  442.0 0.0 copy-done.2
  442.0 0.0 copy-done.3
  442.0 1.2 multiply_convert_fusion.1
  443.2 0.9 convolution_convert_fusion
  444.2 0.0 all-gather.2.cloned.1.call-update
  444.2 0.0 all-reduce.5.cloned.1.call-start
  444.3 2.0 fusion.2
  446.2 0.0 all-reduce.5.cloned.1.call-update
  446.3 0.0 reduce-scatter.2.cloned.1.call-start
  446.3 60.4 %all-gather.2.cloned.1.call-done = bf16[2048,512]{1,0:T(8,128)(2,1)} async-done(((bf16[128,512]{1,0:T(8,128)(2,1)}), bf16[2048,512]{1,0:T(8,128)(2,1)}) %all-gather.2.cloned.1.call-update) | async-done | bytes 2097168 | tf_op jit(solution)/shard_map/all_gather | solution.py:49
  506.7 7.1 %gather_fusion = bf16[64,128,512]{2,1,0:T(8,128)(2,1)} fusion(bf16[16,128,512]{2,1,0:T(8,128)(2,1)} %bitcast.26, s32[1024]{0:T(1024)S(1)} %pad_clamp_fusion), kind=kCustom, calls=%fused_computation | custom fusion | bytes 16777472 | tf_op jit(solution)/shard_map/gather | solution.py:50
  513.8 8.4 %multiply_reduce_fusion = bf16[512,128]{1,0:T(8,128)(2,1)} fusion(bf16[64,128,512]{2,1,0:T(8,128)(2,1)} %gather_fusion, bf16[64,128,128]{2,1,0:T(8,128)(2,1)S(1)} %copy-done, f32[64]{0:T(128)S(1)} %convert_rsqrt_fusion), kind=kOutput, calls=%fused_computation.2 | convolution fusion | flops 1082064896 | bytes 10617088 | tf_op jit(solution)/shard_map/tij,tif->tjf/dot_general | solution.py:52
  522.2 0.0 reduce-scatter.2.cloned.1.call-update
  522.2 0.7 fusion
  522.9 96.5 %all-reduce.5.cloned.1.call-done = f32[512,256]{1,0:T(8,128)} async-done(((f32[512,256]{1,0:T(8,128)}), f32[512,256]{1,0:T(8,128)}) %all-reduce.5.cloned.1.call-update) | async-done | bytes 524304 | tf_op jit(solution)/shard_map/psum | solution.py:47
  619.4 1.9 broadcast_multiply_fusion
  621.2 6.7 %reduce-scatter.2.cloned.1.call-done = bf16[128,256]{0,1:T(8,128)(2,1)} async-done(((bf16[128,512]{0,1:T(8,128)(2,1)}), bf16[128,256]{0,1:T(8,128)(2,1)}) %reduce-scatter.2.cloned.1.call-update) | async-done | bytes 65552 | tf_op jit(solution)/shard_map/reduce_scatter | solution.py:56
  628.0 1.6 copy.14
  (1 shorter events, 0.0 us)
Async XLA Ops:
  7.2 2.4 copy-start
  7.2 434.8 %all-reduce.3.cloned.1.call-start = ((), (), s32[]{:S(2)}) async-start(), calls=%async_computation.2 | async-start | bytes 262144 | tf_op jit(solution)/shard_map/psum | solution.py:38
  415.9 26.1 %copy-start.1 = (bf16[512,512]{1,0:T(8,128)(2,1)S(1)}, bf16[512,512]{1,0:T(8,128)(2,1)}, u32[]{:S(2)}) copy-start(bf16[512,512]{1,0:T(8,128)(2,1)} %param.11) | copy-start | bytes 1572868
  415.9 26.1 %copy-start.2 = (bf16[128,512]{1,0:T(8,128)(2,1)S(1)}, bf16[128,512]{1,0:T(8,128)(2,1)}, u32[]{:S(2)}) copy-start(bf16[128,512]{1,0:T(8,128)(2,1)} %param.13) | copy-start | bytes 393220
  415.9 26.1 %copy-start.3 = (f32[512]{0:T(512)S(1)}, f32[512]{0:T(512)}, u32[]{:S(2)}) copy-start(f32[512]{0:T(512)} %param.12) | copy-start | bytes 6148
  425.6 81.0 %all-gather.2.cloned.1.call-start = ((), (), s32[]{:S(2)}) async-start(), calls=%async_computation.4 | async-start | bytes 2228224 | tf_op jit(solution)/shard_map/all_gather | solution.py:49
  444.2 175.2 %all-reduce.5.cloned.1.call-start = ((), (), s32[]{:S(2)}) async-start(), calls=%async_computation.3 | async-start | bytes 1048576 | tf_op jit(solution)/shard_map/psum | solution.py:47
  446.3 181.7 %reduce-scatter.2.cloned.1.call-start = ((), (), s32[]{:S(2)}) async-start(), calls=%async_computation.5 | async-start | bytes 196608 | tf_op jit(solution)/shard_map/reduce_scatter | solution.py:56
Sparse Core Ops, SparseCore 0:
  425.8 16.1 all-reduce.2
  444.8 61.8 all-gather.1
  512.4 106.9 all-reduce.4
  621.5 6.4 reduce-scatter.1
where the time goes:
time: 637 us; the launch traced here: 636 us
  blocking collectives  372 us (58%)
  waiting for transfers between devices  180 us (28%)
  local copies, waits for them, and re-layouts  36.7 us (6%)
  matrix products  19 us (3%)
  other arithmetic  14.6 us (2%)
  between operations  13.8 us (2%)
    all_to_all x1, blocking collectives, per_device(): lax.all_to_all(send_buf.reshape(domains, slots, block, width), 'dom', spl...  372 us
    psum x1, waiting for transfers between devices, per_device(): lax.psum(weight_part, 'dom') / jnp.sqrt(jnp.float32(domains * block))  96.5 us
    all_gather x1, waiting for transfers between devices, per_device(): lax.all_gather(row_grad, 'dom', axis=0, tiled=True)  60.4 us
    scatter x1, local copies, waits for them, and re-layouts, per_device(): send_buf = jnp.zeros((domains * slots, block, width), jnp.bfloat16).at[sl...  22.1 us
    psum x1, waiting for transfers between devices, per_device(): aggregated = lax.psum(partial_rows.astype(jnp.bfloat16), 'rep')  16.3 us
  transfers between devices with their start and end apart: 4, of which 4 were waited for; matrix products, arithmetic and copies ran while one was open for 3% of the time, Pallas kernels for 0%

commit v1 on v0

v1 whole, which is shorter than its diff:
```python
import functools
import math

import jax
import jax.numpy as jnp
from jax import lax
from jax.experimental import pallas as pl
from jax.experimental.pallas import tpu as pltpu
from jax.sharding import PartitionSpec as P

F32, BF16 = jnp.float32, jnp.bfloat16
VMEM_LIMIT = 48 * 1024 * 1024


def place(group):
    dom = lax.axis_index("dom")
    return lax.axis_index("rep"), lax.div(dom, group), lax.rem(dom, group)


def rows(start, size):
    return pl.ds(pl.multiple_of(start * size, size), size)


def call(kernel, outs, scratch=(), smem=0, args=()):
    spec = pl.BlockSpec(memory_space=pltpu.VMEM)
    return pl.pallas_call(
        kernel,
        out_shape=[jax.ShapeDtypeStruct(shape, dtype) for shape, dtype in outs],
        in_specs=[pl.BlockSpec(memory_space=pltpu.SMEM)] * smem + [spec] * (len(args) - smem),
        out_specs=[spec] * len(outs),
        scratch_shapes=list(scratch),
        compiler_params=pltpu.CompilerParams(vmem_limit_bytes=VMEM_LIMIT),
    )(*args)


def combine_kernel(per_step, dest_ref, count_ref, tiles_ref, own_ref, send_ref, total):
    step = pl.program_id(0)
    half = total.shape[1] // 2

    @pl.when(step == 0)
    def _():
        total[...] = jnp.zeros_like(total)

    def add(i, carry):
        t = step * per_step + i
        count = jnp.full((1, total.shape[2]), count_ref[t], jnp.int32)
        scale = lax.rsqrt(count.astype(F32))
        d = dest_ref[t]
        total[d] = total[d] + tiles_ref[i].astype(F32) * scale
        return carry

    lax.fori_loop(0, per_step, add, 0, unroll=2)

    @pl.when(step == pl.num_programs(0) - 1)
    def _():
        rep = lax.axis_index("rep")
        own_ref[...] = total[:, rows(rep, half), :].astype(BF16)
        send_ref[...] = total[:, rows(1 - rep, half), :].astype(BF16)


def combine(dest, count, tiles, domains):
    number, block, _ = tiles.shape
    per_step = number // 4
    half = (domains, block // 2, block)
    whole = lambda i: (0, 0, 0)
    return pl.pallas_call(
        functools.partial(combine_kernel, per_step),
        grid=(number // per_step,),
        out_shape=[jax.ShapeDtypeStruct(half, BF16)] * 2,
        in_specs=[
            pl.BlockSpec(memory_space=pltpu.SMEM),
            pl.BlockSpec(memory_space=pltpu.SMEM),
            pl.BlockSpec((per_step, block, block), lambda i: (i, 0, 0)),
        ],
        out_specs=[pl.BlockSpec(half, whole)] * 2,
        scratch_shapes=[pltpu.VMEM((domains, block, block), F32)],
        compiler_params=pltpu.CompilerParams(vmem_limit_bytes=VMEM_LIMIT),
    )(dest, count, tiles)


def split_kernel(group, own_ref, got_ref, features_ref, *outs):
    rep, _, q = place(group)
    outer = own_ref.shape[0] // group
    for s in range(group):
        for z in range(outer):
            b = z * group + lax.bitwise_xor(q, s)
            outs[s][z] = (own_ref[b].astype(F32) + got_ref[b].astype(F32)).astype(BF16)
    width = features_ref.shape[1] // 2
    outs[group][...] = features_ref[:, rows(rep, width)]


def forward_kernel(group, *refs):
    own, got = refs[:group], refs[group : 2 * group]
    features = refs[2 * group : 3 * group]
    adjacency = refs[3 * group]
    outs = refs[3 * group + 1 :]
    rep, z, _ = place(group)
    outer, half, block = own[0].shape
    for t in range(outer):
        far = lax.bitwise_xor(z, t)
        for s in range(group):
            columns = slice(s * block, (s + 1) * block)
            adjacency[t, rows(rep, half), columns] = own[s][far]
            adjacency[t, rows(1 - rep, half), columns] = got[s][far]
    panel = jnp.concatenate([f[...] for f in features], axis=0)
    for t in range(outer):
        part = jnp.dot(adjacency[t], panel, preferred_element_type=F32)
        outs[t][...] = part.astype(outs[t].dtype)


def sum_kernel(scale, *refs):
    out = refs[-1]
    total = refs[0][...].astype(F32)
    for ref in refs[1:-1]:
        total = total + ref[...].astype(F32)
    out[...] = (total * scale if scale is not None else total).astype(out.dtype)


def dense_kernel(group, own_ref, got_ref, weight_ref, bias_ref, cotangent_ref, *refs):
    active_ref, row_grad_ref = refs[:2]
    outs = refs[2 : 2 + group]
    agg, pre_ref, grad, parts = refs[2 + group :]
    rep, _, q = place(group)
    width = own_ref.shape[1]
    agg[:, rows(rep, width)] = own_ref[...]
    agg[:, rows(1 - rep, width)] = got_ref[...]
    pre = jnp.dot(agg[...], weight_ref[...], preferred_element_type=F32) + bias_ref[...]
    sig = jax.nn.sigmoid(pre)
    pre_ref[...] = pre * sig
    active_ref[...] = pre_ref[:, rows(rep, width)].astype(BF16)
    slope = cotangent_ref[...].astype(F32) * sig * (1.0 + pre * (1.0 - sig))
    grad[...] = slope.astype(BF16)
    row_grad = lax.dot_general(
        grad[...], weight_ref[rows(rep, width), :], (((1,), (1,)), ((), ())), preferred_element_type=F32
    )
    row_grad_ref[...] = row_grad.astype(BF16)
    parts[...] = lax.dot_general(
        agg[...], grad[:, rows(rep, width)], (((0,), (0,)), ((), ())), preferred_element_type=F32
    )
    size = parts.shape[0] // group
    for s in range(group):
        outs[s][...] = parts[rows(lax.bitwise_xor(q, s), size), :].astype(outs[s].dtype)


def backward_kernel(group, adjacency, *refs):
    outer, block, _ = adjacency.shape
    grads, outs = refs[:outer], refs[outer:]
    for s in range(group):
        columns = slice(s * block, (s + 1) * block)
        total = jnp.zeros(outs[s].shape, F32)
        for t in range(outer):
            total = total + lax.dot_general(
                adjacency[t, :, columns], grads[t][...], (((0,), (0,)), ((), ())), preferred_element_type=F32
            )
        outs[s][...] = total.astype(outs[s].dtype)


def assemble_kernel(group, *refs):
    out = refs[-1]
    _, _, q = place(group)
    size = refs[0].shape[0]
    for s in range(group):
        out[rows(lax.bitwise_xor(q, s), size), :] = refs[s][...].astype(F32)


def per_device(features, tiles, tile_dest, tile_count, weight, bias, cotangent):
    domains = lax.axis_size("dom")
    group = 4
    outer = domains // group
    block, width = features.shape
    half = width // 2
    nodes = domains * block

    def rep_swap(x):
        return lax.ppermute(x, "rep", [(0, 1), (1, 0)])

    def inner_swap(x, s):
        return lax.ppermute(x, "dom", [(i, i ^ s) for i in range(domains)])

    def outer_swap(x, t):
        return lax.ppermute(x, "dom", [(i, i ^ (t * group)) for i in range(domains)])

    own, send = combine(tile_dest[:, 0], tile_count, tiles, domains)
    got = rep_swap(send)
    *cut, panel = call(
        functools.partial(split_kernel, group),
        [((outer, block // 2, block), BF16)] * group + [((block, half), BF16)],
        args=(own, got, features),
    )
    mine = [cut[0]] + [inner_swap(cut[s], s) for s in range(1, group)]
    panels = [panel] + [inner_swap(panel, s) for s in range(1, group)]
    others = [rep_swap(x) for x in mine]
    adjacency, *parts = call(
        functools.partial(forward_kernel, group),
        [((outer, block, group * block), BF16), ((block, half), F32)] + [((block, half), BF16)] * (outer - 1),
        args=(*mine, *others, *panels),
    )
    parts = [parts[0]] + [outer_swap(parts[t], t) for t in range(1, outer)]
    (agg,) = call(functools.partial(sum_kernel, None), [((block, half), BF16)], args=parts)
    activated, row_grad, *pieces = call(
        functools.partial(dense_kernel, group),
        [((block, half), BF16), ((block, half), BF16), ((width // group, half), F32)]
        + [((width // group, half), BF16)] * (group - 1),
        scratch=(
            pltpu.VMEM((block, width), BF16),
            pltpu.VMEM((block, width), F32),
            pltpu.VMEM((block, width), BF16),
            pltpu.VMEM((width, half), F32),
        ),
        args=(agg, rep_swap(agg), weight, bias.reshape(1, width), cotangent),
    )
    grads = [row_grad] + [outer_swap(row_grad, t) for t in range(1, outer)]
    pieces = [pieces[0]] + [inner_swap(pieces[s], s) for s in range(1, group)]
    back = call(
        functools.partial(backward_kernel, group),
        [((block, half), F32)] + [((block, half), BF16)] * (group - 1),
        args=(adjacency, *grads),
    )
    back = [back[0]] + [inner_swap(back[s], s) for s in range(1, group)]
    (piece,) = call(functools.partial(sum_kernel, None), [((width // group, half), BF16)], args=pieces)
    pieces = [piece] + [outer_swap(piece, t) for t in range(1, outer)]
    (piece,) = call(
        functools.partial(sum_kernel, 1.0 / math.sqrt(nodes)), [((width // group, half), BF16)], args=pieces
    )
    pieces = [piece] + [inner_swap(piece, s) for s in range(1, group)]
    (weight_grad,) = call(functools.partial(assemble_kernel, group), [((width, half), F32)], args=pieces)
    (feature_grad,) = call(functools.partial(sum_kernel, None), [((block, half), BF16)], args=back)
    return (activated, weight_grad, feature_grad)


def solution(mesh):
    in_specs = (
        P("dom", None),
        P(("rep", "dom"), None, None),
        P(("rep", "dom"), None),
        P(("rep", "dom")),
        P(),
        P(),
        P("dom", None),
    )
    out_specs = (P("dom", "rep"), P(None, "rep"), P("dom", "rep"))
    return jax.shard_map(
        per_device, mesh=mesh, in_specs=in_specs, out_specs=out_specs, check_vma=False
    )
```

time: 637 us -> 60 us (0.09)
  blocking collectives: 372 us -> 0 us
  waiting for transfers between devices: 180 us -> 16.8 us
  starting transfers between devices: 0.16 us -> 34 us
  local copies, waits for them, and re-layouts: 36.7 us -> 2.91 us
  matrix products: 19 us -> 0 us
  other arithmetic: 14.6 us -> 0 us
  between operations: 13.8 us -> 0.74 us
    all_to_all x1 -> x0, blocking collectives: 372 us -> none  [per_device(): lax.all_to_all(send_buf.reshape(domains, slots, block, width), 'dom', spl...]
    psum x2 -> x0, waiting for transfers between devices: 113 us -> none  [the longest x1 96.5 us: per_device(): lax.psum(weight_part, 'dom') / jnp.sqrt(jnp.float32(domains * block))]
    all_gather x1 -> x0, waiting for transfers between devices: 60.4 us -> none  [per_device(): lax.all_gather(row_grad, 'dom', axis=0, tiled=True)]
    ppermute x0 -> x30, starting transfers between devices: none -> 34 us  [the longest x15 19.5 us: inner_swap(): return lax.ppermute(x, 'dom', [(i, i ^ s) for i in range(domains)])]
    scatter x1 -> x0, local copies, waits for them, and re-layouts: 22.1 us -> none  [per_device(): send_buf = jnp.zeros((domains * slots, block, width), jnp.bfloat16).at[sl...]
    dot_general x5 -> x0, matrix products: 19 us -> none  [the longest x1 8.42 us: per_device(): jnp.einsum('tij,tif->tjf', tiles, picked, preferred_element_type=jnp.floa...]
    ppermute x0 -> x30, waiting for transfers between devices: none -> 16.8 us  [the longest x9 9.1 us: outer_swap(): return lax.ppermute(x, 'dom', [(i, i ^ t * group) for i in range(domains)])]
    reduce_sum x2 -> x0, other arithmetic: 10.7 us -> none  [the longest x1 9.7 us: per_device(): partial_rows = jnp.sum(received, axis=(0, 1), dtype=jnp.float32)]
  transfers between devices with their start and end apart: 4 -> 30, of which waited for: 4 -> 11; matrix products, arithmetic and copies ran while one was open for 3% -> 0% of each run, Pallas kernels for 0% -> 2%
where the time goes in v1:
time: 60 us; the launch traced here: 59.8 us
  starting transfers between devices  34 us (57%)
  waiting for transfers between devices  16.8 us (28%)
  Pallas kernels  5.31 us (9%)
  local copies, waits for them, and re-layouts  2.91 us (5%)
  between operations  0.74 us (1%)
    ppermute x15, starting transfers between devices, inner_swap(): return lax.ppermute(x, 'dom', [(i, i ^ s) for i in range(domains)])  19.5 us
    ppermute x9, starting transfers between devices, outer_swap(): return lax.ppermute(x, 'dom', [(i, i ^ t * group) for i in range(domains)])  13.5 us
    ppermute x9, waiting for transfers between devices, outer_swap(): return lax.ppermute(x, 'dom', [(i, i ^ t * group) for i in range(domains)])  9.1 us
    ppermute x15, waiting for transfers between devices, inner_swap(): return lax.ppermute(x, 'dom', [(i, i ^ s) for i in range(domains)])  5.3 us
    pallas_call x9, Pallas kernels, call(): pl.pallas_call(kernel, out_shape=[jax.ShapeDtypeStruct(shape, dtype) for...  3.7 us
    unnamed x14, local copies, waits for them, and re-layouts  2.91 us
    ppermute x6, waiting for transfers between devices, rep_swap(): return lax.ppermute(x, 'rep', [(0, 1), (1, 0)])  2.41 us
    pallas_call x1, Pallas kernels, combine(): pl.pallas_call(functools.partial(combine_kernel, per_step), grid=(number...  1.6 us
  transfers between devices with their start and end apart: 30, of which 11 were waited for; matrix products, arithmetic and copies ran while one was open for 0% of the time, Pallas kernels for 2%

profile of v1, /device:TPU:0, one launch (start us, length us, event | category | flops | bytes accessed | tf_op | source)
XLA Modules:
  0.0 59.8 jit_solution(817491891612202995)
XLA Ops:
  0.6 1.6 %copy-done = bf16[64,128,128]{2,1,0:T(8,128)(2,1)S(1)} copy-done((bf16[64,128,128]{2,1,0:T(8,128)(2,1)S(1)}, bf16[64,128,128]{2,1,0:T(8,128)(2,1)}, u32[]{:S(2)}) %copy-start) | copy-done | bytes 2097176
  2.2 0.7 %copy-done.5 = s32[64,1]{0,1:T(1,128)S(1)} copy-done((s32[64,1]{0,1:T(1,128)S(1)}, s32[64,1]{0,1:T(1,128)}, u32[]{:S(2)}) %copy-start.5) | copy-done | bytes 280
  2.9 0.7 %copy-done.6 = s32[64]{0:T(128)S(1)} copy-done((s32[64]{0:T(128)S(1)}, s32[64]{0:T(128)}, u32[]{:S(2)}) %copy-start.6) | copy-done | bytes 280
  3.5 1.6 %shard_map.94 = (bf16[16,64,128]{2,1,0:T(8,128)(2,1)S(1)}, bf16[16,64,128]{2,1,0:T(8,128)(2,1)S(1)}) custom-call(s32[64]{0:T(128)S(1)} %bitcast.3, s32[64]{0:T(128)S(1)} %copy-done.6, bf16[64,128,128]{2,1,0:T(8,128)(2,1)S(1)} %copy-done), custom_call_target="tpu_custom_call" | custom-call | tf_op jit(solution)/shard_map/pallas_call | solution.py:66
  5.2 0.5 collective-permute-start
  5.7 1.2 %collective-permute-done.got_ref = bf16[16,64,128]{2,1,0:T(8,128)(2,1)S(1)} collective-permute-done((bf16[16,64,128]{2,1,0:T(8,128)(2,1)S(1)}, bf16[16,64,128]{2,1,0:T(8,128)(2,1)S(1)}, u32[]{:S(2)}, u32[]{:S(2)}) %collective-permute-start) | collective-permute-done | bytes 262176 | tf_op jit(solution)/shard_map/ppermute | solution.py:175
  6.8 0.1 shard_map.95
  6.9 2.9 %collective-permute-start.1 = (bf16[4,64,128]{2,1,0:T(8,128)(2,1)S(1)}, bf16[4,64,128]{2,1,0:T(8,128)(2,1)S(1)}, u32[]{:S(2)}, u32[]{:S(2)}) collective-permute-start(bf16[4,64,128]{2,1,0:T(8,128)(2,1)S(1)} %get-tuple-element.28), channel_id=1, source_target_pairs={{0,1},{1,0},{2,3},{3,2},{4,5},{5,4},{6,7},{7,6},{8,9},{9,8},{10,11... | collective-permute-start | bytes 196616 | tf_op jit(solution)/shard_map/ppermute | solution.py:178
  9.8 1.5 %collective-permute-start.2 = (bf16[4,64,128]{2,1,0:T(8,128)(2,1)S(1)}, bf16[4,64,128]{2,1,0:T(8,128)(2,1)S(1)}, u32[]{:S(2)}, u32[]{:S(2)}) collective-permute-start(bf16[4,64,128]{2,1,0:T(8,128)(2,1)S(1)} %get-tuple-element.29), channel_id=1, source_target_pairs={{0,2},{1,3},{2,0},{3,1},{4,6},{5,7},{6,4},{7,5},{8,10},{9,11},{10,... | collective-permute-start | bytes 196616 | tf_op jit(solution)/shard_map/ppermute | solution.py:178
  11.4 2.9 %collective-permute-start.10 = (bf16[128,256]{1,0:T(8,128)(2,1)S(1)}, bf16[128,256]{1,0:T(8,128)(2,1)S(1)}, u32[]{:S(2)}, u32[]{:S(2)}) collective-permute-start(bf16[128,256]{1,0:T(8,128)(2,1)S(1)} %get-tuple-element.31.refs_8_), channel_id=1, source_target_pairs={{0,3},{1,2},{2,1},{3,0},{4,7},{5,6},{6,5},{7,4},{8,11},{9,10},{10,... | collective-permute-start | bytes 196616 | tf_op jit(solution)/shard_map/ppermute | solution.py:178
  14.3 0.5 collective-permute-start.9
  14.8 1.0 %collective-permute-start.8 = (bf16[128,256]{1,0:T(8,128)(2,1)S(1)}, bf16[128,256]{1,0:T(8,128)(2,1)S(1)}, u32[]{:S(2)}, u32[]{:S(2)}) collective-permute-start(bf16[128,256]{1,0:T(8,128)(2,1)S(1)} %get-tuple-element.31.refs_8_), channel_id=1, source_target_pairs={{0,1},{1,0},{2,3},{3,2},{4,5},{5,4},{6,7},{7,6},{8,9},{9,8},{10,11... | collective-permute-start | bytes 196616 | tf_op jit(solution)/shard_map/ppermute | solution.py:178
  15.8 1.3 %collective-permute-done.3.refs_3_ = bf16[4,64,128]{2,1,0:T(8,128)(2,1)S(1)} collective-permute-done((bf16[4,64,128]{2,1,0:T(8,128)(2,1)S(1)}, bf16[4,64,128]{2,1,0:T(8,128)(2,1)S(1)}, u32[]{:S(2)}, u32[]{:S(2)}) %collective-permute-start.3) | collective-permute-done | bytes 65568 | tf_op jit(solution)/shard_map/ppermute | solution.py:178
  17.1 0.5 collective-permute-start.6
  17.6 0.3 collective-permute-done.10.refs_11_
  17.8 1.3 %collective-permute-done.9.refs_10_ = bf16[128,256]{1,0:T(8,128)(2,1)S(1)} collective-permute-done((bf16[128,256]{1,0:T(8,128)(2,1)S(1)}, bf16[128,256]{1,0:T(8,128)(2,1)S(1)}, u32[]{:S(2)}, u32[]{:S(2)}) %collective-permute-start.9) | collective-permute-done | bytes 65568 | tf_op jit(solution)/shard_map/ppermute | solution.py:178
  19.2 0.4 shard_map.96
  19.6 1.8 %collective-permute-start.11 = (bf16[128,256]{1,0:T(8,128)(2,1)S(1)}, bf16[128,256]{1,0:T(8,128)(2,1)S(1)}, u32[]{:S(2)}, u32[]{:S(2)}) collective-permute-start(bf16[128,256]{1,0:T(8,128)(2,1)S(1)} %get-tuple-element.33), channel_id=1, source_target_pairs={{0,4},{1,5},{2,6},{3,7},{4,0},{5,1},{6,2},{7,3},{8,12},{9,13},{10,... | collective-permute-start | bytes 196616 | tf_op jit(solution)/shard_map/ppermute | solution.py:181
  21.4 2.6 %collective-permute-start.12 = (bf16[128,256]{1,0:T(8,128)(2,1)S(1)}, bf16[128,256]{1,0:T(8,128)(2,1)S(1)}, u32[]{:S(2)}, u32[]{:S(2)}) collective-permute-start(bf16[128,256]{1,0:T(8,128)(2,1)S(1)} %get-tuple-element.34), channel_id=1, source_target_pairs={{0,8},{1,9},{2,10},{3,11},{4,12},{5,13},{6,14},{7,15},{8,0},{9,1},... | collective-permute-start | bytes 196616 | tf_op jit(solution)/shard_map/ppermute | solution.py:181
  24.0 0.0 collective-permute-start.13
  24.1 4.9 %collective-permute-done.12.refs_2_ = bf16[128,256]{1,0:T(8,128)(2,1)S(1)} collective-permute-done((bf16[128,256]{1,0:T(8,128)(2,1)S(1)}, bf16[128,256]{1,0:T(8,128)(2,1)S(1)}, u32[]{:S(2)}, u32[]{:S(2)}) %collective-permute-start.12) | collective-permute-done | bytes 65568 | tf_op jit(solution)/shard_map/ppermute | solution.py:181
  28.9 1.3 %collective-permute-done.13.refs_3_ = bf16[128,256]{1,0:T(8,128)(2,1)S(1)} collective-permute-done((bf16[128,256]{1,0:T(8,128)(2,1)S(1)}, bf16[128,256]{1,0:T(8,128)(2,1)S(1)}, u32[]{:S(2)}, u32[]{:S(2)}) %collective-permute-start.13) | collective-permute-done | bytes 65568 | tf_op jit(solution)/shard_map/ppermute | solution.py:181
  30.2 0.1 collective-permute-start.14
  30.3 1.2 %collective-permute-done.14.got_ref = bf16[128,256]{1,0:T(8,128)(2,1)S(1)} collective-permute-done((bf16[128,256]{1,0:T(8,128)(2,1)S(1)}, bf16[128,256]{1,0:T(8,128)(2,1)S(1)}, u32[]{:S(2)}, u32[]{:S(2)}) %collective-permute-start.14) | collective-permute-done | bytes 65568 | tf_op jit(solution)/shard_map/ppermute | solution.py:175
  31.6 1.1 %shard_map.98 = (bf16[128,256]{1,0:T(8,128)(2,1)}, bf16[128,256]{1,0:T(8,128)(2,1)S(1)}, f32[128,256]{1,0:T(8,128)S(1)}, bf16[128,256]{1,0:T(8,128)(2,1)S(1)}, b...) custom-call(bf16[128,256]{1,0:T(8,128)(2,1)S(1)} %shard_map.97.own_ref, ...), custom_call_target="tpu_custom_call" | custom-call | tf_op jit(solution)/shard_map/pallas_call | solution.py:26
  32.7 0.9 %collective-permute-start.15 = (bf16[128,256]{1,0:T(8,128)(2,1)S(1)}, bf16[128,256]{1,0:T(8,128)(2,1)S(1)}, u32[]{:S(2)}, u32[]{:S(2)}) collective-permute-start(bf16[128,256]{1,0:T(8,128)(2,1)S(1)} %get-tuple-element.38), channel_id=1, source_target_pairs={{0,1},{1,0},{2,3},{3,2},{4,5},{5,4},{6,7},{7,6},{8,9},{9,8},{10,11... | collective-permute-start | bytes 196616 | tf_op jit(solution)/shard_map/ppermute | solution.py:178
  33.5 1.7 %collective-permute-start.16 = (bf16[128,256]{1,0:T(8,128)(2,1)S(1)}, bf16[128,256]{1,0:T(8,128)(2,1)S(1)}, u32[]{:S(2)}, u32[]{:S(2)}) collective-permute-start(bf16[128,256]{1,0:T(8,128)(2,1)S(1)} %get-tuple-element.39), channel_id=1, source_target_pairs={{0,2},{1,3},{2,0},{3,1},{4,6},{5,7},{6,4},{7,5},{8,10},{9,11},{10,... | collective-permute-start | bytes 196616 | tf_op jit(solution)/shard_map/ppermute | solution.py:178
  35.2 0.9 %collective-permute-start.17 = (bf16[128,256]{1,0:T(8,128)(2,1)S(1)}, bf16[128,256]{1,0:T(8,128)(2,1)S(1)}, u32[]{:S(2)}, u32[]{:S(2)}) collective-permute-start(bf16[128,256]{1,0:T(8,128)(2,1)S(1)} %get-tuple-element.40), channel_id=1, source_target_pairs={{0,3},{1,2},{2,1},{3,0},{4,7},{5,6},{6,5},{7,4},{8,11},{9,10},{10,... | collective-permute-start | bytes 196616 | tf_op jit(solution)/shard_map/ppermute | solution.py:178
  36.2 1.9 %collective-permute-start.26 = (bf16[128,256]{1,0:T(8,128)(2,1)S(1)}, bf16[128,256]{1,0:T(8,128)(2,1)S(1)}, u32[]{:S(2)}, u32[]{:S(2)}) collective-permute-start(bf16[128,256]{1,0:T(8,128)(2,1)S(1)} %get-tuple-element.42.refs_0_), channel_id=1, source_target_pairs={{0,12},{1,13},{2,14},{3,15},{4,8},{5,9},{6,10},{7,11},{8,4},{9,5},... | collective-permute-start | bytes 196616 | tf_op jit(solution)/shard_map/ppermute | solution.py:181
  38.1 0.3 collective-permute-start.25
  38.4 2.2 %collective-permute-start.24 = (bf16[128,256]{1,0:T(8,128)(2,1)S(1)}, bf16[128,256]{1,0:T(8,128)(2,1)S(1)}, u32[]{:S(2)}, u32[]{:S(2)}) collective-permute-start(bf16[128,256]{1,0:T(8,128)(2,1)S(1)} %get-tuple-element.42.refs_0_), channel_id=1, source_target_pairs={{0,4},{1,5},{2,6},{3,7},{4,0},{5,1},{6,2},{7,3},{8,12},{9,13},{10,... | collective-permute-start | bytes 196616 | tf_op jit(solution)/shard_map/ppermute | solution.py:181
  40.6 2.0 %collective-permute-start.20 = (bf16[128,256]{1,0:T(8,128)(2,1)S(1)}, bf16[128,256]{1,0:T(8,128)(2,1)S(1)}, u32[]{:S(2)}, u32[]{:S(2)}) collective-permute-start(bf16[128,256]{1,0:T(8,128)(2,1)S(1)} %shard_map.99.refs_0_), channel_id=1, source_target_pairs={{0,12},{1,13},{2,14},{3,15},{4,8},{5,9},{6,10},{7,11},{8,4},{9,5},... | collective-permute-start | bytes 196616 | tf_op jit(solution)/shard_map/ppermute | solution.py:181
  42.6 0.2 collective-permute-start.19
  42.8 2.4 %collective-permute-start.18 = (bf16[128,256]{1,0:T(8,128)(2,1)S(1)}, bf16[128,256]{1,0:T(8,128)(2,1)S(1)}, u32[]{:S(2)}, u32[]{:S(2)}) collective-permute-start(bf16[128,256]{1,0:T(8,128)(2,1)S(1)} %shard_map.99.refs_0_), channel_id=1, source_target_pairs={{0,4},{1,5},{2,6},{3,7},{4,0},{5,1},{6,2},{7,3},{8,12},{9,13},{10,... | collective-permute-start | bytes 196616 | tf_op jit(solution)/shard_map/ppermute | solution.py:181
  45.3 3.0 %collective-permute-done.25.refs_2_ = bf16[128,256]{1,0:T(8,128)(2,1)S(1)} collective-permute-done((bf16[128,256]{1,0:T(8,128)(2,1)S(1)}, bf16[128,256]{1,0:T(8,128)(2,1)S(1)}, u32[]{:S(2)}, u32[]{:S(2)}) %collective-permute-start.25) | collective-permute-done | bytes 65568 | tf_op jit(solution)/shard_map/ppermute | solution.py:181
  48.3 0.5 shard_map.102
  48.7 0.9 %collective-permute-start.27 = (bf16[128,256]{1,0:T(8,128)(2,1)S(1)}, bf16[128,256]{1,0:T(8,128)(2,1)S(1)}, u32[]{:S(2)}, u32[]{:S(2)}) collective-permute-start(bf16[128,256]{1,0:T(8,128)(2,1)S(1)} %get-tuple-element.44), channel_id=1, source_target_pairs={{0,1},{1,0},{2,3},{3,2},{4,5},{5,4},{6,7},{7,6},{8,9},{9,8},{10,11... | collective-permute-start | bytes 196616 | tf_op jit(solution)/shard_map/ppermute | solution.py:178
  49.6 1.7 %collective-permute-start.28 = (bf16[128,256]{1,0:T(8,128)(2,1)S(1)}, bf16[128,256]{1,0:T(8,128)(2,1)S(1)}, u32[]{:S(2)}, u32[]{:S(2)}) collective-permute-start(bf16[128,256]{1,0:T(8,128)(2,1)S(1)} %get-tuple-element.45), channel_id=1, source_target_pairs={{0,2},{1,3},{2,0},{3,1},{4,6},{5,7},{6,4},{7,5},{8,10},{9,11},{10,... | collective-permute-start | bytes 196616 | tf_op jit(solution)/shard_map/ppermute | solution.py:178
  51.3 1.0 %collective-permute-start.29 = (bf16[128,256]{1,0:T(8,128)(2,1)S(1)}, bf16[128,256]{1,0:T(8,128)(2,1)S(1)}, u32[]{:S(2)}, u32[]{:S(2)}) collective-permute-start(bf16[128,256]{1,0:T(8,128)(2,1)S(1)} %get-tuple-element.46), channel_id=1, source_target_pairs={{0,3},{1,2},{2,1},{3,0},{4,7},{5,6},{6,5},{7,4},{8,11},{9,10},{10,... | collective-permute-start | bytes 196616 | tf_op jit(solution)/shard_map/ppermute | solution.py:178
  52.3 2.0 %collective-permute-start.23 = (bf16[128,256]{1,0:T(8,128)(2,1)S(1)}, bf16[128,256]{1,0:T(8,128)(2,1)S(1)}, u32[]{:S(2)}, u32[]{:S(2)}) collective-permute-start(bf16[128,256]{1,0:T(8,128)(2,1)S(1)} %shard_map.100.refs_0_), channel_id=1, source_target_pairs={{0,3},{1,2},{2,1},{3,0},{4,7},{5,6},{6,5},{7,4},{8,11},{9,10},{10,... | collective-permute-start | bytes 196616 | tf_op jit(solution)/shard_map/ppermute | solution.py:178
  54.4 0.3 collective-permute-start.22
  54.7 1.2 %collective-permute-start.21 = (bf16[128,256]{1,0:T(8,128)(2,1)S(1)}, bf16[128,256]{1,0:T(8,128)(2,1)S(1)}, u32[]{:S(2)}, u32[]{:S(2)}) collective-permute-start(bf16[128,256]{1,0:T(8,128)(2,1)S(1)} %shard_map.100.refs_0_), channel_id=1, source_target_pairs={{0,1},{1,0},{2,3},{3,2},{4,5},{5,4},{6,7},{7,6},{8,9},{9,8},{10,11... | collective-permute-start | bytes 196616 | tf_op jit(solution)/shard_map/ppermute | solution.py:178
  55.9 1.0 %collective-permute-done.29.refs_3_ = bf16[128,256]{1,0:T(8,128)(2,1)S(1)} collective-permute-done((bf16[128,256]{1,0:T(8,128)(2,1)S(1)}, bf16[128,256]{1,0:T(8,128)(2,1)S(1)}, u32[]{:S(2)}, u32[]{:S(2)}) %collective-permute-start.29) | collective-permute-done | bytes 65568 | tf_op jit(solution)/shard_map/ppermute | solution.py:178
  56.9 0.7 %shard_map.103 = bf16[128,256]{1,0:T(8,128)(2,1)} custom-call(f32[128,256]{1,0:T(8,128)S(1)} %get-tuple-element.43.refs_0_, bf16[128,256]{1,0:T(8,128)(2,1)S(1)} %collective-permute-done.27.refs_1_, bf16[128,256]{1,0:T(8,128)(2,1)S(1)} %collective-permute-done.28.refs_2_, bf16[128,256]{1,0:T(8,128)(2,1)S(1)} %collective-permute-done.29.refs_3_), custom_call_target="tpu_custom_call" | custom-call | tf_op jit(solution)/shard_map/pallas_call | solution.py:26
  57.5 0.0 collective-permute-done.23.refs_3_
  57.6 1.1 %collective-permute-done.22.refs_2_ = bf16[128,256]{1,0:T(8,128)(2,1)S(1)} collective-permute-done((bf16[128,256]{1,0:T(8,128)(2,1)S(1)}, bf16[128,256]{1,0:T(8,128)(2,1)S(1)}, u32[]{:S(2)}, u32[]{:S(2)}) %collective-permute-start.22) | collective-permute-done | bytes 65568 | tf_op jit(solution)/shard_map/ppermute | solution.py:178
  58.6 0.3 collective-permute-done.21.refs_1_
  59.0 0.8 %shard_map.101 = f32[512,256]{1,0:T(8,128)} custom-call(bf16[128,256]{1,0:T(8,128)(2,1)S(1)} %shard_map.100.refs_0_, bf16[128,256]{1,0:T(8,128)(2,1)S(1)} %collective-permute-done.21.refs_1_, bf16[128,256]{1,0:T(8,128)(2,1)S(1)} %collective-permute-done.22.refs_2_, bf16[128,256]{1,0:T(8,128)(2,1)S(1)} %collective-permute-done.23.refs_3_), custom_call_target="tpu_custom_call" | custom-call | tf_op jit(solution)/shard_map/pallas_call | solution.py:26
  (36 shorter events, 0.2 us)
Async XLA Ops:
  0.6 1.6 %copy-start = (bf16[64,128,128]{2,1,0:T(8,128)(2,1)S(1)}, bf16[64,128,128]{2,1,0:T(8,128)(2,1)}, u32[]{:S(2)}) copy-start(bf16[64,128,128]{2,1,0:T(8,128)(2,1)} %tiles_ref.1) | copy-start | bytes 6291460
  2.2 0.7 %copy-start.5 = (s32[64,1]{0,1:T(1,128)S(1)}, s32[64,1]{0,1:T(1,128)}, u32[]{:S(2)}) copy-start(s32[64,1]{0,1:T(1,128)} %param.9) | copy-start | bytes 772
  2.9 0.7 %copy-start.6 = (s32[64]{0:T(128)S(1)}, s32[64]{0:T(128)}, u32[]{:S(2)}) copy-start(s32[64]{0:T(128)} %count_ref.1) | copy-start | bytes 772
  3.5 3.3 %copy-start.2 = (bf16[128,512]{1,0:T(8,128)(2,1)S(1)}, bf16[128,512]{1,0:T(8,128)(2,1)}, u32[]{:S(2)}) copy-start(bf16[128,512]{1,0:T(8,128)(2,1)} %features_ref.1) | copy-start | bytes 393220
  3.5 28.0 %copy-start.1 = (bf16[512,512]{1,0:T(8,128)(2,1)S(1)}, bf16[512,512]{1,0:T(8,128)(2,1)}, u32[]{:S(2)}) copy-start(bf16[512,512]{1,0:T(8,128)(2,1)} %weight_ref.1) | copy-start | bytes 1572868
  3.5 28.0 %copy-start.3 = (bf16[128,512]{1,0:T(8,128)(2,1)S(1)}, bf16[128,512]{1,0:T(8,128)(2,1)}, u32[]{:S(2)}) copy-start(bf16[128,512]{1,0:T(8,128)(2,1)} %cotangent_ref.1) | copy-start | bytes 393220
  3.5 28.0 %copy-start.4 = (f32[512]{0:T(512)S(1)}, f32[512]{0:T(512)}, u32[]{:S(2)}) copy-start(f32[512]{0:T(512)} %param.12) | copy-start | bytes 6148
  5.2 1.7 %collective-permute-start = (bf16[16,64,128]{2,1,0:T(8,128)(2,1)S(1)}, bf16[16,64,128]{2,1,0:T(8,128)(2,1)S(1)}, u32[]{:S(2)}, u32[]{:S(2)}) collective-permute-start(bf16[16,64,128]{2,1,0:T(8,128)(2,1)S(1)} %get-tuple-element.26), channel_id=1, source_target_pairs={{0,16},{16,0},{1,17},{17,1},{2,18},{18,2},{3,19},{19,3},{4,20},{20... | collective-permute-start | bytes 786440 | tf_op jit(solution)/shard_map/ppermute | solution.py:175
  6.9 7.4 %collective-permute-start.1 = (bf16[4,64,128]{2,1,0:T(8,128)(2,1)S(1)}, bf16[4,64,128]{2,1,0:T(8,128)(2,1)S(1)}, u32[]{:S(2)}, u32[]{:S(2)}) collective-permute-start(bf16[4,64,128]{2,1,0:T(8,128)(2,1)S(1)} %get-tuple-element.28), channel_id=1, source_target_pairs={{0,1},{1,0},{2,3},{3,2},{4,5},{5,4},{6,7},{7,6},{8,9},{9,8},{10,11... | collective-permute-start | bytes 196616 | tf_op jit(solution)/shard_map/ppermute | solution.py:178
  9.8 5.0 %collective-permute-start.2 = (bf16[4,64,128]{2,1,0:T(8,128)(2,1)S(1)}, bf16[4,64,128]{2,1,0:T(8,128)(2,1)S(1)}, u32[]{:S(2)}, u32[]{:S(2)}) collective-permute-start(bf16[4,64,128]{2,1,0:T(8,128)(2,1)S(1)} %get-tuple-element.29), channel_id=1, source_target_pairs={{0,2},{1,3},{2,0},{3,1},{4,6},{5,7},{6,4},{7,5},{8,10},{9,11},{10,... | collective-permute-start | bytes 196616 | tf_op jit(solution)/shard_map/ppermute | solution.py:178
  11.4 5.7 %collective-permute-start.3 = (bf16[4,64,128]{2,1,0:T(8,128)(2,1)S(1)}, bf16[4,64,128]{2,1,0:T(8,128)(2,1)S(1)}, u32[]{:S(2)}, u32[]{:S(2)}) collective-permute-start(bf16[4,64,128]{2,1,0:T(8,128)(2,1)S(1)} %get-tuple-element.30), channel_id=1, source_target_pairs={{0,3},{1,2},{2,1},{3,0},{4,7},{5,6},{6,5},{7,4},{8,11},{9,10},{10,... | collective-permute-start | bytes 196616 | tf_op jit(solution)/shard_map/ppermute | solution.py:178
  11.4 5.7 %collective-permute-start.4 = (bf16[4,64,128]{2,1,0:T(8,128)(2,1)S(1)}, bf16[4,64,128]{2,1,0:T(8,128)(2,1)S(1)}, u32[]{:S(2)}, u32[]{:S(2)}) collective-permute-start(bf16[4,64,128]{2,1,0:T(8,128)(2,1)S(1)} %get-tuple-element.27.refs_0_), channel_id=1, source_target_pairs={{0,16},{16,0},{1,17},{17,1},{2,18},{18,2},{3,19},{19,3},{4,20},{20... | collective-permute-start | bytes 196616 | tf_op jit(solution)/shard_map/ppermute | solution.py:175
  11.4 6.4 %collective-permute-start.10 = (bf16[128,256]{1,0:T(8,128)(2,1)S(1)}, bf16[128,256]{1,0:T(8,128)(2,1)S(1)}, u32[]{:S(2)}, u32[]{:S(2)}) collective-permute-start(bf16[128,256]{1,0:T(8,128)(2,1)S(1)} %get-tuple-element.31.refs_8_), channel_id=1, source_target_pairs={{0,3},{1,2},{2,1},{3,0},{4,7},{5,6},{6,5},{7,4},{8,11},{9,10},{10,... | collective-permute-start | bytes 196616 | tf_op jit(solution)/shard_map/ppermute | solution.py:178
  14.3 4.9 %collective-permute-start.9 = (bf16[128,256]{1,0:T(8,128)(2,1)S(1)}, bf16[128,256]{1,0:T(8,128)(2,1)S(1)}, u32[]{:S(2)}, u32[]{:S(2)}) collective-permute-start(bf16[128,256]{1,0:T(8,128)(2,1)S(1)} %get-tuple-element.31.refs_8_), channel_id=1, source_target_pairs={{0,2},{1,3},{2,0},{3,1},{4,6},{5,7},{6,4},{7,5},{8,10},{9,11},{10,... | collective-permute-start | bytes 196616 | tf_op jit(solution)/shard_map/ppermute | solution.py:178
  14.8 4.4 %collective-permute-start.8 = (bf16[128,256]{1,0:T(8,128)(2,1)S(1)}, bf16[128,256]{1,0:T(8,128)(2,1)S(1)}, u32[]{:S(2)}, u32[]{:S(2)}) collective-permute-start(bf16[128,256]{1,0:T(8,128)(2,1)S(1)} %get-tuple-element.31.refs_8_), channel_id=1, source_target_pairs={{0,1},{1,0},{2,3},{3,2},{4,5},{5,4},{6,7},{7,6},{8,9},{9,8},{10,11... | collective-permute-start | bytes 196616 | tf_op jit(solution)/shard_map/ppermute | solution.py:178
  17.0 2.1 %collective-permute-start.5 = (bf16[4,64,128]{2,1,0:T(8,128)(2,1)S(1)}, bf16[4,64,128]{2,1,0:T(8,128)(2,1)S(1)}, u32[]{:S(2)}, u32[]{:S(2)}) collective-permute-start(bf16[4,64,128]{2,1,0:T(8,128)(2,1)S(1)} %collective-permute-done.1.refs_1_), channel_id=1, source_target_pairs={{0,16},{16,0},{1,17},{17,1},{2,18},{18,2},{3,19},{19,3},{4,20},{20... | collective-permute-start | bytes 196616 | tf_op jit(solution)/shard_map/ppermute | solution.py:175
  17.1 2.1 %collective-permute-start.6 = (bf16[4,64,128]{2,1,0:T(8,128)(2,1)S(1)}, bf16[4,64,128]{2,1,0:T(8,128)(2,1)S(1)}, u32[]{:S(2)}, u32[]{:S(2)}) collective-permute-start(bf16[4,64,128]{2,1,0:T(8,128)(2,1)S(1)} %collective-permute-done.2.refs_2_), channel_id=1, source_target_pairs={{0,16},{16,0},{1,17},{17,1},{2,18},{18,2},{3,19},{19,3},{4,20},{20... | collective-permute-start | bytes 196616 | tf_op jit(solution)/shard_map/ppermute | solution.py:175
  17.8 1.4 %collective-permute-start.7 = (bf16[4,64,128]{2,1,0:T(8,128)(2,1)S(1)}, bf16[4,64,128]{2,1,0:T(8,128)(2,1)S(1)}, u32[]{:S(2)}, u32[]{:S(2)}) collective-permute-start(bf16[4,64,128]{2,1,0:T(8,128)(2,1)S(1)} %collective-permute-done.3.refs_3_), channel_id=1, source_target_pairs={{0,16},{16,0},{1,17},{17,1},{2,18},{18,2},{3,19},{19,3},{4,20},{20... | collective-permute-start | bytes 196616 | tf_op jit(solution)/shard_map/ppermute | solution.py:175
  19.6 4.5 %collective-permute-start.11 = (bf16[128,256]{1,0:T(8,128)(2,1)S(1)}, bf16[128,256]{1,0:T(8,128)(2,1)S(1)}, u32[]{:S(2)}, u32[]{:S(2)}) collective-permute-start(bf16[128,256]{1,0:T(8,128)(2,1)S(1)} %get-tuple-element.33), channel_id=1, source_target_pairs={{0,4},{1,5},{2,6},{3,7},{4,0},{5,1},{6,2},{7,3},{8,12},{9,13},{10,... | collective-permute-start | bytes 196616 | tf_op jit(solution)/shard_map/ppermute | solution.py:181
  21.4 7.5 %collective-permute-start.12 = (bf16[128,256]{1,0:T(8,128)(2,1)S(1)}, bf16[128,256]{1,0:T(8,128)(2,1)S(1)}, u32[]{:S(2)}, u32[]{:S(2)}) collective-permute-start(bf16[128,256]{1,0:T(8,128)(2,1)S(1)} %get-tuple-element.34), channel_id=1, source_target_pairs={{0,8},{1,9},{2,10},{3,11},{4,12},{5,13},{6,14},{7,15},{8,0},{9,1},... | collective-permute-start | bytes 196616 | tf_op jit(solution)/shard_map/ppermute | solution.py:181
  24.0 6.2 %collective-permute-start.13 = (bf16[128,256]{1,0:T(8,128)(2,1)S(1)}, bf16[128,256]{1,0:T(8,128)(2,1)S(1)}, u32[]{:S(2)}, u32[]{:S(2)}) collective-permute-start(bf16[128,256]{1,0:T(8,128)(2,1)S(1)} %get-tuple-element.35), channel_id=1, source_target_pairs={{0,12},{1,13},{2,14},{3,15},{4,8},{5,9},{6,10},{7,11},{8,4},{9,5},... | collective-permute-start | bytes 196616 | tf_op jit(solution)/shard_map/ppermute | solution.py:181
  30.2 1.3 %collective-permute-start.14 = (bf16[128,256]{1,0:T(8,128)(2,1)S(1)}, bf16[128,256]{1,0:T(8,128)(2,1)S(1)}, u32[]{:S(2)}, u32[]{:S(2)}) collective-permute-start(bf16[128,256]{1,0:T(8,128)(2,1)S(1)} %shard_map.97.own_ref), channel_id=1, source_target_pairs={{0,16},{16,0},{1,17},{17,1},{2,18},{18,2},{3,19},{19,3},{4,20},{20... | collective-permute-start | bytes 196616 | tf_op jit(solution)/shard_map/ppermute | solution.py:175
  32.7 5.7 %collective-permute-start.15 = (bf16[128,256]{1,0:T(8,128)(2,1)S(1)}, bf16[128,256]{1,0:T(8,128)(2,1)S(1)}, u32[]{:S(2)}, u32[]{:S(2)}) collective-permute-start(bf16[128,256]{1,0:T(8,128)(2,1)S(1)} %get-tuple-element.38), channel_id=1, source_target_pairs={{0,1},{1,0},{2,3},{3,2},{4,5},{5,4},{6,7},{7,6},{8,9},{9,8},{10,11... | collective-permute-start | bytes 196616 | tf_op jit(solution)/shard_map/ppermute | solution.py:178
  33.5 7.0 %collective-permute-start.16 = (bf16[128,256]{1,0:T(8,128)(2,1)S(1)}, bf16[128,256]{1,0:T(8,128)(2,1)S(1)}, u32[]{:S(2)}, u32[]{:S(2)}) collective-permute-start(bf16[128,256]{1,0:T(8,128)(2,1)S(1)} %get-tuple-element.39), channel_id=1, source_target_pairs={{0,2},{1,3},{2,0},{3,1},{4,6},{5,7},{6,4},{7,5},{8,10},{9,11},{10,... | collective-permute-start | bytes 196616 | tf_op jit(solution)/shard_map/ppermute | solution.py:178
  35.2 5.3 %collective-permute-start.17 = (bf16[128,256]{1,0:T(8,128)(2,1)S(1)}, bf16[128,256]{1,0:T(8,128)(2,1)S(1)}, u32[]{:S(2)}, u32[]{:S(2)}) collective-permute-start(bf16[128,256]{1,0:T(8,128)(2,1)S(1)} %get-tuple-element.40), channel_id=1, source_target_pairs={{0,3},{1,2},{2,1},{3,0},{4,7},{5,6},{6,5},{7,4},{8,11},{9,10},{10,... | collective-permute-start | bytes 196616 | tf_op jit(solution)/shard_map/ppermute | solution.py:178
  36.2 6.7 %collective-permute-start.26 = (bf16[128,256]{1,0:T(8,128)(2,1)S(1)}, bf16[128,256]{1,0:T(8,128)(2,1)S(1)}, u32[]{:S(2)}, u32[]{:S(2)}) collective-permute-start(bf16[128,256]{1,0:T(8,128)(2,1)S(1)} %get-tuple-element.42.refs_0_), channel_id=1, source_target_pairs={{0,12},{1,13},{2,14},{3,15},{4,8},{5,9},{6,10},{7,11},{8,4},{9,5},... | collective-permute-start | bytes 196616 | tf_op jit(solution)/shard_map/ppermute | solution.py:181
  38.1 10.2 %collective-permute-start.25 = (bf16[128,256]{1,0:T(8,128)(2,1)S(1)}, bf16[128,256]{1,0:T(8,128)(2,1)S(1)}, u32[]{:S(2)}, u32[]{:S(2)}) collective-permute-start(bf16[128,256]{1,0:T(8,128)(2,1)S(1)} %get-tuple-element.42.refs_0_), channel_id=1, source_target_pairs={{0,8},{1,9},{2,10},{3,11},{4,12},{5,13},{6,14},{7,15},{8,0},{9,1},... | collective-permute-start | bytes 196616 | tf_op jit(solution)/shard_map/ppermute | solution.py:181
  38.4 9.8 %collective-permute-start.24 = (bf16[128,256]{1,0:T(8,128)(2,1)S(1)}, bf16[128,256]{1,0:T(8,128)(2,1)S(1)}, u32[]{:S(2)}, u32[]{:S(2)}) collective-permute-start(bf16[128,256]{1,0:T(8,128)(2,1)S(1)} %get-tuple-element.42.refs_0_), channel_id=1, source_target_pairs={{0,4},{1,5},{2,6},{3,7},{4,0},{5,1},{6,2},{7,3},{8,12},{9,13},{10,... | collective-permute-start | bytes 196616 | tf_op jit(solution)/shard_map/ppermute | solution.py:181
  40.6 10.7 %collective-permute-start.20 = (bf16[128,256]{1,0:T(8,128)(2,1)S(1)}, bf16[128,256]{1,0:T(8,128)(2,1)S(1)}, u32[]{:S(2)}, u32[]{:S(2)}) collective-permute-start(bf16[128,256]{1,0:T(8,128)(2,1)S(1)} %shard_map.99.refs_0_), channel_id=1, source_target_pairs={{0,12},{1,13},{2,14},{3,15},{4,8},{5,9},{6,10},{7,11},{8,4},{9,5},... | collective-permute-start | bytes 196616 | tf_op jit(solution)/shard_map/ppermute | solution.py:181
  42.6 9.7 %collective-permute-start.19 = (bf16[128,256]{1,0:T(8,128)(2,1)S(1)}, bf16[128,256]{1,0:T(8,128)(2,1)S(1)}, u32[]{:S(2)}, u32[]{:S(2)}) collective-permute-start(bf16[128,256]{1,0:T(8,128)(2,1)S(1)} %shard_map.99.refs_0_), channel_id=1, source_target_pairs={{0,8},{1,9},{2,10},{3,11},{4,12},{5,13},{6,14},{7,15},{8,0},{9,1},... | collective-permute-start | bytes 196616 | tf_op jit(solution)/shard_map/ppermute | solution.py:181
  42.8 9.5 %collective-permute-start.18 = (bf16[128,256]{1,0:T(8,128)(2,1)S(1)}, bf16[128,256]{1,0:T(8,128)(2,1)S(1)}, u32[]{:S(2)}, u32[]{:S(2)}) collective-permute-start(bf16[128,256]{1,0:T(8,128)(2,1)S(1)} %shard_map.99.refs_0_), channel_id=1, source_target_pairs={{0,4},{1,5},{2,6},{3,7},{4,0},{5,1},{6,2},{7,3},{8,12},{9,13},{10,... | collective-permute-start | bytes 196616 | tf_op jit(solution)/shard_map/ppermute | solution.py:181
  48.7 6.0 %collective-permute-start.27 = (bf16[128,256]{1,0:T(8,128)(2,1)S(1)}, bf16[128,256]{1,0:T(8,128)(2,1)S(1)}, u32[]{:S(2)}, u32[]{:S(2)}) collective-permute-start(bf16[128,256]{1,0:T(8,128)(2,1)S(1)} %get-tuple-element.44), channel_id=1, source_target_pairs={{0,1},{1,0},{2,3},{3,2},{4,5},{5,4},{6,7},{7,6},{8,9},{9,8},{10,11... | collective-permute-start | bytes 196616 | tf_op jit(solution)/shard_map/ppermute | solution.py:178
  49.6 6.3 %collective-permute-start.28 = (bf16[128,256]{1,0:T(8,128)(2,1)S(1)}, bf16[128,256]{1,0:T(8,128)(2,1)S(1)}, u32[]{:S(2)}, u32[]{:S(2)}) collective-permute-start(bf16[128,256]{1,0:T(8,128)(2,1)S(1)} %get-tuple-element.45), channel_id=1, source_target_pairs={{0,2},{1,3},{2,0},{3,1},{4,6},{5,7},{6,4},{7,5},{8,10},{9,11},{10,... | collective-permute-start | bytes 196616 | tf_op jit(solution)/shard_map/ppermute | solution.py:178
  51.3 5.6 %collective-permute-start.29 = (bf16[128,256]{1,0:T(8,128)(2,1)S(1)}, bf16[128,256]{1,0:T(8,128)(2,1)S(1)}, u32[]{:S(2)}, u32[]{:S(2)}) collective-permute-start(bf16[128,256]{1,0:T(8,128)(2,1)S(1)} %get-tuple-element.46), channel_id=1, source_target_pairs={{0,3},{1,2},{2,1},{3,0},{4,7},{5,6},{6,5},{7,4},{8,11},{9,10},{10,... | collective-permute-start | bytes 196616 | tf_op jit(solution)/shard_map/ppermute | solution.py:178
  52.3 5.3 %collective-permute-start.23 = (bf16[128,256]{1,0:T(8,128)(2,1)S(1)}, bf16[128,256]{1,0:T(8,128)(2,1)S(1)}, u32[]{:S(2)}, u32[]{:S(2)}) collective-permute-start(bf16[128,256]{1,0:T(8,128)(2,1)S(1)} %shard_map.100.refs_0_), channel_id=1, source_target_pairs={{0,3},{1,2},{2,1},{3,0},{4,7},{5,6},{6,5},{7,4},{8,11},{9,10},{10,... | collective-permute-start | bytes 196616 | tf_op jit(solution)/shard_map/ppermute | solution.py:178
  54.4 4.3 %collective-permute-start.22 = (bf16[128,256]{1,0:T(8,128)(2,1)S(1)}, bf16[128,256]{1,0:T(8,128)(2,1)S(1)}, u32[]{:S(2)}, u32[]{:S(2)}) collective-permute-start(bf16[128,256]{1,0:T(8,128)(2,1)S(1)} %shard_map.100.refs_0_), channel_id=1, source_target_pairs={{0,2},{1,3},{2,0},{3,1},{4,6},{5,7},{6,4},{7,5},{8,10},{9,11},{10,... | collective-permute-start | bytes 196616 | tf_op jit(solution)/shard_map/ppermute | solution.py:178
  54.7 4.3 %collective-permute-start.21 = (bf16[128,256]{1,0:T(8,128)(2,1)S(1)}, bf16[128,256]{1,0:T(8,128)(2,1)S(1)}, u32[]{:S(2)}, u32[]{:S(2)}) collective-permute-start(bf16[128,256]{1,0:T(8,128)(2,1)S(1)} %shard_map.100.refs_0_), channel_id=1, source_target_pairs={{0,1},{1,0},{2,3},{3,2},{4,5},{5,4},{6,7},{7,6},{8,9},{9,8},{10,11... | collective-permute-start | bytes 196616 | tf_op jit(solution)/shard_map/ppermute | solution.py:178

commit v2 on v1

v2 whole, which is shorter than its diff:
```python
import functools
import math

import jax
import jax.numpy as jnp
from jax import lax
from jax.experimental import pallas as pl
from jax.experimental.pallas import tpu as pltpu
from jax.sharding import PartitionSpec as P

F32, BF16 = jnp.float32, jnp.bfloat16
VMEM_LIMIT = 48 * 1024 * 1024
SHORT = pl.CostEstimate(flops=1024, bytes_accessed=1024, transcendentals=0)
CHUNKS = 4


def place(group):
    dom = lax.axis_index("dom")
    return lax.axis_index("rep"), lax.div(dom, group), lax.rem(dom, group)


def rows(start, size):
    return pl.ds(pl.multiple_of(start * size, size), size)


def call(kernel, outs, scratch=(), smem=0, args=()):
    spec = pl.BlockSpec(memory_space=pltpu.VMEM)
    return pl.pallas_call(
        kernel,
        out_shape=[jax.ShapeDtypeStruct(shape, dtype) for shape, dtype in outs],
        in_specs=[pl.BlockSpec(memory_space=pltpu.SMEM)] * smem + [spec] * (len(args) - smem),
        out_specs=[spec] * len(outs),
        scratch_shapes=list(scratch),
        compiler_params=pltpu.CompilerParams(vmem_limit_bytes=VMEM_LIMIT),
        cost_estimate=SHORT,
    )(*args)


def combine_kernel(dest_hbm, count_hbm, tiles_hbm, own_ref, send_ref, total, tiles, dest, count, sems):
    half = total.shape[1] // 2
    size = tiles.shape[0] // CHUNKS
    copies = [
        pltpu.make_async_copy(dest_hbm, dest, sems.at[CHUNKS]),
        pltpu.make_async_copy(count_hbm, count, sems.at[CHUNKS + 1]),
    ]
    for c in range(CHUNKS):
        part = pl.ds(c * size, size)
        copies.append(pltpu.make_async_copy(tiles_hbm.at[part], tiles.at[part], sems.at[c]))
    for copy in copies:
        copy.start()
    total[...] = jnp.zeros_like(total)
    copies[0].wait()
    copies[1].wait()

    def add(t, carry):
        scale = lax.rsqrt(jnp.full((1, total.shape[2]), count[t], jnp.int32).astype(F32))
        d = dest[t]
        total[d] = total[d] + tiles[t].astype(F32) * scale
        return carry

    for c in range(CHUNKS):
        copies[2 + c].wait()
        lax.fori_loop(c * size, (c + 1) * size, add, 0, unroll=2)
    rep = lax.axis_index("rep")
    own_ref[...] = total[:, rows(rep, half), :].astype(BF16)
    send_ref[...] = total[:, rows(1 - rep, half), :].astype(BF16)


def combine(dest, count, tiles, domains):
    number, block, _ = tiles.shape
    half = (domains, block // 2, block)
    return pl.pallas_call(
        combine_kernel,
        out_shape=[jax.ShapeDtypeStruct(half, BF16)] * 2,
        in_specs=[pl.BlockSpec(memory_space=pltpu.HBM)] * 3,
        out_specs=[pl.BlockSpec(memory_space=pltpu.VMEM)] * 2,
        scratch_shapes=[
            pltpu.VMEM((domains, block, block), F32),
            pltpu.VMEM(tiles.shape, BF16),
            pltpu.SMEM((number,), jnp.int32),
            pltpu.SMEM((number,), jnp.int32),
            pltpu.SemaphoreType.DMA((CHUNKS + 2,)),
        ],
        compiler_params=pltpu.CompilerParams(vmem_limit_bytes=VMEM_LIMIT),
        cost_estimate=SHORT,
    )(*[pltpu.with_memory_space_constraint(x, pltpu.HBM) for x in (dest, count, tiles)])


def split_kernel(group, near, own_ref, got_ref, features_ref, *outs):
    rep, _, q = place(group)
    outer = own_ref.shape[0] // group
    _, half, block = own_ref.shape
    for i, s in enumerate(near):
        for z in range(outer):
            b = z * group + lax.bitwise_xor(q, s)
            outs[i][z * half : (z + 1) * half] = (own_ref[b].astype(F32) + got_ref[b].astype(F32)).astype(BF16)
    parts = features_ref.shape[1] // 2 // block
    for i in range(parts):
        piece = features_ref[:, rows(rep * parts + i, block)]
        at = outer * half + i * block
        for s in range(1, group):
            outs[s][at : at + block] = piece


def forward_kernel(group, outer, near, far, *refs):
    own = [refs[near.index(s)] for s in range(group)]
    got = [refs[group + near.index(s)] for s in range(group)]
    features_ref, adjacency = refs[2 * group : 2 * group + 2]
    outs, panel = refs[2 * group + 2 : -1], refs[-1]
    rep, z, _ = place(group)
    block, width = features_ref.shape
    half, side = block // 2, width // 2
    for t in range(outer):
        at = pl.ds(pl.multiple_of(lax.bitwise_xor(z, t) * half, half), half)
        for s in range(group):
            columns = slice(s * block, (s + 1) * block)
            adjacency[t, rows(rep, half), columns] = own[s][at, :]
            adjacency[t, rows(1 - rep, half), columns] = got[s][at, :]
    panel[:block, :] = features_ref[:, rows(rep, side)]
    for s in range(1, group):
        for i in range(side // block):
            start = outer * half + i * block
            panel[s * block : (s + 1) * block, i * block : (i + 1) * block] = own[s][start : start + block, :]
    for i, t in enumerate(far):
        part = jnp.dot(adjacency[t], panel[...], preferred_element_type=F32)
        outs[i][...] = part.astype(outs[i].dtype)


def sum_kernel(scale, *refs):
    out = refs[-1]
    total = refs[0][...].astype(F32)
    for ref in refs[1:-1]:
        total = total + ref[...].astype(F32)
    out[...] = (total * scale if scale is not None else total).astype(out.dtype)


def dense_kernel(group, near, own_ref, got_ref, weight_ref, bias_ref, cotangent_ref, *refs):
    active_ref, row_grad_ref = refs[:2]
    outs = refs[2 : 2 + group]
    agg, pre_ref, grad, parts = refs[2 + group :]
    rep, _, q = place(group)
    width = own_ref.shape[1]
    agg[:, rows(rep, width)] = own_ref[...]
    agg[:, rows(1 - rep, width)] = got_ref[...]
    pre = jnp.dot(agg[...], weight_ref[...], preferred_element_type=F32) + bias_ref[...]
    sig = jax.nn.sigmoid(pre)
    pre_ref[...] = pre * sig
    active_ref[...] = pre_ref[:, rows(rep, width)].astype(BF16)
    slope = cotangent_ref[...].astype(F32) * sig * (1.0 + pre * (1.0 - sig))
    grad[...] = slope.astype(BF16)
    row_grad = lax.dot_general(
        grad[...], weight_ref[rows(rep, width), :], (((1,), (1,)), ((), ())), preferred_element_type=F32
    )
    row_grad_ref[...] = row_grad.astype(BF16)
    parts[...] = lax.dot_general(
        agg[...], grad[:, rows(rep, width)], (((0,), (0,)), ((), ())), preferred_element_type=F32
    )
    size = parts.shape[0] // group
    for i, s in enumerate(near):
        outs[i][...] = parts[rows(lax.bitwise_xor(q, s), size), :].astype(outs[i].dtype)


def backward_kernel(group, near, far, adjacency, *refs):
    outer, block, _ = adjacency.shape
    grads, outs = refs[:outer], refs[outer:]
    for i, s in enumerate(near):
        columns = slice(s * block, (s + 1) * block)
        total = jnp.zeros(outs[i].shape, F32)
        for j, t in enumerate(far):
            total = total + lax.dot_general(
                adjacency[t, :, columns], grads[j][...], (((0,), (0,)), ((), ())), preferred_element_type=F32
            )
        outs[i][...] = total.astype(outs[i].dtype)


def assemble_kernel(near, *refs):
    out = refs[-1]
    _, _, q = place(len(near))
    size = refs[0].shape[0]
    for i, s in enumerate(near):
        out[rows(lax.bitwise_xor(q, s), size), :] = refs[i][...].astype(F32)


def per_device(features, tiles, tile_dest, tile_count, weight, bias, cotangent):
    domains = lax.axis_size("dom")
    group = 4
    outer = domains // group
    block, width = features.shape
    half = width // 2
    nodes = domains * block

    near = [0, group - 1, *range(1, group - 1)]
    far = [0, *range(outer // 2, outer), *range(1, outer // 2)]

    near_back, far_back = [0, *near[:0:-1]], [0, *far[:0:-1]]

    def rep_swap(x):
        return lax.ppermute(x, "rep", [(0, 1), (1, 0)])

    def inner_swap(x, s):
        return lax.ppermute(x, "dom", [(i, i ^ s) for i in range(domains)])

    def outer_swap(x, t):
        return lax.ppermute(x, "dom", [(i, i ^ (t * group)) for i in range(domains)])

    own, send = combine(tile_dest[:, 0], tile_count, tiles, domains)
    cut_rows = outer * block // 2
    cut = call(
        functools.partial(split_kernel, group, near),
        [((cut_rows, block), BF16)] + [((cut_rows + half, block), BF16)] * (group - 1),
        args=(own, rep_swap(send), features),
    )
    mine = [inner_swap(cut[i], s) if s else cut[i] for i, s in enumerate(near)]
    others = [rep_swap(x) for x in mine]
    adjacency, *parts = call(
        functools.partial(forward_kernel, group, outer, near, far),
        [((outer, block, group * block), BF16), ((block, half), F32)] + [((block, half), BF16)] * (outer - 1),
        scratch=(pltpu.VMEM((group * block, half), BF16),),
        args=(*mine, *others, features),
    )
    parts = [outer_swap(parts[i], t) if t else parts[i] for i, t in enumerate(far)]
    (agg,) = call(functools.partial(sum_kernel, None), [((block, half), BF16)], args=parts)
    activated, row_grad, *pieces = call(
        functools.partial(dense_kernel, group, near),
        [((block, half), BF16), ((block, half), BF16), ((width // group, half), F32)]
        + [((width // group, half), BF16)] * (group - 1),
        scratch=(
            pltpu.VMEM((block, width), BF16),
            pltpu.VMEM((block, width), F32),
            pltpu.VMEM((block, width), BF16),
            pltpu.VMEM((width, half), F32),
        ),
        args=(agg, rep_swap(agg), weight, bias.reshape(1, width), cotangent),
    )
    pieces = [inner_swap(pieces[i], s) if s else pieces[i] for i, s in enumerate(near)]
    (piece,) = call(functools.partial(sum_kernel, None), [((width // group, half), BF16)], args=pieces)
    grads = [outer_swap(row_grad, t) if t else row_grad for t in far_back]
    back = call(
        functools.partial(backward_kernel, group, near, far_back),
        [((block, half), F32)] + [((block, half), BF16)] * (group - 1),
        args=(adjacency, *grads),
    )
    back = [inner_swap(back[i], s) if s else back[i] for i, s in enumerate(near)]
    pieces = [outer_swap(piece, t) if t else piece for t in far_back]
    (piece,) = call(
        functools.partial(sum_kernel, 1.0 / math.sqrt(nodes)), [((width // group, half), BF16)], args=pieces
    )
    pieces = [inner_swap(piece, s) if s else piece for s in near_back]
    (weight_grad,) = call(functools.partial(assemble_kernel, near_back), [((width, half), F32)], args=pieces)
    (feature_grad,) = call(functools.partial(sum_kernel, None), [((block, half), BF16)], args=back)
    return (activated, weight_grad, feature_grad)


def solution(mesh):
    in_specs = (
        P("dom", None),
        P(("rep", "dom"), None, None),
        P(("rep", "dom"), None),
        P(("rep", "dom")),
        P(),
        P(),
        P("dom", None),
    )
    out_specs = (P("dom", "rep"), P(None, "rep"), P("dom", "rep"))
    return jax.shard_map(
        per_device, mesh=mesh, in_specs=in_specs, out_specs=out_specs, check_vma=False
    )
```

time: 60 us -> 55 us (0.917)
  starting transfers between devices: 34 us -> 28 us
  waiting for transfers between devices: 16.8 us -> 20.4 us
  local copies, waits for them, and re-layouts: 2.91 us -> 0.02 us
    ppermute x15 -> x12, starting transfers between devices: 19.5 us -> 14.7 us  [inner_swap(): return lax.ppermute(x, 'dom', [(i, i ^ s) for i in range(domains)])]
    ppermute x15 -> x12, waiting for transfers between devices: 5.3 us -> 9.46 us  [inner_swap(): return lax.ppermute(x, 'dom', [(i, i ^ s) for i in range(domains)])]
    unnamed x14 -> x8, local copies, waits for them, and re-layouts: 2.91 us -> 0.02 us
    ppermute x9, waiting for transfers between devices: 9.1 us -> 7.28 us  [outer_swap(): return lax.ppermute(x, 'dom', [(i, i ^ t * group) for i in range(domains)])]
    ppermute x9, starting transfers between devices: 13.5 us -> 12.1 us  [outer_swap(): return lax.ppermute(x, 'dom', [(i, i ^ t * group) for i in range(domains)])]
    ppermute x6, waiting for transfers between devices: 2.41 us -> 3.66 us  [rep_swap(): return lax.ppermute(x, 'rep', [(0, 1), (1, 0)])]
  transfers between devices with their start and end apart: 30 -> 27, of which waited for: 11 -> 13; matrix products, arithmetic and copies ran while one was open for 0% -> 0% of each run, Pallas kernels for 2% -> 2%
where the time goes in v2:
time: 55 us; the launch traced here: 54.9 us
  starting transfers between devices  28 us (51%)
  waiting for transfers between devices  20.4 us (37%)
  Pallas kernels  5.73 us (10%)
  between operations  0.75 us (1%)
    ppermute x12, starting transfers between devices, inner_swap(): return lax.ppermute(x, 'dom', [(i, i ^ s) for i in range(domains)])  14.7 us
    ppermute x9, starting transfers between devices, outer_swap(): return lax.ppermute(x, 'dom', [(i, i ^ t * group) for i in range(domains)])  12.1 us
    ppermute x12, waiting for transfers between devices, inner_swap(): return lax.ppermute(x, 'dom', [(i, i ^ s) for i in range(domains)])  9.46 us
    ppermute x9, waiting for transfers between devices, outer_swap(): return lax.ppermute(x, 'dom', [(i, i ^ t * group) for i in range(domains)])  7.28 us
    pallas_call x9, Pallas kernels, call(): pl.pallas_call(kernel, out_shape=[jax.ShapeDtypeStruct(shape, dtype) for...  3.72 us
    ppermute x6, waiting for transfers between devices, rep_swap(): return lax.ppermute(x, 'rep', [(0, 1), (1, 0)])  3.66 us
    pallas_call x1, Pallas kernels, combine(): pl.pallas_call(combine_kernel, out_shape=[jax.ShapeDtypeStruct(half, BF16...  2.01 us
    ppermute x6, starting transfers between devices, rep_swap(): return lax.ppermute(x, 'rep', [(0, 1), (1, 0)])  1.11 us
  transfers between devices with their start and end apart: 27, of which 13 were waited for; matrix products, arithmetic and copies ran while one was open for 0% of the time, Pallas kernels for 2%

profile of v2, /device:TPU:0, one launch (start us, length us, event | category | flops | bytes accessed | tf_op | source)
XLA Modules:
  0.0 54.9 jit_solution(1775491804381356117)
XLA Ops:
  0.7 2.0 %shard_map.94 = (bf16[16,64,128]{2,1,0:T(8,128)(2,1)S(1)}, bf16[16,64,128]{2,1,0:T(8,128)(2,1)S(1)}) custom-call(s32[64]{0:T(128)} %bitcast.3, s32[64]{0:T(128)} %count_hbm.1, bf16[64,128,128]{2,1,0:T(8,128)(2,1)} %tiles_hbm.1), custom_call_target="tpu_custom_call" | custom-call | flops 1024 | bytes 1024 | tf_op jit(solution)/shard_map/pallas_call | solution.py:72
  2.7 0.5 collective-permute-start
  3.2 1.2 %collective-permute-done.got_ref = bf16[16,64,128]{2,1,0:T(8,128)(2,1)S(1)} collective-permute-done((bf16[16,64,128]{2,1,0:T(8,128)(2,1)S(1)}, bf16[16,64,128]{2,1,0:T(8,128)(2,1)S(1)}, u32[]{:S(2)}, u32[]{:S(2)}) %collective-permute-start) | collective-permute-done | bytes 262176 | tf_op jit(solution)/shard_map/ppermute | solution.py:198
  4.4 0.1 shard_map.95
  4.4 3.9 %collective-permute-start.1 = (bf16[512,128]{1,0:T(8,128)(2,1)S(1)}, bf16[512,128]{1,0:T(8,128)(2,1)S(1)}, u32[]{:S(2)}, u32[]{:S(2)}) collective-permute-start(bf16[512,128]{1,0:T(8,128)(2,1)S(1)} %get-tuple-element.27), channel_id=1, source_target_pairs={{0,3},{1,2},{2,1},{3,0},{4,7},{5,6},{6,5},{7,4},{8,11},{9,10},{10,... | collective-permute-start | bytes 393224 | tf_op jit(solution)/shard_map/ppermute | solution.py:201
  8.3 0.5 collective-permute-start.2
  8.9 0.1 collective-permute-start.3
  9.0 3.6 %collective-permute-done.1.refs_1_ = bf16[512,128]{1,0:T(8,128)(2,1)S(1)} collective-permute-done((bf16[512,128]{1,0:T(8,128)(2,1)S(1)}, bf16[512,128]{1,0:T(8,128)(2,1)S(1)}, u32[]{:S(2)}, u32[]{:S(2)}) %collective-permute-start.1) | collective-permute-done | bytes 131104 | tf_op jit(solution)/shard_map/ppermute | solution.py:201
  12.6 0.0 collective-permute-start.5
  12.6 2.6 %collective-permute-done.2.refs_2_ = bf16[512,128]{1,0:T(8,128)(2,1)S(1)} collective-permute-done((bf16[512,128]{1,0:T(8,128)(2,1)S(1)}, bf16[512,128]{1,0:T(8,128)(2,1)S(1)}, u32[]{:S(2)}, u32[]{:S(2)}) %collective-permute-start.2) | collective-permute-done | bytes 131104 | tf_op jit(solution)/shard_map/ppermute | solution.py:201
  15.2 0.0 collective-permute-start.6
  15.2 0.5 collective-permute-start.7
  15.7 0.0 collective-permute-start.4
  15.7 1.3 %collective-permute-done.4.refs_4_ = bf16[256,128]{1,0:T(8,128)(2,1)S(1)} collective-permute-done((bf16[256,128]{1,0:T(8,128)(2,1)S(1)}, bf16[256,128]{1,0:T(8,128)(2,1)S(1)}, u32[]{:S(2)}, u32[]{:S(2)}) %collective-permute-start.4) | collective-permute-done | bytes 65568 | tf_op jit(solution)/shard_map/ppermute | solution.py:198
  17.0 0.0 collective-permute-done.5.refs_5_
  17.0 0.4 shard_map.96
  17.4 2.6 %collective-permute-start.8 = (bf16[128,256]{1,0:T(8,128)(2,1)S(1)}, bf16[128,256]{1,0:T(8,128)(2,1)S(1)}, u32[]{:S(2)}, u32[]{:S(2)}) collective-permute-start(bf16[128,256]{1,0:T(8,128)(2,1)S(1)} %get-tuple-element.31), channel_id=1, source_target_pairs={{0,8},{1,9},{2,10},{3,11},{4,12},{5,13},{6,14},{7,15},{8,0},{9,1},... | collective-permute-start | bytes 196616 | tf_op jit(solution)/shard_map/ppermute | solution.py:204
  20.1 1.3 %collective-permute-start.9 = (bf16[128,256]{1,0:T(8,128)(2,1)S(1)}, bf16[128,256]{1,0:T(8,128)(2,1)S(1)}, u32[]{:S(2)}, u32[]{:S(2)}) collective-permute-start(bf16[128,256]{1,0:T(8,128)(2,1)S(1)} %get-tuple-element.32), channel_id=1, source_target_pairs={{0,12},{1,13},{2,14},{3,15},{4,8},{5,9},{6,10},{7,11},{8,4},{9,5},... | collective-permute-start | bytes 196616 | tf_op jit(solution)/shard_map/ppermute | solution.py:204
  21.4 0.2 collective-permute-start.10
  21.7 2.9 %collective-permute-done.8.refs_1_ = bf16[128,256]{1,0:T(8,128)(2,1)S(1)} collective-permute-done((bf16[128,256]{1,0:T(8,128)(2,1)S(1)}, bf16[128,256]{1,0:T(8,128)(2,1)S(1)}, u32[]{:S(2)}, u32[]{:S(2)}) %collective-permute-start.8) | collective-permute-done | bytes 65568 | tf_op jit(solution)/shard_map/ppermute | solution.py:204
  24.5 2.0 %collective-permute-done.9.refs_2_ = bf16[128,256]{1,0:T(8,128)(2,1)S(1)} collective-permute-done((bf16[128,256]{1,0:T(8,128)(2,1)S(1)}, bf16[128,256]{1,0:T(8,128)(2,1)S(1)}, u32[]{:S(2)}, u32[]{:S(2)}) %collective-permute-start.9) | collective-permute-done | bytes 65568 | tf_op jit(solution)/shard_map/ppermute | solution.py:204
  26.5 0.3 collective-permute-done.10.refs_3_
  26.9 0.1 collective-permute-start.11
  27.0 1.2 %collective-permute-done.11.got_ref = bf16[128,256]{1,0:T(8,128)(2,1)S(1)} collective-permute-done((bf16[128,256]{1,0:T(8,128)(2,1)S(1)}, bf16[128,256]{1,0:T(8,128)(2,1)S(1)}, u32[]{:S(2)}, u32[]{:S(2)}) %collective-permute-start.11) | collective-permute-done | bytes 65568 | tf_op jit(solution)/shard_map/ppermute | solution.py:198
  28.2 1.1 %shard_map.98 = (bf16[128,256]{1,0:T(8,128)(2,1)}, bf16[128,256]{1,0:T(8,128)(2,1)S(1)}, f32[128,256]{1,0:T(8,128)S(1)}, bf16[128,256]{1,0:T(8,128)(2,1)S(1)}, b...) custom-call(bf16[128,256]{1,0:T(8,128)(2,1)S(1)} %shard_map.97.own_ref, ...), custom_call_target="tpu_custom_call" | custom-call | flops 1024 | bytes 1024 | tf_op jit(solution)/shard_map/pallas_call | solution.py:28
  29.4 2.1 %collective-permute-start.12 = (bf16[128,256]{1,0:T(8,128)(2,1)S(1)}, bf16[128,256]{1,0:T(8,128)(2,1)S(1)}, u32[]{:S(2)}, u32[]{:S(2)}) collective-permute-start(bf16[128,256]{1,0:T(8,128)(2,1)S(1)} %get-tuple-element.36), channel_id=1, source_target_pairs={{0,3},{1,2},{2,1},{3,0},{4,7},{5,6},{6,5},{7,4},{8,11},{9,10},{10,... | collective-permute-start | bytes 196616 | tf_op jit(solution)/shard_map/ppermute | solution.py:201
  31.5 0.5 collective-permute-start.13
  32.0 0.9 %collective-permute-start.14 = (bf16[128,256]{1,0:T(8,128)(2,1)S(1)}, bf16[128,256]{1,0:T(8,128)(2,1)S(1)}, u32[]{:S(2)}, u32[]{:S(2)}) collective-permute-start(bf16[128,256]{1,0:T(8,128)(2,1)S(1)} %get-tuple-element.38), channel_id=1, source_target_pairs={{0,2},{1,3},{2,0},{3,1},{4,6},{5,7},{6,4},{7,5},{8,10},{9,11},{10,... | collective-permute-start | bytes 196616 | tf_op jit(solution)/shard_map/ppermute | solution.py:201
  32.9 2.6 %collective-permute-start.23 = (bf16[128,256]{1,0:T(8,128)(2,1)S(1)}, bf16[128,256]{1,0:T(8,128)(2,1)S(1)}, u32[]{:S(2)}, u32[]{:S(2)}) collective-permute-start(bf16[128,256]{1,0:T(8,128)(2,1)S(1)} %get-tuple-element.40.refs_0_), channel_id=1, source_target_pairs={{0,8},{1,9},{2,10},{3,11},{4,12},{5,13},{6,14},{7,15},{8,0},{9,1},... | collective-permute-start | bytes 196616 | tf_op jit(solution)/shard_map/ppermute | solution.py:204
  35.4 0.6 %collective-permute-start.22 = (bf16[128,256]{1,0:T(8,128)(2,1)S(1)}, bf16[128,256]{1,0:T(8,128)(2,1)S(1)}, u32[]{:S(2)}, u32[]{:S(2)}) collective-permute-start(bf16[128,256]{1,0:T(8,128)(2,1)S(1)} %get-tuple-element.40.refs_0_), channel_id=1, source_target_pairs={{0,12},{1,13},{2,14},{3,15},{4,8},{5,9},{6,10},{7,11},{8,4},{9,5},... | collective-permute-start | bytes 196616 | tf_op jit(solution)/shard_map/ppermute | solution.py:204
  36.1 0.6 %collective-permute-start.21 = (bf16[128,256]{1,0:T(8,128)(2,1)S(1)}, bf16[128,256]{1,0:T(8,128)(2,1)S(1)}, u32[]{:S(2)}, u32[]{:S(2)}) collective-permute-start(bf16[128,256]{1,0:T(8,128)(2,1)S(1)} %get-tuple-element.40.refs_0_), channel_id=1, source_target_pairs={{0,4},{1,5},{2,6},{3,7},{4,0},{5,1},{6,2},{7,3},{8,12},{9,13},{10,... | collective-permute-start | bytes 196616 | tf_op jit(solution)/shard_map/ppermute | solution.py:204
  36.7 3.3 %collective-permute-start.17 = (bf16[128,256]{1,0:T(8,128)(2,1)S(1)}, bf16[128,256]{1,0:T(8,128)(2,1)S(1)}, u32[]{:S(2)}, u32[]{:S(2)}) collective-permute-start(bf16[128,256]{1,0:T(8,128)(2,1)S(1)} %shard_map.99.refs_0_), channel_id=1, source_target_pairs={{0,8},{1,9},{2,10},{3,11},{4,12},{5,13},{6,14},{7,15},{8,0},{9,1},... | collective-permute-start | bytes 196616 | tf_op jit(solution)/shard_map/ppermute | solution.py:204
  39.9 0.6 %collective-permute-start.16 = (bf16[128,256]{1,0:T(8,128)(2,1)S(1)}, bf16[128,256]{1,0:T(8,128)(2,1)S(1)}, u32[]{:S(2)}, u32[]{:S(2)}) collective-permute-start(bf16[128,256]{1,0:T(8,128)(2,1)S(1)} %shard_map.99.refs_0_), channel_id=1, source_target_pairs={{0,12},{1,13},{2,14},{3,15},{4,8},{5,9},{6,10},{7,11},{8,4},{9,5},... | collective-permute-start | bytes 196616 | tf_op jit(solution)/shard_map/ppermute | solution.py:204
  40.6 0.3 collective-permute-start.15
  40.8 1.0 %collective-permute-done.22.refs_2_ = bf16[128,256]{1,0:T(8,128)(2,1)S(1)} collective-permute-done((bf16[128,256]{1,0:T(8,128)(2,1)S(1)}, bf16[128,256]{1,0:T(8,128)(2,1)S(1)}, u32[]{:S(2)}, u32[]{:S(2)}) %collective-permute-start.22) | collective-permute-done | bytes 65568 | tf_op jit(solution)/shard_map/ppermute | solution.py:204
  41.8 0.5 shard_map.102
  42.3 2.3 %collective-permute-start.24 = (bf16[128,256]{1,0:T(8,128)(2,1)S(1)}, bf16[128,256]{1,0:T(8,128)(2,1)S(1)}, u32[]{:S(2)}, u32[]{:S(2)}) collective-permute-start(bf16[128,256]{1,0:T(8,128)(2,1)S(1)} %get-tuple-element.42), channel_id=1, source_target_pairs={{0,3},{1,2},{2,1},{3,0},{4,7},{5,6},{6,5},{7,4},{8,11},{9,10},{10,... | collective-permute-start | bytes 196616 | tf_op jit(solution)/shard_map/ppermute | solution.py:201
  44.5 0.5 collective-permute-start.25
  45.1 1.1 %collective-permute-done.17.refs_3_ = bf16[128,256]{1,0:T(8,128)(2,1)S(1)} collective-permute-done((bf16[128,256]{1,0:T(8,128)(2,1)S(1)}, bf16[128,256]{1,0:T(8,128)(2,1)S(1)}, u32[]{:S(2)}, u32[]{:S(2)}) %collective-permute-start.17) | collective-permute-done | bytes 65568 | tf_op jit(solution)/shard_map/ppermute | solution.py:204
  46.2 0.4 collective-permute-start.26
  46.6 2.7 %collective-permute-start.20 = (bf16[128,256]{1,0:T(8,128)(2,1)S(1)}, bf16[128,256]{1,0:T(8,128)(2,1)S(1)}, u32[]{:S(2)}, u32[]{:S(2)}) collective-permute-start(bf16[128,256]{1,0:T(8,128)(2,1)S(1)} %shard_map.100.refs_0_), channel_id=1, source_target_pairs={{0,3},{1,2},{2,1},{3,0},{4,7},{5,6},{6,5},{7,4},{8,11},{9,10},{10,... | collective-permute-start | bytes 196616 | tf_op jit(solution)/shard_map/ppermute | solution.py:201
  49.3 0.5 collective-permute-start.19
  49.8 0.4 collective-permute-start.18
  50.2 1.7 %collective-permute-done.26.refs_3_ = bf16[128,256]{1,0:T(8,128)(2,1)S(1)} collective-permute-done((bf16[128,256]{1,0:T(8,128)(2,1)S(1)}, bf16[128,256]{1,0:T(8,128)(2,1)S(1)}, u32[]{:S(2)}, u32[]{:S(2)}) %collective-permute-start.26) | collective-permute-done | bytes 65568 | tf_op jit(solution)/shard_map/ppermute | solution.py:201
  51.9 0.7 %shard_map.103 = bf16[128,256]{1,0:T(8,128)(2,1)} custom-call(f32[128,256]{1,0:T(8,128)S(1)} %get-tuple-element.41.refs_0_, bf16[128,256]{1,0:T(8,128)(2,1)S(1)} %collective-permute-done.24.refs_1_, bf16[128,256]{1,0:T(8,128)(2,1)S(1)} %collective-permute-done.25.refs_2_, bf16[128,256]{1,0:T(8,128)(2,1)S(1)} %collective-permute-done.26.refs_3_), custom_call_target="tpu_custom_call" | custom-call | flops 1024 | bytes 1024 | tf_op jit(solution)/shard_map/pallas_call | solution.py:28
  52.6 1.0 %collective-permute-done.19.refs_2_ = bf16[128,256]{1,0:T(8,128)(2,1)S(1)} collective-permute-done((bf16[128,256]{1,0:T(8,128)(2,1)S(1)}, bf16[128,256]{1,0:T(8,128)(2,1)S(1)}, u32[]{:S(2)}, u32[]{:S(2)}) %collective-permute-start.19) | collective-permute-done | bytes 65568 | tf_op jit(solution)/shard_map/ppermute | solution.py:201
  53.5 0.5 collective-permute-done.18.refs_1_
  54.0 0.8 %shard_map.101 = f32[512,256]{1,0:T(8,128)} custom-call(bf16[128,256]{1,0:T(8,128)(2,1)S(1)} %shard_map.100.refs_0_, bf16[128,256]{1,0:T(8,128)(2,1)S(1)} %collective-permute-done.18.refs_1_, bf16[128,256]{1,0:T(8,128)(2,1)S(1)} %collective-permute-done.19.refs_2_, bf16[128,256]{1,0:T(8,128)(2,1)S(1)} %collective-permute-done.20.refs_3_), custom_call_target="tpu_custom_call" | custom-call | flops 1024 | bytes 1024 | tf_op jit(solution)/shard_map/pallas_call | solution.py:28
  (24 shorter events, 0.2 us)
Async XLA Ops:
  0.6 3.7 %copy-start.1 = (bf16[128,512]{1,0:T(8,128)(2,1)S(1)}, bf16[128,512]{1,0:T(8,128)(2,1)}, u32[]{:S(2)}) copy-start(bf16[128,512]{1,0:T(8,128)(2,1)} %refs_8_.1) | copy-start | bytes 393220
  0.6 27.6 %copy-start = (bf16[512,512]{1,0:T(8,128)(2,1)S(1)}, bf16[512,512]{1,0:T(8,128)(2,1)}, u32[]{:S(2)}) copy-start(bf16[512,512]{1,0:T(8,128)(2,1)} %weight_ref.1) | copy-start | bytes 1572868
  0.7 27.6 %copy-start.2 = (bf16[128,512]{1,0:T(8,128)(2,1)S(1)}, bf16[128,512]{1,0:T(8,128)(2,1)}, u32[]{:S(2)}) copy-start(bf16[128,512]{1,0:T(8,128)(2,1)} %cotangent_ref.1) | copy-start | bytes 393220
  0.7 27.6 %copy-start.3 = (f32[512]{0:T(512)S(1)}, f32[512]{0:T(512)}, u32[]{:S(2)}) copy-start(f32[512]{0:T(512)} %param.12) | copy-start | bytes 6148
  2.7 1.7 %collective-permute-start = (bf16[16,64,128]{2,1,0:T(8,128)(2,1)S(1)}, bf16[16,64,128]{2,1,0:T(8,128)(2,1)S(1)}, u32[]{:S(2)}, u32[]{:S(2)}) collective-permute-start(bf16[16,64,128]{2,1,0:T(8,128)(2,1)S(1)} %get-tuple-element.25), channel_id=1, source_target_pairs={{0,16},{16,0},{1,17},{17,1},{2,18},{18,2},{3,19},{19,3},{4,20},{20... | collective-permute-start | bytes 786440 | tf_op jit(solution)/shard_map/ppermute | solution.py:198
  4.4 8.2 %collective-permute-start.1 = (bf16[512,128]{1,0:T(8,128)(2,1)S(1)}, bf16[512,128]{1,0:T(8,128)(2,1)S(1)}, u32[]{:S(2)}, u32[]{:S(2)}) collective-permute-start(bf16[512,128]{1,0:T(8,128)(2,1)S(1)} %get-tuple-element.27), channel_id=1, source_target_pairs={{0,3},{1,2},{2,1},{3,0},{4,7},{5,6},{6,5},{7,4},{8,11},{9,10},{10,... | collective-permute-start | bytes 393224 | tf_op jit(solution)/shard_map/ppermute | solution.py:201
  8.3 6.9 %collective-permute-start.2 = (bf16[512,128]{1,0:T(8,128)(2,1)S(1)}, bf16[512,128]{1,0:T(8,128)(2,1)S(1)}, u32[]{:S(2)}, u32[]{:S(2)}) collective-permute-start(bf16[512,128]{1,0:T(8,128)(2,1)S(1)} %get-tuple-element.28), channel_id=1, source_target_pairs={{0,1},{1,0},{2,3},{3,2},{4,5},{5,4},{6,7},{7,6},{8,9},{9,8},{10,11... | collective-permute-start | bytes 393224 | tf_op jit(solution)/shard_map/ppermute | solution.py:201
  8.9 6.3 %collective-permute-start.3 = (bf16[512,128]{1,0:T(8,128)(2,1)S(1)}, bf16[512,128]{1,0:T(8,128)(2,1)S(1)}, u32[]{:S(2)}, u32[]{:S(2)}) collective-permute-start(bf16[512,128]{1,0:T(8,128)(2,1)S(1)} %get-tuple-element.29), channel_id=1, source_target_pairs={{0,2},{1,3},{2,0},{3,1},{4,6},{5,7},{6,4},{7,5},{8,10},{9,11},{10,... | collective-permute-start | bytes 393224 | tf_op jit(solution)/shard_map/ppermute | solution.py:201
  12.6 4.4 %collective-permute-start.5 = (bf16[512,128]{1,0:T(8,128)(2,1)S(1)}, bf16[512,128]{1,0:T(8,128)(2,1)S(1)}, u32[]{:S(2)}, u32[]{:S(2)}) collective-permute-start(bf16[512,128]{1,0:T(8,128)(2,1)S(1)} %collective-permute-done.1.refs_1_), channel_id=1, source_target_pairs={{0,16},{16,0},{1,17},{17,1},{2,18},{18,2},{3,19},{19,3},{4,20},{20... | collective-permute-start | bytes 393224 | tf_op jit(solution)/shard_map/ppermute | solution.py:198
  15.2 1.8 %collective-permute-start.6 = (bf16[512,128]{1,0:T(8,128)(2,1)S(1)}, bf16[512,128]{1,0:T(8,128)(2,1)S(1)}, u32[]{:S(2)}, u32[]{:S(2)}) collective-permute-start(bf16[512,128]{1,0:T(8,128)(2,1)S(1)} %collective-permute-done.2.refs_2_), channel_id=1, source_target_pairs={{0,16},{16,0},{1,17},{17,1},{2,18},{18,2},{3,19},{19,3},{4,20},{20... | collective-permute-start | bytes 393224 | tf_op jit(solution)/shard_map/ppermute | solution.py:198
  15.2 1.8 %collective-permute-start.7 = (bf16[512,128]{1,0:T(8,128)(2,1)S(1)}, bf16[512,128]{1,0:T(8,128)(2,1)S(1)}, u32[]{:S(2)}, u32[]{:S(2)}) collective-permute-start(bf16[512,128]{1,0:T(8,128)(2,1)S(1)} %collective-permute-done.3.refs_3_), channel_id=1, source_target_pairs={{0,16},{16,0},{1,17},{17,1},{2,18},{18,2},{3,19},{19,3},{4,20},{20... | collective-permute-start | bytes 393224 | tf_op jit(solution)/shard_map/ppermute | solution.py:198
  15.7 1.3 %collective-permute-start.4 = (bf16[256,128]{1,0:T(8,128)(2,1)S(1)}, bf16[256,128]{1,0:T(8,128)(2,1)S(1)}, u32[]{:S(2)}, u32[]{:S(2)}) collective-permute-start(bf16[256,128]{1,0:T(8,128)(2,1)S(1)} %get-tuple-element.26.refs_0_), channel_id=1, source_target_pairs={{0,16},{16,0},{1,17},{17,1},{2,18},{18,2},{3,19},{19,3},{4,20},{20... | collective-permute-start | bytes 196616 | tf_op jit(solution)/shard_map/ppermute | solution.py:198
  17.4 7.1 %collective-permute-start.8 = (bf16[128,256]{1,0:T(8,128)(2,1)S(1)}, bf16[128,256]{1,0:T(8,128)(2,1)S(1)}, u32[]{:S(2)}, u32[]{:S(2)}) collective-permute-start(bf16[128,256]{1,0:T(8,128)(2,1)S(1)} %get-tuple-element.31), channel_id=1, source_target_pairs={{0,8},{1,9},{2,10},{3,11},{4,12},{5,13},{6,14},{7,15},{8,0},{9,1},... | collective-permute-start | bytes 196616 | tf_op jit(solution)/shard_map/ppermute | solution.py:204
  20.1 6.4 %collective-permute-start.9 = (bf16[128,256]{1,0:T(8,128)(2,1)S(1)}, bf16[128,256]{1,0:T(8,128)(2,1)S(1)}, u32[]{:S(2)}, u32[]{:S(2)}) collective-permute-start(bf16[128,256]{1,0:T(8,128)(2,1)S(1)} %get-tuple-element.32), channel_id=1, source_target_pairs={{0,12},{1,13},{2,14},{3,15},{4,8},{5,9},{6,10},{7,11},{8,4},{9,5},... | collective-permute-start | bytes 196616 | tf_op jit(solution)/shard_map/ppermute | solution.py:204
  21.4 5.4 %collective-permute-start.10 = (bf16[128,256]{1,0:T(8,128)(2,1)S(1)}, bf16[128,256]{1,0:T(8,128)(2,1)S(1)}, u32[]{:S(2)}, u32[]{:S(2)}) collective-permute-start(bf16[128,256]{1,0:T(8,128)(2,1)S(1)} %get-tuple-element.33), channel_id=1, source_target_pairs={{0,4},{1,5},{2,6},{3,7},{4,0},{5,1},{6,2},{7,3},{8,12},{9,13},{10,... | collective-permute-start | bytes 196616 | tf_op jit(solution)/shard_map/ppermute | solution.py:204
  26.9 1.3 %collective-permute-start.11 = (bf16[128,256]{1,0:T(8,128)(2,1)S(1)}, bf16[128,256]{1,0:T(8,128)(2,1)S(1)}, u32[]{:S(2)}, u32[]{:S(2)}) collective-permute-start(bf16[128,256]{1,0:T(8,128)(2,1)S(1)} %shard_map.97.own_ref), channel_id=1, source_target_pairs={{0,16},{16,0},{1,17},{17,1},{2,18},{18,2},{3,19},{19,3},{4,20},{20... | collective-permute-start | bytes 196616 | tf_op jit(solution)/shard_map/ppermute | solution.py:198
  29.4 6.7 %collective-permute-start.12 = (bf16[128,256]{1,0:T(8,128)(2,1)S(1)}, bf16[128,256]{1,0:T(8,128)(2,1)S(1)}, u32[]{:S(2)}, u32[]{:S(2)}) collective-permute-start(bf16[128,256]{1,0:T(8,128)(2,1)S(1)} %get-tuple-element.36), channel_id=1, source_target_pairs={{0,3},{1,2},{2,1},{3,0},{4,7},{5,6},{6,5},{7,4},{8,11},{9,10},{10,... | collective-permute-start | bytes 196616 | tf_op jit(solution)/shard_map/ppermute | solution.py:201
  31.5 5.2 %collective-permute-start.13 = (bf16[128,256]{1,0:T(8,128)(2,1)S(1)}, bf16[128,256]{1,0:T(8,128)(2,1)S(1)}, u32[]{:S(2)}, u32[]{:S(2)}) collective-permute-start(bf16[128,256]{1,0:T(8,128)(2,1)S(1)} %get-tuple-element.37), channel_id=1, source_target_pairs={{0,1},{1,0},{2,3},{3,2},{4,5},{5,4},{6,7},{7,6},{8,9},{9,8},{10,11... | collective-permute-start | bytes 196616 | tf_op jit(solution)/shard_map/ppermute | solution.py:201
  32.0 4.6 %collective-permute-start.14 = (bf16[128,256]{1,0:T(8,128)(2,1)S(1)}, bf16[128,256]{1,0:T(8,128)(2,1)S(1)}, u32[]{:S(2)}, u32[]{:S(2)}) collective-permute-start(bf16[128,256]{1,0:T(8,128)(2,1)S(1)} %get-tuple-element.38), channel_id=1, source_target_pairs={{0,2},{1,3},{2,0},{3,1},{4,6},{5,7},{6,4},{7,5},{8,10},{9,11},{10,... | collective-permute-start | bytes 196616 | tf_op jit(solution)/shard_map/ppermute | solution.py:201
  32.9 7.7 %collective-permute-start.23 = (bf16[128,256]{1,0:T(8,128)(2,1)S(1)}, bf16[128,256]{1,0:T(8,128)(2,1)S(1)}, u32[]{:S(2)}, u32[]{:S(2)}) collective-permute-start(bf16[128,256]{1,0:T(8,128)(2,1)S(1)} %get-tuple-element.40.refs_0_), channel_id=1, source_target_pairs={{0,8},{1,9},{2,10},{3,11},{4,12},{5,13},{6,14},{7,15},{8,0},{9,1},... | collective-permute-start | bytes 196616 | tf_op jit(solution)/shard_map/ppermute | solution.py:204
  35.4 6.4 %collective-permute-start.22 = (bf16[128,256]{1,0:T(8,128)(2,1)S(1)}, bf16[128,256]{1,0:T(8,128)(2,1)S(1)}, u32[]{:S(2)}, u32[]{:S(2)}) collective-permute-start(bf16[128,256]{1,0:T(8,128)(2,1)S(1)} %get-tuple-element.40.refs_0_), channel_id=1, source_target_pairs={{0,12},{1,13},{2,14},{3,15},{4,8},{5,9},{6,10},{7,11},{8,4},{9,5},... | collective-permute-start | bytes 196616 | tf_op jit(solution)/shard_map/ppermute | solution.py:204
  36.1 5.7 %collective-permute-start.21 = (bf16[128,256]{1,0:T(8,128)(2,1)S(1)}, bf16[128,256]{1,0:T(8,128)(2,1)S(1)}, u32[]{:S(2)}, u32[]{:S(2)}) collective-permute-start(bf16[128,256]{1,0:T(8,128)(2,1)S(1)} %get-tuple-element.40.refs_0_), channel_id=1, source_target_pairs={{0,4},{1,5},{2,6},{3,7},{4,0},{5,1},{6,2},{7,3},{8,12},{9,13},{10,... | collective-permute-start | bytes 196616 | tf_op jit(solution)/shard_map/ppermute | solution.py:204
  36.7 9.5 %collective-permute-start.17 = (bf16[128,256]{1,0:T(8,128)(2,1)S(1)}, bf16[128,256]{1,0:T(8,128)(2,1)S(1)}, u32[]{:S(2)}, u32[]{:S(2)}) collective-permute-start(bf16[128,256]{1,0:T(8,128)(2,1)S(1)} %shard_map.99.refs_0_), channel_id=1, source_target_pairs={{0,8},{1,9},{2,10},{3,11},{4,12},{5,13},{6,14},{7,15},{8,0},{9,1},... | collective-permute-start | bytes 196616 | tf_op jit(solution)/shard_map/ppermute | solution.py:204
  39.9 6.6 %collective-permute-start.16 = (bf16[128,256]{1,0:T(8,128)(2,1)S(1)}, bf16[128,256]{1,0:T(8,128)(2,1)S(1)}, u32[]{:S(2)}, u32[]{:S(2)}) collective-permute-start(bf16[128,256]{1,0:T(8,128)(2,1)S(1)} %shard_map.99.refs_0_), channel_id=1, source_target_pairs={{0,12},{1,13},{2,14},{3,15},{4,8},{5,9},{6,10},{7,11},{8,4},{9,5},... | collective-permute-start | bytes 196616 | tf_op jit(solution)/shard_map/ppermute | solution.py:204
  40.6 6.0 %collective-permute-start.15 = (bf16[128,256]{1,0:T(8,128)(2,1)S(1)}, bf16[128,256]{1,0:T(8,128)(2,1)S(1)}, u32[]{:S(2)}, u32[]{:S(2)}) collective-permute-start(bf16[128,256]{1,0:T(8,128)(2,1)S(1)} %shard_map.99.refs_0_), channel_id=1, source_target_pairs={{0,4},{1,5},{2,6},{3,7},{4,0},{5,1},{6,2},{7,3},{8,12},{9,13},{10,... | collective-permute-start | bytes 196616 | tf_op jit(solution)/shard_map/ppermute | solution.py:204
  42.3 7.5 %collective-permute-start.24 = (bf16[128,256]{1,0:T(8,128)(2,1)S(1)}, bf16[128,256]{1,0:T(8,128)(2,1)S(1)}, u32[]{:S(2)}, u32[]{:S(2)}) collective-permute-start(bf16[128,256]{1,0:T(8,128)(2,1)S(1)} %get-tuple-element.42), channel_id=1, source_target_pairs={{0,3},{1,2},{2,1},{3,0},{4,7},{5,6},{6,5},{7,4},{8,11},{9,10},{10,... | collective-permute-start | bytes 196616 | tf_op jit(solution)/shard_map/ppermute | solution.py:201
  44.5 5.6 %collective-permute-start.25 = (bf16[128,256]{1,0:T(8,128)(2,1)S(1)}, bf16[128,256]{1,0:T(8,128)(2,1)S(1)}, u32[]{:S(2)}, u32[]{:S(2)}) collective-permute-start(bf16[128,256]{1,0:T(8,128)(2,1)S(1)} %get-tuple-element.43), channel_id=1, source_target_pairs={{0,1},{1,0},{2,3},{3,2},{4,5},{5,4},{6,7},{7,6},{8,9},{9,8},{10,11... | collective-permute-start | bytes 196616 | tf_op jit(solution)/shard_map/ppermute | solution.py:201
  46.2 5.7 %collective-permute-start.26 = (bf16[128,256]{1,0:T(8,128)(2,1)S(1)}, bf16[128,256]{1,0:T(8,128)(2,1)S(1)}, u32[]{:S(2)}, u32[]{:S(2)}) collective-permute-start(bf16[128,256]{1,0:T(8,128)(2,1)S(1)} %get-tuple-element.44), channel_id=1, source_target_pairs={{0,2},{1,3},{2,0},{3,1},{4,6},{5,7},{6,4},{7,5},{8,10},{9,11},{10,... | collective-permute-start | bytes 196616 | tf_op jit(solution)/shard_map/ppermute | solution.py:201
  46.6 6.0 %collective-permute-start.20 = (bf16[128,256]{1,0:T(8,128)(2,1)S(1)}, bf16[128,256]{1,0:T(8,128)(2,1)S(1)}, u32[]{:S(2)}, u32[]{:S(2)}) collective-permute-start(bf16[128,256]{1,0:T(8,128)(2,1)S(1)} %shard_map.100.refs_0_), channel_id=1, source_target_pairs={{0,3},{1,2},{2,1},{3,0},{4,7},{5,6},{6,5},{7,4},{8,11},{9,10},{10,... | collective-permute-start | bytes 196616 | tf_op jit(solution)/shard_map/ppermute | solution.py:201
  49.3 4.3 %collective-permute-start.19 = (bf16[128,256]{1,0:T(8,128)(2,1)S(1)}, bf16[128,256]{1,0:T(8,128)(2,1)S(1)}, u32[]{:S(2)}, u32[]{:S(2)}) collective-permute-start(bf16[128,256]{1,0:T(8,128)(2,1)S(1)} %shard_map.100.refs_0_), channel_id=1, source_target_pairs={{0,1},{1,0},{2,3},{3,2},{4,5},{5,4},{6,7},{7,6},{8,9},{9,8},{10,11... | collective-permute-start | bytes 196616 | tf_op jit(solution)/shard_map/ppermute | solution.py:201
  49.8 4.3 %collective-permute-start.18 = (bf16[128,256]{1,0:T(8,128)(2,1)S(1)}, bf16[128,256]{1,0:T(8,128)(2,1)S(1)}, u32[]{:S(2)}, u32[]{:S(2)}) collective-permute-start(bf16[128,256]{1,0:T(8,128)(2,1)S(1)} %shard_map.100.refs_0_), channel_id=1, source_target_pairs={{0,2},{1,3},{2,0},{3,1},{4,6},{5,7},{6,4},{7,5},{8,10},{9,11},{10,... | collective-permute-start | bytes 196616 | tf_op jit(solution)/shard_map/ppermute | solution.py:201

commit v3 on v2

--- a/solution.py
+++ b/solution.py
@@ -36,16 +36,17 @@
     )(*args)
 
 
-def combine_kernel(dest_hbm, count_hbm, tiles_hbm, own_ref, send_ref, total, tiles, dest, count, sems):
-    half = total.shape[1] // 2
+def combine_kernel(mine, dest_hbm, count_hbm, tiles_hbm, out_ref, total, tiles, dest, count, sems):
+    rep = lax.axis_index("rep")
     size = tiles.shape[0] // CHUNKS
+    part = rows(rep if mine else 1 - rep, tiles.shape[1])
     copies = [
         pltpu.make_async_copy(dest_hbm, dest, sems.at[CHUNKS]),
         pltpu.make_async_copy(count_hbm, count, sems.at[CHUNKS + 1]),
     ]
     for c in range(CHUNKS):
-        part = pl.ds(c * size, size)
-        copies.append(pltpu.make_async_copy(tiles_hbm.at[part], tiles.at[part], sems.at[c]))
+        chunk = pl.ds(c * size, size)
+        copies.append(pltpu.make_async_copy(tiles_hbm.at[chunk, part, :], tiles.at[chunk], sems.at[c]))
     for copy in copies:
         copy.start()
     total[...] = jnp.zeros_like(total)
@@ -60,23 +61,21 @@
 
     for c in range(CHUNKS):
         copies[2 + c].wait()
-        lax.fori_loop(c * size, (c + 1) * size, add, 0, unroll=2)
-    rep = lax.axis_index("rep")
-    own_ref[...] = total[:, rows(rep, half), :].astype(BF16)
-    send_ref[...] = total[:, rows(1 - rep, half), :].astype(BF16)
-
-
-def combine(dest, count, tiles, domains):
+        lax.fori_loop(c * size, (c + 1) * size, add, 0, unroll=4)
+    out_ref[...] = total[...].astype(BF16)
+
+
+def combine(mine, dest, count, tiles, domains):
     number, block, _ = tiles.shape
-    half = (domains, block // 2, block)
+    half = block // 2
     return pl.pallas_call(
-        combine_kernel,
-        out_shape=[jax.ShapeDtypeStruct(half, BF16)] * 2,
+        functools.partial(combine_kernel, mine),
+        out_shape=jax.ShapeDtypeStruct((domains, half, block), BF16),
         in_specs=[pl.BlockSpec(memory_space=pltpu.HBM)] * 3,
-        out_specs=[pl.BlockSpec(memory_space=pltpu.VMEM)] * 2,
+        out_specs=pl.BlockSpec(memory_space=pltpu.VMEM),
         scratch_shapes=[
-            pltpu.VMEM((domains, block, block), F32),
-            pltpu.VMEM(tiles.shape, BF16),
+            pltpu.VMEM((domains, half, block), F32),
+            pltpu.VMEM((number, half, block), BF16),
             pltpu.SMEM((number,), jnp.int32),
             pltpu.SMEM((number,), jnp.int32),
             pltpu.SemaphoreType.DMA((CHUNKS + 2,)),
@@ -173,6 +172,11 @@
         outs[i][...] = total.astype(outs[i].dtype)
 
 
+def feature_kernel(*refs):
+    sum_kernel(None, *refs[:-3], refs[-2])
+    refs[-1][...] = refs[-3][...]
+
+
 def assemble_kernel(near, *refs):
     out = refs[-1]
     _, _, q = place(len(near))
@@ -203,12 +207,14 @@
     def outer_swap(x, t):
         return lax.ppermute(x, "dom", [(i, i ^ (t * group)) for i in range(domains)])
 
-    own, send = combine(tile_dest[:, 0], tile_count, tiles, domains)
+    given = (tile_dest[:, 0], tile_count, tiles, domains)
+    got = rep_swap(combine(False, *given))
+    own = combine(True, *given)
     cut_rows = outer * block // 2
     cut = call(
         functools.partial(split_kernel, group, near),
         [((cut_rows, block), BF16)] + [((cut_rows + half, block), BF16)] * (group - 1),
-        args=(own, rep_swap(send), features),
+        args=(own, got, features),
     )
     mine = [inner_swap(cut[i], s) if s else cut[i] for i, s in enumerate(near)]
     others = [rep_swap(x) for x in mine]
@@ -220,7 +226,7 @@
     )
     parts = [outer_swap(parts[i], t) if t else parts[i] for i, t in enumerate(far)]
     (agg,) = call(functools.partial(sum_kernel, None), [((block, half), BF16)], args=parts)
-    activated, row_grad, *pieces = call(
+    active, row_grad, *pieces = call(
         functools.partial(dense_kernel, group, near),
         [((block, half), BF16), ((block, half), BF16), ((width // group, half), F32)]
         + [((width // group, half), BF16)] * (group - 1),
@@ -247,7 +253,9 @@
     )
     pieces = [inner_swap(piece, s) if s else piece for s in near_back]
     (weight_grad,) = call(functools.partial(assemble_kernel, near_back), [((width, half), F32)], args=pieces)
-    (feature_grad,) = call(functools.partial(sum_kernel, None), [((block, half), BF16)], args=back)
+    feature_grad, activated = call(
+        feature_kernel, [((block, half), BF16), ((block, half), BF16)], args=(*back, active)
+    )
     return (activated, weight_grad, feature_grad)
 
 

time: 55 us -> 54.6 us (level)
  waiting for transfers between devices: 20.4 us -> 19.6 us
    ppermute x6, waiting for transfers between devices: 3.66 us -> 2.5 us  [rep_swap(): return lax.ppermute(x, 'rep', [(0, 1), (1, 0)])]
    pallas_call x1 -> x2, Pallas kernels: 2.01 us -> 3.02 us  [combine(): pl.pallas_call(functools.partial(combine_kernel, mine), out_shape=jax.Sha...]
  transfers between devices with their start and end apart: 27 -> 27, of which waited for: 13 -> 12; matrix products, arithmetic and copies ran while one was open for 0% -> 0% of each run, Pallas kernels for 2% -> 5%
where the time goes in v3:
time: 54.6 us; the launch traced here: 54.4 us
  starting transfers between devices  27.7 us (51%)
  waiting for transfers between devices  19.6 us (36%)
  Pallas kernels  6.28 us (12%)
  between operations  0.78 us (1%)
    ppermute x12, starting transfers between devices, inner_swap(): return lax.ppermute(x, 'dom', [(i, i ^ s) for i in range(domains)])  14.4 us
    ppermute x9, starting transfers between devices, outer_swap(): return lax.ppermute(x, 'dom', [(i, i ^ t * group) for i in range(domains)])  12.2 us
    ppermute x12, waiting for transfers between devices, inner_swap(): return lax.ppermute(x, 'dom', [(i, i ^ s) for i in range(domains)])  9.84 us
    ppermute x9, waiting for transfers between devices, outer_swap(): return lax.ppermute(x, 'dom', [(i, i ^ t * group) for i in range(domains)])  7.3 us
    pallas_call x9, Pallas kernels, call(): pl.pallas_call(kernel, out_shape=[jax.ShapeDtypeStruct(shape, dtype) for...  3.26 us
    pallas_call x2, Pallas kernels, combine(): pl.pallas_call(functools.partial(combine_kernel, mine), out_shape=jax.Sha...  3.02 us
    ppermute x6, waiting for transfers between devices, rep_swap(): return lax.ppermute(x, 'rep', [(0, 1), (1, 0)])  2.5 us
    ppermute x6, starting transfers between devices, rep_swap(): return lax.ppermute(x, 'rep', [(0, 1), (1, 0)])  1.1 us
  transfers between devices with their start and end apart: 27, of which 12 were waited for; matrix products, arithmetic and copies ran while one was open for 0% of the time, Pallas kernels for 5%

profile of v3, /device:TPU:0, one launch (start us, length us, event | category | flops | bytes accessed | tf_op | source)
XLA Modules:
  0.0 54.4 jit_solution(7247951463772421228)
XLA Ops:
  0.6 1.5 %shard_map.95 = bf16[16,64,128]{2,1,0:T(8,128)(2,1)S(1)} custom-call(s32[64]{0:T(128)} %bitcast.3, s32[64]{0:T(128)} %count_hbm.3, bf16[64,128,128]{2,1,0:T(8,128)(2,1)} %tiles_hbm.3), custom_call_target="tpu_custom_call" | custom-call | flops 1024 | bytes 1024 | tf_op jit(solution)/shard_map/pallas_call | solution.py:71
  2.2 0.0 copy-start
  2.2 0.0 copy-start.2
  2.2 0.0 copy-start.3
  2.2 0.5 collective-permute-start
  2.7 1.5 %shard_map.94.own_ref = bf16[16,64,128]{2,1,0:T(8,128)(2,1)S(1)} custom-call(s32[64]{0:T(128)} %bitcast.4, s32[64]{0:T(128)} %count_hbm.3, bf16[64,128,128]{2,1,0:T(8,128)(2,1)} %tiles_hbm.3), custom_call_target="tpu_custom_call" | custom-call | flops 1024 | bytes 1024 | tf_op jit(solution)/shard_map/pallas_call | solution.py:71
  4.2 0.1 shard_map.96
  4.3 3.6 %collective-permute-start.1 = (bf16[512,128]{1,0:T(8,128)(2,1)S(1)}, bf16[512,128]{1,0:T(8,128)(2,1)S(1)}, u32[]{:S(2)}, u32[]{:S(2)}) collective-permute-start(bf16[512,128]{1,0:T(8,128)(2,1)S(1)} %get-tuple-element.25), channel_id=1, source_target_pairs={{0,3},{1,2},{2,1},{3,0},{4,7},{5,6},{6,5},{7,4},{8,11},{9,10},{10,... | collective-permute-start | bytes 393224 | tf_op jit(solution)/shard_map/ppermute | solution.py:205
  7.9 0.5 collective-permute-start.2
  8.5 0.1 collective-permute-start.3
  8.6 3.7 %collective-permute-done.1.refs_1_ = bf16[512,128]{1,0:T(8,128)(2,1)S(1)} collective-permute-done((bf16[512,128]{1,0:T(8,128)(2,1)S(1)}, bf16[512,128]{1,0:T(8,128)(2,1)S(1)}, u32[]{:S(2)}, u32[]{:S(2)}) %collective-permute-start.1) | collective-permute-done | bytes 131104 | tf_op jit(solution)/shard_map/ppermute | solution.py:205
  12.3 2.8 %collective-permute-done.2.refs_2_ = bf16[512,128]{1,0:T(8,128)(2,1)S(1)} collective-permute-done((bf16[512,128]{1,0:T(8,128)(2,1)S(1)}, bf16[512,128]{1,0:T(8,128)(2,1)S(1)}, u32[]{:S(2)}, u32[]{:S(2)}) %collective-permute-start.2) | collective-permute-done | bytes 131104 | tf_op jit(solution)/shard_map/ppermute | solution.py:205
  15.1 0.5 collective-permute-start.7
  15.6 0.0 collective-permute-start.4
  15.6 1.3 %collective-permute-done.4.refs_4_ = bf16[256,128]{1,0:T(8,128)(2,1)S(1)} collective-permute-done((bf16[256,128]{1,0:T(8,128)(2,1)S(1)}, bf16[256,128]{1,0:T(8,128)(2,1)S(1)}, u32[]{:S(2)}, u32[]{:S(2)}) %collective-permute-start.4) | collective-permute-done | bytes 65568 | tf_op jit(solution)/shard_map/ppermute | solution.py:202
  16.9 0.4 shard_map.97
  17.4 2.7 %collective-permute-start.8 = (bf16[128,256]{1,0:T(8,128)(2,1)S(1)}, bf16[128,256]{1,0:T(8,128)(2,1)S(1)}, u32[]{:S(2)}, u32[]{:S(2)}) collective-permute-start(bf16[128,256]{1,0:T(8,128)(2,1)S(1)} %get-tuple-element.30), channel_id=1, source_target_pairs={{0,8},{1,9},{2,10},{3,11},{4,12},{5,13},{6,14},{7,15},{8,0},{9,1},... | collective-permute-start | bytes 196616 | tf_op jit(solution)/shard_map/ppermute | solution.py:208
  20.0 1.3 %collective-permute-start.9 = (bf16[128,256]{1,0:T(8,128)(2,1)S(1)}, bf16[128,256]{1,0:T(8,128)(2,1)S(1)}, u32[]{:S(2)}, u32[]{:S(2)}) collective-permute-start(bf16[128,256]{1,0:T(8,128)(2,1)S(1)} %get-tuple-element.31), channel_id=1, source_target_pairs={{0,12},{1,13},{2,14},{3,15},{4,8},{5,9},{6,10},{7,11},{8,4},{9,5},... | collective-permute-start | bytes 196616 | tf_op jit(solution)/shard_map/ppermute | solution.py:208
  21.4 0.2 collective-permute-start.10
  21.6 2.8 %collective-permute-done.8.refs_1_ = bf16[128,256]{1,0:T(8,128)(2,1)S(1)} collective-permute-done((bf16[128,256]{1,0:T(8,128)(2,1)S(1)}, bf16[128,256]{1,0:T(8,128)(2,1)S(1)}, u32[]{:S(2)}, u32[]{:S(2)}) %collective-permute-start.8) | collective-permute-done | bytes 65568 | tf_op jit(solution)/shard_map/ppermute | solution.py:208
  24.5 2.0 %collective-permute-done.9.refs_2_ = bf16[128,256]{1,0:T(8,128)(2,1)S(1)} collective-permute-done((bf16[128,256]{1,0:T(8,128)(2,1)S(1)}, bf16[128,256]{1,0:T(8,128)(2,1)S(1)}, u32[]{:S(2)}, u32[]{:S(2)}) %collective-permute-start.9) | collective-permute-done | bytes 65568 | tf_op jit(solution)/shard_map/ppermute | solution.py:208
  26.5 0.3 collective-permute-done.10.refs_3_
  26.8 0.1 collective-permute-start.11
  26.9 1.2 %collective-permute-done.11.got_ref = bf16[128,256]{1,0:T(8,128)(2,1)S(1)} collective-permute-done((bf16[128,256]{1,0:T(8,128)(2,1)S(1)}, bf16[128,256]{1,0:T(8,128)(2,1)S(1)}, u32[]{:S(2)}, u32[]{:S(2)}) %collective-permute-start.11) | collective-permute-done | bytes 65568 | tf_op jit(solution)/shard_map/ppermute | solution.py:202
  28.2 0.7 %shard_map.99 = (bf16[128,256]{1,0:T(8,128)(2,1)S(1)}, bf16[128,256]{1,0:T(8,128)(2,1)S(1)}, f32[128,256]{1,0:T(8,128)S(1)}, bf16[128,256]{1,0:T(8,128)(2,1)S(1)...) custom-call(bf16[128,256]{1,0:T(8,128)(2,1)S(1)} %shard_map.98.own_ref, ...), custom_call_target="tpu_custom_call" | custom-call | flops 1024 | bytes 1024 | tf_op jit(solution)/shard_map/pallas_call | solution.py:28
  28.8 2.1 %collective-permute-start.18 = (bf16[128,256]{1,0:T(8,128)(2,1)S(1)}, bf16[128,256]{1,0:T(8,128)(2,1)S(1)}, u32[]{:S(2)}, u32[]{:S(2)}) collective-permute-start(bf16[128,256]{1,0:T(8,128)(2,1)S(1)} %get-tuple-element.41), channel_id=1, source_target_pairs={{0,3},{1,2},{2,1},{3,0},{4,7},{5,6},{6,5},{7,4},{8,11},{9,10},{10,... | collective-permute-start | bytes 196616 | tf_op jit(solution)/shard_map/ppermute | solution.py:205
  31.0 0.5 collective-permute-start.19
  31.5 0.9 %collective-permute-start.20 = (bf16[128,256]{1,0:T(8,128)(2,1)S(1)}, bf16[128,256]{1,0:T(8,128)(2,1)S(1)}, u32[]{:S(2)}, u32[]{:S(2)}) collective-permute-start(bf16[128,256]{1,0:T(8,128)(2,1)S(1)} %get-tuple-element.43), channel_id=1, source_target_pairs={{0,2},{1,3},{2,0},{3,1},{4,6},{5,7},{6,4},{7,5},{8,10},{9,11},{10,... | collective-permute-start | bytes 196616 | tf_op jit(solution)/shard_map/ppermute | solution.py:205
  32.4 2.6 %collective-permute-start.14 = (bf16[128,256]{1,0:T(8,128)(2,1)S(1)}, bf16[128,256]{1,0:T(8,128)(2,1)S(1)}, u32[]{:S(2)}, u32[]{:S(2)}) collective-permute-start(bf16[128,256]{1,0:T(8,128)(2,1)S(1)} %get-tuple-element.33.refs_0_), channel_id=1, source_target_pairs={{0,8},{1,9},{2,10},{3,11},{4,12},{5,13},{6,14},{7,15},{8,0},{9,1},... | collective-permute-start | bytes 196616 | tf_op jit(solution)/shard_map/ppermute | solution.py:208
  34.9 0.6 %collective-permute-start.13 = (bf16[128,256]{1,0:T(8,128)(2,1)S(1)}, bf16[128,256]{1,0:T(8,128)(2,1)S(1)}, u32[]{:S(2)}, u32[]{:S(2)}) collective-permute-start(bf16[128,256]{1,0:T(8,128)(2,1)S(1)} %get-tuple-element.33.refs_0_), channel_id=1, source_target_pairs={{0,12},{1,13},{2,14},{3,15},{4,8},{5,9},{6,10},{7,11},{8,4},{9,5},... | collective-permute-start | bytes 196616 | tf_op jit(solution)/shard_map/ppermute | solution.py:208
  35.6 0.6 %collective-permute-start.12 = (bf16[128,256]{1,0:T(8,128)(2,1)S(1)}, bf16[128,256]{1,0:T(8,128)(2,1)S(1)}, u32[]{:S(2)}, u32[]{:S(2)}) collective-permute-start(bf16[128,256]{1,0:T(8,128)(2,1)S(1)} %get-tuple-element.33.refs_0_), channel_id=1, source_target_pairs={{0,4},{1,5},{2,6},{3,7},{4,0},{5,1},{6,2},{7,3},{8,12},{9,13},{10,... | collective-permute-start | bytes 196616 | tf_op jit(solution)/shard_map/ppermute | solution.py:208
  36.2 3.2 %collective-permute-start.23 = (bf16[128,256]{1,0:T(8,128)(2,1)S(1)}, bf16[128,256]{1,0:T(8,128)(2,1)S(1)}, u32[]{:S(2)}, u32[]{:S(2)}) collective-permute-start(bf16[128,256]{1,0:T(8,128)(2,1)S(1)} %shard_map.102.refs_0_), channel_id=1, source_target_pairs={{0,8},{1,9},{2,10},{3,11},{4,12},{5,13},{6,14},{7,15},{8,0},{9,1},... | collective-permute-start | bytes 196616 | tf_op jit(solution)/shard_map/ppermute | solution.py:208
  39.5 0.6 %collective-permute-start.22 = (bf16[128,256]{1,0:T(8,128)(2,1)S(1)}, bf16[128,256]{1,0:T(8,128)(2,1)S(1)}, u32[]{:S(2)}, u32[]{:S(2)}) collective-permute-start(bf16[128,256]{1,0:T(8,128)(2,1)S(1)} %shard_map.102.refs_0_), channel_id=1, source_target_pairs={{0,12},{1,13},{2,14},{3,15},{4,8},{5,9},{6,10},{7,11},{8,4},{9,5},... | collective-permute-start | bytes 196616 | tf_op jit(solution)/shard_map/ppermute | solution.py:208
  40.1 0.3 collective-permute-start.21
  40.4 1.0 %collective-permute-done.13.refs_2_ = bf16[128,256]{1,0:T(8,128)(2,1)S(1)} collective-permute-done((bf16[128,256]{1,0:T(8,128)(2,1)S(1)}, bf16[128,256]{1,0:T(8,128)(2,1)S(1)}, u32[]{:S(2)}, u32[]{:S(2)}) %collective-permute-start.13) | collective-permute-done | bytes 65568 | tf_op jit(solution)/shard_map/ppermute | solution.py:208
  41.3 0.5 shard_map.100
  41.8 2.2 %collective-permute-start.15 = (bf16[128,256]{1,0:T(8,128)(2,1)S(1)}, bf16[128,256]{1,0:T(8,128)(2,1)S(1)}, u32[]{:S(2)}, u32[]{:S(2)}) collective-permute-start(bf16[128,256]{1,0:T(8,128)(2,1)S(1)} %get-tuple-element.35), channel_id=1, source_target_pairs={{0,3},{1,2},{2,1},{3,0},{4,7},{5,6},{6,5},{7,4},{8,11},{9,10},{10,... | collective-permute-start | bytes 196616 | tf_op jit(solution)/shard_map/ppermute | solution.py:205
  44.0 0.5 collective-permute-start.16
  44.6 1.1 %collective-permute-done.23.refs_3_ = bf16[128,256]{1,0:T(8,128)(2,1)S(1)} collective-permute-done((bf16[128,256]{1,0:T(8,128)(2,1)S(1)}, bf16[128,256]{1,0:T(8,128)(2,1)S(1)}, u32[]{:S(2)}, u32[]{:S(2)}) %collective-permute-start.23) | collective-permute-done | bytes 65568 | tf_op jit(solution)/shard_map/ppermute | solution.py:208
  45.7 0.3 collective-permute-start.17
  46.1 2.7 %collective-permute-start.26 = (bf16[128,256]{1,0:T(8,128)(2,1)S(1)}, bf16[128,256]{1,0:T(8,128)(2,1)S(1)}, u32[]{:S(2)}, u32[]{:S(2)}) collective-permute-start(bf16[128,256]{1,0:T(8,128)(2,1)S(1)} %shard_map.103.refs_0_), channel_id=1, source_target_pairs={{0,3},{1,2},{2,1},{3,0},{4,7},{5,6},{6,5},{7,4},{8,11},{9,10},{10,... | collective-permute-start | bytes 196616 | tf_op jit(solution)/shard_map/ppermute | solution.py:205
  48.8 0.6 %collective-permute-start.25 = (bf16[128,256]{1,0:T(8,128)(2,1)S(1)}, bf16[128,256]{1,0:T(8,128)(2,1)S(1)}, u32[]{:S(2)}, u32[]{:S(2)}) collective-permute-start(bf16[128,256]{1,0:T(8,128)(2,1)S(1)} %shard_map.103.refs_0_), channel_id=1, source_target_pairs={{0,1},{1,0},{2,3},{3,2},{4,5},{5,4},{6,7},{7,6},{8,9},{9,8},{10,11... | collective-permute-start | bytes 196616 | tf_op jit(solution)/shard_map/ppermute | solution.py:205
  49.3 0.3 collective-permute-start.24
  49.6 1.9 %collective-permute-done.17.refs_3_ = bf16[128,256]{1,0:T(8,128)(2,1)S(1)} collective-permute-done((bf16[128,256]{1,0:T(8,128)(2,1)S(1)}, bf16[128,256]{1,0:T(8,128)(2,1)S(1)}, u32[]{:S(2)}, u32[]{:S(2)}) %collective-permute-start.17) | collective-permute-done | bytes 65568 | tf_op jit(solution)/shard_map/ppermute | solution.py:205
  51.5 0.7 %shard_map.101 = (bf16[128,256]{1,0:T(8,128)(2,1)}, bf16[128,256]{1,0:T(8,128)(2,1)}) custom-call(f32[128,256]{1,0:T(8,128)S(1)} %get-tuple-element.34.refs_0_, bf16[128,256]{1,0:T(8,128)(2,1)S(1)} %collective-permute-done.15.refs_1_, bf16[128,256]{1,0:T(8,128)(2,1)S(1)} %collective-permute-done.16.refs_2_, ...), custom_call_target="tpu_custom_call" | custom-call | flops 1024 | bytes 1024 | tf_op jit(solution)/shard_map/pallas_call | solution.py:28
  52.2 0.8 %collective-permute-done.25.refs_2_ = bf16[128,256]{1,0:T(8,128)(2,1)S(1)} collective-permute-done((bf16[128,256]{1,0:T(8,128)(2,1)S(1)}, bf16[128,256]{1,0:T(8,128)(2,1)S(1)}, u32[]{:S(2)}, u32[]{:S(2)}) %collective-permute-start.25) | collective-permute-done | bytes 65568 | tf_op jit(solution)/shard_map/ppermute | solution.py:205
  53.0 0.6 %collective-permute-done.24.refs_1_ = bf16[128,256]{1,0:T(8,128)(2,1)S(1)} collective-permute-done((bf16[128,256]{1,0:T(8,128)(2,1)S(1)}, bf16[128,256]{1,0:T(8,128)(2,1)S(1)}, u32[]{:S(2)}, u32[]{:S(2)}) %collective-permute-start.24) | collective-permute-done | bytes 65568 | tf_op jit(solution)/shard_map/ppermute | solution.py:205
  53.6 0.8 %shard_map.104 = f32[512,256]{1,0:T(8,128)} custom-call(bf16[128,256]{1,0:T(8,128)(2,1)S(1)} %shard_map.103.refs_0_, bf16[128,256]{1,0:T(8,128)(2,1)S(1)} %collective-permute-done.24.refs_1_, bf16[128,256]{1,0:T(8,128)(2,1)S(1)} %collective-permute-done.25.refs_2_, bf16[128,256]{1,0:T(8,128)(2,1)S(1)} %collective-permute-done.26.refs_3_), custom_call_target="tpu_custom_call" | custom-call | flops 1024 | bytes 1024 | tf_op jit(solution)/shard_map/pallas_call | solution.py:28
  (25 shorter events, 0.2 us)
Async XLA Ops:
  0.6 3.6 %copy-start.1 = (bf16[128,512]{1,0:T(8,128)(2,1)S(1)}, bf16[128,512]{1,0:T(8,128)(2,1)}, u32[]{:S(2)}) copy-start(bf16[128,512]{1,0:T(8,128)(2,1)} %refs_8_.1) | copy-start | bytes 393220
  2.2 26.0 %copy-start = (bf16[512,512]{1,0:T(8,128)(2,1)S(1)}, bf16[512,512]{1,0:T(8,128)(2,1)}, u32[]{:S(2)}) copy-start(bf16[512,512]{1,0:T(8,128)(2,1)} %weight_ref.1) | copy-start | bytes 1572868
  2.2 26.0 %copy-start.2 = (bf16[128,512]{1,0:T(8,128)(2,1)S(1)}, bf16[128,512]{1,0:T(8,128)(2,1)}, u32[]{:S(2)}) copy-start(bf16[128,512]{1,0:T(8,128)(2,1)} %cotangent_ref.1) | copy-start | bytes 393220
  2.2 26.0 %copy-start.3 = (f32[512]{0:T(512)S(1)}, f32[512]{0:T(512)}, u32[]{:S(2)}) copy-start(f32[512]{0:T(512)} %param.12) | copy-start | bytes 6148
  2.2 2.0 %collective-permute-start = (bf16[16,64,128]{2,1,0:T(8,128)(2,1)S(1)}, bf16[16,64,128]{2,1,0:T(8,128)(2,1)S(1)}, u32[]{:S(2)}, u32[]{:S(2)}) collective-permute-start(bf16[16,64,128]{2,1,0:T(8,128)(2,1)S(1)} %shard_map.95), channel_id=1, source_target_pairs={{0,16},{16,0},{1,17},{17,1},{2,18},{18,2},{3,19},{19,3},{4,20},{20... | collective-permute-start | bytes 786440 | tf_op jit(solution)/shard_map/ppermute | solution.py:202
  4.3 7.9 %collective-permute-start.1 = (bf16[512,128]{1,0:T(8,128)(2,1)S(1)}, bf16[512,128]{1,0:T(8,128)(2,1)S(1)}, u32[]{:S(2)}, u32[]{:S(2)}) collective-permute-start(bf16[512,128]{1,0:T(8,128)(2,1)S(1)} %get-tuple-element.25), channel_id=1, source_target_pairs={{0,3},{1,2},{2,1},{3,0},{4,7},{5,6},{6,5},{7,4},{8,11},{9,10},{10,... | collective-permute-start | bytes 393224 | tf_op jit(solution)/shard_map/ppermute | solution.py:205
  7.9 7.2 %collective-permute-start.2 = (bf16[512,128]{1,0:T(8,128)(2,1)S(1)}, bf16[512,128]{1,0:T(8,128)(2,1)S(1)}, u32[]{:S(2)}, u32[]{:S(2)}) collective-permute-start(bf16[512,128]{1,0:T(8,128)(2,1)S(1)} %get-tuple-element.26), channel_id=1, source_target_pairs={{0,1},{1,0},{2,3},{3,2},{4,5},{5,4},{6,7},{7,6},{8,9},{9,8},{10,11... | collective-permute-start | bytes 393224 | tf_op jit(solution)/shard_map/ppermute | solution.py:205
  8.5 6.7 %collective-permute-start.3 = (bf16[512,128]{1,0:T(8,128)(2,1)S(1)}, bf16[512,128]{1,0:T(8,128)(2,1)S(1)}, u32[]{:S(2)}, u32[]{:S(2)}) collective-permute-start(bf16[512,128]{1,0:T(8,128)(2,1)S(1)} %get-tuple-element.27), channel_id=1, source_target_pairs={{0,2},{1,3},{2,0},{3,1},{4,6},{5,7},{6,4},{7,5},{8,10},{9,11},{10,... | collective-permute-start | bytes 393224 | tf_op jit(solution)/shard_map/ppermute | solution.py:205
  12.3 4.6 %collective-permute-start.5 = (bf16[512,128]{1,0:T(8,128)(2,1)S(1)}, bf16[512,128]{1,0:T(8,128)(2,1)S(1)}, u32[]{:S(2)}, u32[]{:S(2)}) collective-permute-start(bf16[512,128]{1,0:T(8,128)(2,1)S(1)} %collective-permute-done.1.refs_1_), channel_id=1, source_target_pairs={{0,16},{16,0},{1,17},{17,1},{2,18},{18,2},{3,19},{19,3},{4,20},{20... | collective-permute-start | bytes 393224 | tf_op jit(solution)/shard_map/ppermute | solution.py:202
  15.1 1.8 %collective-permute-start.6 = (bf16[512,128]{1,0:T(8,128)(2,1)S(1)}, bf16[512,128]{1,0:T(8,128)(2,1)S(1)}, u32[]{:S(2)}, u32[]{:S(2)}) collective-permute-start(bf16[512,128]{1,0:T(8,128)(2,1)S(1)} %collective-permute-done.2.refs_2_), channel_id=1, source_target_pairs={{0,16},{16,0},{1,17},{17,1},{2,18},{18,2},{3,19},{19,3},{4,20},{20... | collective-permute-start | bytes 393224 | tf_op jit(solution)/shard_map/ppermute | solution.py:202
  15.1 1.8 %collective-permute-start.7 = (bf16[512,128]{1,0:T(8,128)(2,1)S(1)}, bf16[512,128]{1,0:T(8,128)(2,1)S(1)}, u32[]{:S(2)}, u32[]{:S(2)}) collective-permute-start(bf16[512,128]{1,0:T(8,128)(2,1)S(1)} %collective-permute-done.3.refs_3_), channel_id=1, source_target_pairs={{0,16},{16,0},{1,17},{17,1},{2,18},{18,2},{3,19},{19,3},{4,20},{20... | collective-permute-start | bytes 393224 | tf_op jit(solution)/shard_map/ppermute | solution.py:202
  15.6 1.3 %collective-permute-start.4 = (bf16[256,128]{1,0:T(8,128)(2,1)S(1)}, bf16[256,128]{1,0:T(8,128)(2,1)S(1)}, u32[]{:S(2)}, u32[]{:S(2)}) collective-permute-start(bf16[256,128]{1,0:T(8,128)(2,1)S(1)} %get-tuple-element.24.refs_0_), channel_id=1, source_target_pairs={{0,16},{16,0},{1,17},{17,1},{2,18},{18,2},{3,19},{19,3},{4,20},{20... | collective-permute-start | bytes 196616 | tf_op jit(solution)/shard_map/ppermute | solution.py:202
  17.4 7.1 %collective-permute-start.8 = (bf16[128,256]{1,0:T(8,128)(2,1)S(1)}, bf16[128,256]{1,0:T(8,128)(2,1)S(1)}, u32[]{:S(2)}, u32[]{:S(2)}) collective-permute-start(bf16[128,256]{1,0:T(8,128)(2,1)S(1)} %get-tuple-element.30), channel_id=1, source_target_pairs={{0,8},{1,9},{2,10},{3,11},{4,12},{5,13},{6,14},{7,15},{8,0},{9,1},... | collective-permute-start | bytes 196616 | tf_op jit(solution)/shard_map/ppermute | solution.py:208
  20.0 6.4 %collective-permute-start.9 = (bf16[128,256]{1,0:T(8,128)(2,1)S(1)}, bf16[128,256]{1,0:T(8,128)(2,1)S(1)}, u32[]{:S(2)}, u32[]{:S(2)}) collective-permute-start(bf16[128,256]{1,0:T(8,128)(2,1)S(1)} %get-tuple-element.31), channel_id=1, source_target_pairs={{0,12},{1,13},{2,14},{3,15},{4,8},{5,9},{6,10},{7,11},{8,4},{9,5},... | collective-permute-start | bytes 196616 | tf_op jit(solution)/shard_map/ppermute | solution.py:208
  21.4 5.4 %collective-permute-start.10 = (bf16[128,256]{1,0:T(8,128)(2,1)S(1)}, bf16[128,256]{1,0:T(8,128)(2,1)S(1)}, u32[]{:S(2)}, u32[]{:S(2)}) collective-permute-start(bf16[128,256]{1,0:T(8,128)(2,1)S(1)} %get-tuple-element.32), channel_id=1, source_target_pairs={{0,4},{1,5},{2,6},{3,7},{4,0},{5,1},{6,2},{7,3},{8,12},{9,13},{10,... | collective-permute-start | bytes 196616 | tf_op jit(solution)/shard_map/ppermute | solution.py:208
  26.8 1.3 %collective-permute-start.11 = (bf16[128,256]{1,0:T(8,128)(2,1)S(1)}, bf16[128,256]{1,0:T(8,128)(2,1)S(1)}, u32[]{:S(2)}, u32[]{:S(2)}) collective-permute-start(bf16[128,256]{1,0:T(8,128)(2,1)S(1)} %shard_map.98.own_ref), channel_id=1, source_target_pairs={{0,16},{16,0},{1,17},{17,1},{2,18},{18,2},{3,19},{19,3},{4,20},{20... | collective-permute-start | bytes 196616 | tf_op jit(solution)/shard_map/ppermute | solution.py:202
  28.8 6.8 %collective-permute-start.18 = (bf16[128,256]{1,0:T(8,128)(2,1)S(1)}, bf16[128,256]{1,0:T(8,128)(2,1)S(1)}, u32[]{:S(2)}, u32[]{:S(2)}) collective-permute-start(bf16[128,256]{1,0:T(8,128)(2,1)S(1)} %get-tuple-element.41), channel_id=1, source_target_pairs={{0,3},{1,2},{2,1},{3,0},{4,7},{5,6},{6,5},{7,4},{8,11},{9,10},{10,... | collective-permute-start | bytes 196616 | tf_op jit(solution)/shard_map/ppermute | solution.py:205
  31.0 5.2 %collective-permute-start.19 = (bf16[128,256]{1,0:T(8,128)(2,1)S(1)}, bf16[128,256]{1,0:T(8,128)(2,1)S(1)}, u32[]{:S(2)}, u32[]{:S(2)}) collective-permute-start(bf16[128,256]{1,0:T(8,128)(2,1)S(1)} %get-tuple-element.42), channel_id=1, source_target_pairs={{0,1},{1,0},{2,3},{3,2},{4,5},{5,4},{6,7},{7,6},{8,9},{9,8},{10,11... | collective-permute-start | bytes 196616 | tf_op jit(solution)/shard_map/ppermute | solution.py:205
  31.5 4.7 %collective-permute-start.20 = (bf16[128,256]{1,0:T(8,128)(2,1)S(1)}, bf16[128,256]{1,0:T(8,128)(2,1)S(1)}, u32[]{:S(2)}, u32[]{:S(2)}) collective-permute-start(bf16[128,256]{1,0:T(8,128)(2,1)S(1)} %get-tuple-element.43), channel_id=1, source_target_pairs={{0,2},{1,3},{2,0},{3,1},{4,6},{5,7},{6,4},{7,5},{8,10},{9,11},{10,... | collective-permute-start | bytes 196616 | tf_op jit(solution)/shard_map/ppermute | solution.py:205
  32.4 7.7 %collective-permute-start.14 = (bf16[128,256]{1,0:T(8,128)(2,1)S(1)}, bf16[128,256]{1,0:T(8,128)(2,1)S(1)}, u32[]{:S(2)}, u32[]{:S(2)}) collective-permute-start(bf16[128,256]{1,0:T(8,128)(2,1)S(1)} %get-tuple-element.33.refs_0_), channel_id=1, source_target_pairs={{0,8},{1,9},{2,10},{3,11},{4,12},{5,13},{6,14},{7,15},{8,0},{9,1},... | collective-permute-start | bytes 196616 | tf_op jit(solution)/shard_map/ppermute | solution.py:208
  34.9 6.4 %collective-permute-start.13 = (bf16[128,256]{1,0:T(8,128)(2,1)S(1)}, bf16[128,256]{1,0:T(8,128)(2,1)S(1)}, u32[]{:S(2)}, u32[]{:S(2)}) collective-permute-start(bf16[128,256]{1,0:T(8,128)(2,1)S(1)} %get-tuple-element.33.refs_0_), channel_id=1, source_target_pairs={{0,12},{1,13},{2,14},{3,15},{4,8},{5,9},{6,10},{7,11},{8,4},{9,5},... | collective-permute-start | bytes 196616 | tf_op jit(solution)/shard_map/ppermute | solution.py:208
  35.6 5.7 %collective-permute-start.12 = (bf16[128,256]{1,0:T(8,128)(2,1)S(1)}, bf16[128,256]{1,0:T(8,128)(2,1)S(1)}, u32[]{:S(2)}, u32[]{:S(2)}) collective-permute-start(bf16[128,256]{1,0:T(8,128)(2,1)S(1)} %get-tuple-element.33.refs_0_), channel_id=1, source_target_pairs={{0,4},{1,5},{2,6},{3,7},{4,0},{5,1},{6,2},{7,3},{8,12},{9,13},{10,... | collective-permute-start | bytes 196616 | tf_op jit(solution)/shard_map/ppermute | solution.py:208
  36.2 9.5 %collective-permute-start.23 = (bf16[128,256]{1,0:T(8,128)(2,1)S(1)}, bf16[128,256]{1,0:T(8,128)(2,1)S(1)}, u32[]{:S(2)}, u32[]{:S(2)}) collective-permute-start(bf16[128,256]{1,0:T(8,128)(2,1)S(1)} %shard_map.102.refs_0_), channel_id=1, source_target_pairs={{0,8},{1,9},{2,10},{3,11},{4,12},{5,13},{6,14},{7,15},{8,0},{9,1},... | collective-permute-start | bytes 196616 | tf_op jit(solution)/shard_map/ppermute | solution.py:208
  39.5 6.6 %collective-permute-start.22 = (bf16[128,256]{1,0:T(8,128)(2,1)S(1)}, bf16[128,256]{1,0:T(8,128)(2,1)S(1)}, u32[]{:S(2)}, u32[]{:S(2)}) collective-permute-start(bf16[128,256]{1,0:T(8,128)(2,1)S(1)} %shard_map.102.refs_0_), channel_id=1, source_target_pairs={{0,12},{1,13},{2,14},{3,15},{4,8},{5,9},{6,10},{7,11},{8,4},{9,5},... | collective-permute-start | bytes 196616 | tf_op jit(solution)/shard_map/ppermute | solution.py:208
  40.1 5.9 %collective-permute-start.21 = (bf16[128,256]{1,0:T(8,128)(2,1)S(1)}, bf16[128,256]{1,0:T(8,128)(2,1)S(1)}, u32[]{:S(2)}, u32[]{:S(2)}) collective-permute-start(bf16[128,256]{1,0:T(8,128)(2,1)S(1)} %shard_map.102.refs_0_), channel_id=1, source_target_pairs={{0,4},{1,5},{2,6},{3,7},{4,0},{5,1},{6,2},{7,3},{8,12},{9,13},{10,... | collective-permute-start | bytes 196616 | tf_op jit(solution)/shard_map/ppermute | solution.py:208
  41.8 7.5 %collective-permute-start.15 = (bf16[128,256]{1,0:T(8,128)(2,1)S(1)}, bf16[128,256]{1,0:T(8,128)(2,1)S(1)}, u32[]{:S(2)}, u32[]{:S(2)}) collective-permute-start(bf16[128,256]{1,0:T(8,128)(2,1)S(1)} %get-tuple-element.35), channel_id=1, source_target_pairs={{0,3},{1,2},{2,1},{3,0},{4,7},{5,6},{6,5},{7,4},{8,11},{9,10},{10,... | collective-permute-start | bytes 196616 | tf_op jit(solution)/shard_map/ppermute | solution.py:205
  44.0 5.6 %collective-permute-start.16 = (bf16[128,256]{1,0:T(8,128)(2,1)S(1)}, bf16[128,256]{1,0:T(8,128)(2,1)S(1)}, u32[]{:S(2)}, u32[]{:S(2)}) collective-permute-start(bf16[128,256]{1,0:T(8,128)(2,1)S(1)} %get-tuple-element.36), channel_id=1, source_target_pairs={{0,1},{1,0},{2,3},{3,2},{4,5},{5,4},{6,7},{7,6},{8,9},{9,8},{10,11... | collective-permute-start | bytes 196616 | tf_op jit(solution)/shard_map/ppermute | solution.py:205
  45.7 5.8 %collective-permute-start.17 = (bf16[128,256]{1,0:T(8,128)(2,1)S(1)}, bf16[128,256]{1,0:T(8,128)(2,1)S(1)}, u32[]{:S(2)}, u32[]{:S(2)}) collective-permute-start(bf16[128,256]{1,0:T(8,128)(2,1)S(1)} %get-tuple-element.37), channel_id=1, source_target_pairs={{0,2},{1,3},{2,0},{3,1},{4,6},{5,7},{6,4},{7,5},{8,10},{9,11},{10,... | collective-permute-start | bytes 196616 | tf_op jit(solution)/shard_map/ppermute | solution.py:205
  46.1 6.1 %collective-permute-start.26 = (bf16[128,256]{1,0:T(8,128)(2,1)S(1)}, bf16[128,256]{1,0:T(8,128)(2,1)S(1)}, u32[]{:S(2)}, u32[]{:S(2)}) collective-permute-start(bf16[128,256]{1,0:T(8,128)(2,1)S(1)} %shard_map.103.refs_0_), channel_id=1, source_target_pairs={{0,3},{1,2},{2,1},{3,0},{4,7},{5,6},{6,5},{7,4},{8,11},{9,10},{10,... | collective-permute-start | bytes 196616 | tf_op jit(solution)/shard_map/ppermute | solution.py:205
  48.8 4.3 %collective-permute-start.25 = (bf16[128,256]{1,0:T(8,128)(2,1)S(1)}, bf16[128,256]{1,0:T(8,128)(2,1)S(1)}, u32[]{:S(2)}, u32[]{:S(2)}) collective-permute-start(bf16[128,256]{1,0:T(8,128)(2,1)S(1)} %shard_map.103.refs_0_), channel_id=1, source_target_pairs={{0,1},{1,0},{2,3},{3,2},{4,5},{5,4},{6,7},{7,6},{8,9},{9,8},{10,11... | collective-permute-start | bytes 196616 | tf_op jit(solution)/shard_map/ppermute | solution.py:205
  49.3 4.3 %collective-permute-start.24 = (bf16[128,256]{1,0:T(8,128)(2,1)S(1)}, bf16[128,256]{1,0:T(8,128)(2,1)S(1)}, u32[]{:S(2)}, u32[]{:S(2)}) collective-permute-start(bf16[128,256]{1,0:T(8,128)(2,1)S(1)} %shard_map.103.refs_0_), channel_id=1, source_target_pairs={{0,2},{1,3},{2,0},{3,1},{4,6},{5,7},{6,4},{7,5},{8,10},{9,11},{10,... | collective-permute-start | bytes 196616 | tf_op jit(solution)/shard_map/ppermute | solution.py:205

commit v4 on v3

--- a/solution.py
+++ b/solution.py
@@ -85,6 +85,10 @@
     )(*[pltpu.with_memory_space_constraint(x, pltpu.HBM) for x in (dest, count, tiles)])
 
 
+def half_kernel(whole_ref, out_ref):
+    out_ref[...] = whole_ref[:, rows(lax.axis_index("rep"), out_ref.shape[1])]
+
+
 def split_kernel(group, near, own_ref, got_ref, features_ref, *outs):
     rep, _, q = place(group)
     outer = own_ref.shape[0] // group
@@ -101,28 +105,41 @@
             outs[s][at : at + block] = piece
 
 
-def forward_kernel(group, outer, near, far, *refs):
+def forward_kernel(group, outer, near, far, order, *refs):
     own = [refs[near.index(s)] for s in range(group)]
     got = [refs[group + near.index(s)] for s in range(group)]
-    features_ref, adjacency = refs[2 * group : 2 * group + 2]
-    outs, panel = refs[2 * group + 2 : -1], refs[-1]
+    features_ref, adjacency = refs[2 * group], refs[-outer - 2]
+    outs, panel = refs[-outer - 1 : -1], refs[-1]
     rep, z, _ = place(group)
     block, width = features_ref.shape
     half, side = block // 2, width // 2
-    for t in range(outer):
+    for i, t in enumerate(order):
         at = pl.ds(pl.multiple_of(lax.bitwise_xor(z, t) * half, half), half)
         for s in range(group):
             columns = slice(s * block, (s + 1) * block)
-            adjacency[t, rows(rep, half), columns] = own[s][at, :]
-            adjacency[t, rows(1 - rep, half), columns] = got[s][at, :]
+            adjacency[i, rows(rep, half), columns] = own[s][at, :]
+            adjacency[i, rows(1 - rep, half), columns] = got[s][at, :]
     panel[:block, :] = features_ref[:, rows(rep, side)]
     for s in range(1, group):
         for i in range(side // block):
             start = outer * half + i * block
             panel[s * block : (s + 1) * block, i * block : (i + 1) * block] = own[s][start : start + block, :]
     for i, t in enumerate(far):
-        part = jnp.dot(adjacency[t], panel[...], preferred_element_type=F32)
+        part = jnp.dot(adjacency[order.index(t)], panel[...], preferred_element_type=F32)
         outs[i][...] = part.astype(outs[i].dtype)
+
+
+def top_kernel(whole_ref, _, out_ref):
+    out_ref[...] = whole_ref[: out_ref.shape[0], :]
+
+
+def stack_kernel(number, *refs):
+    for i, ref in enumerate(refs[:number]):
+        refs[-1][i * ref.shape[0] : (i + 1) * ref.shape[0]] = ref[...]
+
+
+def late_sum_kernel(scale, _, *refs):
+    sum_kernel(scale, *refs)
 
 
 def sum_kernel(scale, *refs):
@@ -133,42 +150,45 @@
     out[...] = (total * scale if scale is not None else total).astype(out.dtype)
 
 
-def dense_kernel(group, near, own_ref, got_ref, weight_ref, bias_ref, cotangent_ref, *refs):
-    active_ref, row_grad_ref = refs[:2]
-    outs = refs[2 : 2 + group]
-    agg, pre_ref, grad, parts = refs[2 + group :]
+def dense_kernel(group, near, outer, place_of, *refs):
+    own, got, slopes_ref = refs[:outer], refs[outer : 2 * outer], refs[2 * outer]
+    weight_ref, bias_ref, active_ref, keep_ref, send_ref = refs[2 * outer + 1 : 2 * outer + 6]
+    outs, (agg, grad, parts) = refs[2 * outer + 6 : -3], refs[-3:]
     rep, _, q = place(group)
-    width = own_ref.shape[1]
-    agg[:, rows(rep, width)] = own_ref[...]
-    agg[:, rows(1 - rep, width)] = got_ref[...]
-    pre = jnp.dot(agg[...], weight_ref[...], preferred_element_type=F32) + bias_ref[...]
-    sig = jax.nn.sigmoid(pre)
-    pre_ref[...] = pre * sig
-    active_ref[...] = pre_ref[:, rows(rep, width)].astype(BF16)
-    slope = cotangent_ref[...].astype(F32) * sig * (1.0 + pre * (1.0 - sig))
-    grad[...] = slope.astype(BF16)
-    row_grad = lax.dot_general(
-        grad[...], weight_ref[rows(rep, width), :], (((1,), (1,)), ((), ())), preferred_element_type=F32
-    )
-    row_grad_ref[...] = row_grad.astype(BF16)
-    parts[...] = lax.dot_general(
-        agg[...], grad[:, rows(rep, width)], (((0,), (0,)), ((), ())), preferred_element_type=F32
-    )
+    block, side = own[0].shape
+    mine, other = rows(rep, side), rows(1 - rep, side)
+    for t in range(outer):
+        at = slice(t * block, (t + 1) * block)
+        agg[at, mine] = own[t][...]
+        agg[at, other] = got[t][...]
+        pre = jnp.dot(agg[at, :], weight_ref[:, mine], preferred_element_type=F32) + bias_ref[:, mine]
+        sig = jax.nn.sigmoid(pre)
+        if t == 0:
+            active_ref[...] = (pre * sig).astype(BF16)
+        slope = slopes_ref[place_of[t] * block : (place_of[t] + 1) * block, :].astype(F32)
+        grad[at, :] = (slope * sig * (1.0 + pre * (1.0 - sig))).astype(BF16)
+    parts[...] = lax.dot_general(agg[...], grad[...], (((0,), (0,)), ((), ())), preferred_element_type=F32)
     size = parts.shape[0] // group
     for i, s in enumerate(near):
         outs[i][...] = parts[rows(lax.bitwise_xor(q, s), size), :].astype(outs[i].dtype)
-
-
-def backward_kernel(group, near, far, adjacency, *refs):
-    outer, block, _ = adjacency.shape
-    grads, outs = refs[:outer], refs[outer:]
+    for ref, columns in ((keep_ref, mine), (send_ref, other)):
+        row_grad = lax.dot_general(
+            grad[...], weight_ref[columns, mine], (((1,), (1,)), ((), ())), preferred_element_type=F32
+        )
+        ref[...] = row_grad.astype(ref.dtype)
+
+
+def backward_kernel(group, near, adjacency, keep_ref, got_ref, *refs):
+    outs, grad = refs[:-1], refs[-1]
+    outer, block, columns = adjacency.shape
+    grad[...] = (keep_ref[...] + got_ref[...].astype(F32)).astype(BF16)
     for i, s in enumerate(near):
-        columns = slice(s * block, (s + 1) * block)
-        total = jnp.zeros(outs[i].shape, F32)
-        for j, t in enumerate(far):
-            total = total + lax.dot_general(
-                adjacency[t, :, columns], grads[j][...], (((0,), (0,)), ((), ())), preferred_element_type=F32
-            )
+        total = lax.dot_general(
+            adjacency[...].reshape(outer * block, columns)[:, s * block : (s + 1) * block],
+            grad[...],
+            (((0,), (0,)), ((), ())),
+            preferred_element_type=F32,
+        )
         outs[i][...] = total.astype(outs[i].dtype)
 
 
@@ -183,6 +203,12 @@
     size = refs[0].shape[0]
     for i, s in enumerate(near):
         out[rows(lax.bitwise_xor(q, s), size), :] = refs[i][...].astype(F32)
+
+
+def finish_kernel(near, *refs):
+    group = len(near)
+    assemble_kernel(near, *refs[:group], refs[-3])
+    feature_kernel(*refs[group:-3], *refs[-2:])
 
 
 def per_device(features, tiles, tile_dest, tile_count, weight, bias, cotangent):
@@ -216,45 +242,62 @@
         [((cut_rows, block), BF16)] + [((cut_rows + half, block), BF16)] * (group - 1),
         args=(own, got, features),
     )
+    (slopes,) = call(half_kernel, [((block, half), BF16)], args=(cotangent,))
+    order, bit = [0], outer // 2
+    got_slopes = outer_swap(slopes, bit)
     mine = [inner_swap(cut[i], s) if s else cut[i] for i, s in enumerate(near)]
-    others = [rep_swap(x) for x in mine]
+    (last,) = call(top_kernel, [((cut_rows, block), BF16)], args=(mine[-1], got_slopes))
+    others = [rep_swap(x) for x in (*mine[:-1], last)]
     adjacency, *parts = call(
-        functools.partial(forward_kernel, group, outer, near, far),
+        functools.partial(forward_kernel, group, outer, near, far, far_back),
         [((outer, block, group * block), BF16), ((block, half), F32)] + [((block, half), BF16)] * (outer - 1),
         scratch=(pltpu.VMEM((group * block, half), BF16),),
         args=(*mine, *others, features),
     )
+    own_part = parts[0]
     parts = [outer_swap(parts[i], t) if t else parts[i] for i, t in enumerate(far)]
+    while bit:
+        order = order + [t ^ bit for t in order]
+        (slopes,) = call(
+            functools.partial(stack_kernel, 2),
+            [((len(order) * block, half), BF16)],
+            args=(slopes, got_slopes, own_part),
+        )
+        bit //= 2
+        got_slopes = outer_swap(slopes, bit) if bit else None
     (agg,) = call(functools.partial(sum_kernel, None), [((block, half), BF16)], args=parts)
-    active, row_grad, *pieces = call(
-        functools.partial(dense_kernel, group, near),
-        [((block, half), BF16), ((block, half), BF16), ((width // group, half), F32)]
+    aggs = [outer_swap(agg, t) if t else agg for t in far_back]
+    tall = outer * block
+    active, keep, send, *pieces = call(
+        functools.partial(dense_kernel, group, near, outer, [order.index(t) for t in far_back]),
+        [((block, half), BF16), ((tall, half), F32), ((tall, half), BF16), ((width // group, half), F32)]
         + [((width // group, half), BF16)] * (group - 1),
         scratch=(
-            pltpu.VMEM((block, width), BF16),
-            pltpu.VMEM((block, width), F32),
-            pltpu.VMEM((block, width), BF16),
+            pltpu.VMEM((tall, width), BF16),
+            pltpu.VMEM((tall, half), BF16),
             pltpu.VMEM((width, half), F32),
         ),
-        args=(agg, rep_swap(agg), weight, bias.reshape(1, width), cotangent),
+        args=(*aggs, *[rep_swap(x) for x in aggs], slopes, weight, bias.reshape(1, width)),
     )
     pieces = [inner_swap(pieces[i], s) if s else pieces[i] for i, s in enumerate(near)]
-    (piece,) = call(functools.partial(sum_kernel, None), [((width // group, half), BF16)], args=pieces)
-    grads = [outer_swap(row_grad, t) if t else row_grad for t in far_back]
     back = call(
-        functools.partial(backward_kernel, group, near, far_back),
+        functools.partial(backward_kernel, group, near),
         [((block, half), F32)] + [((block, half), BF16)] * (group - 1),
-        args=(adjacency, *grads),
-    )
+        scratch=(pltpu.VMEM((tall, half), BF16),),
+        args=(adjacency, keep, rep_swap(send)),
+    )
+    back_own = back[0]
     back = [inner_swap(back[i], s) if s else back[i] for i, s in enumerate(near)]
-    pieces = [outer_swap(piece, t) if t else piece for t in far_back]
     (piece,) = call(
-        functools.partial(sum_kernel, 1.0 / math.sqrt(nodes)), [((width // group, half), BF16)], args=pieces
+        functools.partial(late_sum_kernel, 1.0 / math.sqrt(nodes)),
+        [((width // group, half), BF16)],
+        args=(back_own, *pieces),
     )
     pieces = [inner_swap(piece, s) if s else piece for s in near_back]
-    (weight_grad,) = call(functools.partial(assemble_kernel, near_back), [((width, half), F32)], args=pieces)
-    feature_grad, activated = call(
-        feature_kernel, [((block, half), BF16), ((block, half), BF16)], args=(*back, active)
+    weight_grad, feature_grad, activated = call(
+        functools.partial(finish_kernel, near_back),
+        [((width, half), F32), ((block, half), BF16), ((block, half), BF16)],
+        args=(*pieces, *back, active),
     )
     return (activated, weight_grad, feature_grad)
 

time: 54.6 us -> 53.9 us (0.987)
  waiting for transfers between devices: 19.6 us -> 17.7 us
  starting transfers between devices: 27.7 us -> 29.5 us
  Pallas kernels: 6.28 us -> 5.71 us
    ppermute x12, waiting for transfers between devices: 9.84 us -> 6.83 us  [inner_swap(): return lax.ppermute(x, 'dom', [(i, i ^ s) for i in range(domains)])]
    ppermute x9 -> x8, waiting for transfers between devices: 7.3 us -> 8.74 us  [outer_swap(): return lax.ppermute(x, 'dom', [(i, i ^ t * group) for i in range(domains)])]
    ppermute x6 -> x10, starting transfers between devices: 1.1 us -> 1.97 us  [rep_swap(): return lax.ppermute(x, 'rep', [(0, 1), (1, 0)])]
    ppermute x9 -> x8, starting transfers between devices: 12.2 us -> 12.8 us  [outer_swap(): return lax.ppermute(x, 'dom', [(i, i ^ t * group) for i in range(domains)])]
    pallas_call x9 -> x11, Pallas kernels: 3.26 us -> 2.69 us  [call(): pl.pallas_call(kernel, out_shape=[jax.ShapeDtypeStruct(shape, dtype) for...]
    ppermute x6 -> x10, waiting for transfers between devices: 2.5 us -> 2.11 us  [rep_swap(): return lax.ppermute(x, 'rep', [(0, 1), (1, 0)])]
  transfers between devices with their start and end apart: 27 -> 30, of which waited for: 12 -> 16; matrix products, arithmetic and copies ran while one was open for 0% -> 0% of each run, Pallas kernels for 5% -> 4%
where the time goes in v4:
time: 53.9 us; the launch traced here: 53.7 us
  starting transfers between devices  29.5 us (55%)
  waiting for transfers between devices  17.7 us (33%)
  Pallas kernels  5.71 us (11%)
  between operations  0.8 us (1%)
    ppermute x12, starting transfers between devices, inner_swap(): return lax.ppermute(x, 'dom', [(i, i ^ s) for i in range(domains)])  14.8 us
    ppermute x8, starting transfers between devices, outer_swap(): return lax.ppermute(x, 'dom', [(i, i ^ t * group) for i in range(domains)])  12.8 us
    ppermute x8, waiting for transfers between devices, outer_swap(): return lax.ppermute(x, 'dom', [(i, i ^ t * group) for i in range(domains)])  8.74 us
    ppermute x12, waiting for transfers between devices, inner_swap(): return lax.ppermute(x, 'dom', [(i, i ^ s) for i in range(domains)])  6.83 us
    pallas_call x2, Pallas kernels, combine(): pl.pallas_call(functools.partial(combine_kernel, mine), out_shape=jax.Sha...  3.03 us
    pallas_call x11, Pallas kernels, call(): pl.pallas_call(kernel, out_shape=[jax.ShapeDtypeStruct(shape, dtype) for...  2.69 us
    ppermute x10, waiting for transfers between devices, rep_swap(): return lax.ppermute(x, 'rep', [(0, 1), (1, 0)])  2.11 us
    ppermute x10, starting transfers between devices, rep_swap(): return lax.ppermute(x, 'rep', [(0, 1), (1, 0)])  1.97 us
  transfers between devices with their start and end apart: 30, of which 16 were waited for; matrix products, arithmetic and copies ran while one was open for 0% of the time, Pallas kernels for 4%

profile of v4, /device:TPU:0, one launch (start us, length us, event | category | flops | bytes accessed | tf_op | source)
XLA Modules:
  0.0 53.7 jit_solution(2320060998497492041)
XLA Ops:
  0.6 1.5 %shard_map.95 = bf16[16,64,128]{2,1,0:T(8,128)(2,1)S(1)} custom-call(s32[64]{0:T(128)} %bitcast.3, s32[64]{0:T(128)} %count_hbm.3, bf16[64,128,128]{2,1,0:T(8,128)(2,1)} %tiles_hbm.3), custom_call_target="tpu_custom_call" | custom-call | flops 1024 | bytes 1024 | tf_op jit(solution)/shard_map/pallas_call | solution.py:71
  2.2 0.5 collective-permute-start
  2.7 1.5 %shard_map.94.own_ref = bf16[16,64,128]{2,1,0:T(8,128)(2,1)S(1)} custom-call(s32[64]{0:T(128)} %bitcast.4, s32[64]{0:T(128)} %count_hbm.3, bf16[64,128,128]{2,1,0:T(8,128)(2,1)} %tiles_hbm.3), custom_call_target="tpu_custom_call" | custom-call | flops 1024 | bytes 1024 | tf_op jit(solution)/shard_map/pallas_call | solution.py:71
  4.3 0.1 shard_map.96
  4.3 3.5 %collective-permute-start.1 = (bf16[512,128]{1,0:T(8,128)(2,1)S(1)}, bf16[512,128]{1,0:T(8,128)(2,1)S(1)}, u32[]{:S(2)}, u32[]{:S(2)}) collective-permute-start(bf16[512,128]{1,0:T(8,128)(2,1)S(1)} %get-tuple-element.27), channel_id=1, source_target_pairs={{0,3},{1,2},{2,1},{3,0},{4,7},{5,6},{6,5},{7,4},{8,11},{9,10},{10,... | collective-permute-start | bytes 393224 | tf_op jit(solution)/shard_map/ppermute | solution.py:231
  7.9 0.5 %collective-permute-start.2 = (bf16[512,128]{1,0:T(8,128)(2,1)S(1)}, bf16[512,128]{1,0:T(8,128)(2,1)S(1)}, u32[]{:S(2)}, u32[]{:S(2)}) collective-permute-start(bf16[512,128]{1,0:T(8,128)(2,1)S(1)} %get-tuple-element.28), channel_id=1, source_target_pairs={{0,1},{1,0},{2,3},{3,2},{4,5},{5,4},{6,7},{7,6},{8,9},{9,8},{10,11... | collective-permute-start | bytes 393224 | tf_op jit(solution)/shard_map/ppermute | solution.py:231
  8.4 0.1 collective-permute-start.3
  8.5 3.1 %collective-permute-start.7 = (bf16[128,256]{1,0:T(8,128)(2,1)S(1)}, bf16[128,256]{1,0:T(8,128)(2,1)S(1)}, u32[]{:S(2)}, u32[]{:S(2)}) collective-permute-start(bf16[128,256]{1,0:T(8,128)(2,1)S(1)} %shard_map.97.refs_0_), channel_id=1, source_target_pairs={{0,8},{1,9},{2,10},{3,11},{4,12},{5,13},{6,14},{7,15},{8,0},{9,1},... | collective-permute-start | bytes 196616 | tf_op jit(solution)/shard_map/ppermute | solution.py:234
  11.6 0.6 %collective-permute-done.1.refs_1_ = bf16[512,128]{1,0:T(8,128)(2,1)S(1)} collective-permute-done((bf16[512,128]{1,0:T(8,128)(2,1)S(1)}, bf16[512,128]{1,0:T(8,128)(2,1)S(1)}, u32[]{:S(2)}, u32[]{:S(2)}) %collective-permute-start.1) | collective-permute-done | bytes 131104 | tf_op jit(solution)/shard_map/ppermute | solution.py:231
  12.2 2.9 %collective-permute-done.2.refs_2_ = bf16[512,128]{1,0:T(8,128)(2,1)S(1)} collective-permute-done((bf16[512,128]{1,0:T(8,128)(2,1)S(1)}, bf16[512,128]{1,0:T(8,128)(2,1)S(1)}, u32[]{:S(2)}, u32[]{:S(2)}) %collective-permute-start.2) | collective-permute-done | bytes 131104 | tf_op jit(solution)/shard_map/ppermute | solution.py:231
  15.1 0.5 collective-permute-start.4
  15.7 0.1 collective-permute-start.8
  15.7 0.8 %collective-permute-done.4.refs_4_ = bf16[256,128]{1,0:T(8,128)(2,1)S(1)} collective-permute-done((bf16[256,128]{1,0:T(8,128)(2,1)S(1)}, bf16[256,128]{1,0:T(8,128)(2,1)S(1)}, u32[]{:S(2)}, u32[]{:S(2)}) %collective-permute-start.4) | collective-permute-done | bytes 65568 | tf_op jit(solution)/shard_map/ppermute | solution.py:228
  16.6 0.4 collective-permute-done.8.refs_7_
  17.0 0.4 shard_map.99
  17.4 2.6 %collective-permute-start.9 = (bf16[128,256]{1,0:T(8,128)(2,1)S(1)}, bf16[128,256]{1,0:T(8,128)(2,1)S(1)}, u32[]{:S(2)}, u32[]{:S(2)}) collective-permute-start(bf16[128,256]{1,0:T(8,128)(2,1)S(1)} %get-tuple-element.32), channel_id=1, source_target_pairs={{0,8},{1,9},{2,10},{3,11},{4,12},{5,13},{6,14},{7,15},{8,0},{9,1},... | collective-permute-start | bytes 196616 | tf_op jit(solution)/shard_map/ppermute | solution.py:234
  20.1 1.3 %collective-permute-start.10 = (bf16[128,256]{1,0:T(8,128)(2,1)S(1)}, bf16[128,256]{1,0:T(8,128)(2,1)S(1)}, u32[]{:S(2)}, u32[]{:S(2)}) collective-permute-start(bf16[128,256]{1,0:T(8,128)(2,1)S(1)} %get-tuple-element.33), channel_id=1, source_target_pairs={{0,12},{1,13},{2,14},{3,15},{4,8},{5,9},{6,10},{7,11},{8,4},{9,5},... | collective-permute-start | bytes 196616 | tf_op jit(solution)/shard_map/ppermute | solution.py:234
  21.4 0.2 collective-permute-start.11
  21.7 1.9 %collective-permute-start.19 = (bf16[256,256]{1,0:T(8,128)(2,1)S(1)}, bf16[256,256]{1,0:T(8,128)(2,1)S(1)}, u32[]{:S(2)}, u32[]{:S(2)}) collective-permute-start(bf16[256,256]{1,0:T(8,128)(2,1)S(1)} %shard_map.101.refs_0_), channel_id=1, source_target_pairs={{0,4},{1,5},{2,6},{3,7},{4,0},{5,1},{6,2},{7,3},{8,12},{9,13},{10,... | collective-permute-start | bytes 393224 | tf_op jit(solution)/shard_map/ppermute | solution.py:234
  23.5 1.7 %collective-permute-done.9.refs_1_ = bf16[128,256]{1,0:T(8,128)(2,1)S(1)} collective-permute-done((bf16[128,256]{1,0:T(8,128)(2,1)S(1)}, bf16[128,256]{1,0:T(8,128)(2,1)S(1)}, u32[]{:S(2)}, u32[]{:S(2)}) %collective-permute-start.9) | collective-permute-done | bytes 65568 | tf_op jit(solution)/shard_map/ppermute | solution.py:234
  25.2 1.6 %collective-permute-done.10.refs_2_ = bf16[128,256]{1,0:T(8,128)(2,1)S(1)} collective-permute-done((bf16[128,256]{1,0:T(8,128)(2,1)S(1)}, bf16[128,256]{1,0:T(8,128)(2,1)S(1)}, u32[]{:S(2)}, u32[]{:S(2)}) %collective-permute-start.10) | collective-permute-done | bytes 65568 | tf_op jit(solution)/shard_map/ppermute | solution.py:234
  26.8 0.5 collective-permute-done.11.refs_3_
  27.4 2.1 %collective-permute-start.14 = (bf16[128,256]{1,0:T(8,128)(2,1)S(1)}, bf16[128,256]{1,0:T(8,128)(2,1)S(1)}, u32[]{:S(2)}, u32[]{:S(2)}) collective-permute-start(bf16[128,256]{1,0:T(8,128)(2,1)S(1)} %shard_map.100.refs_0_), channel_id=1, source_target_pairs={{0,8},{1,9},{2,10},{3,11},{4,12},{5,13},{6,14},{7,15},{8,0},{9,1},... | collective-permute-start | bytes 196616 | tf_op jit(solution)/shard_map/ppermute | solution.py:234
  29.5 1.0 %collective-permute-start.13 = (bf16[128,256]{1,0:T(8,128)(2,1)S(1)}, bf16[128,256]{1,0:T(8,128)(2,1)S(1)}, u32[]{:S(2)}, u32[]{:S(2)}) collective-permute-start(bf16[128,256]{1,0:T(8,128)(2,1)S(1)} %shard_map.100.refs_0_), channel_id=1, source_target_pairs={{0,12},{1,13},{2,14},{3,15},{4,8},{5,9},{6,10},{7,11},{8,4},{9,5},... | collective-permute-start | bytes 196616 | tf_op jit(solution)/shard_map/ppermute | solution.py:234
  30.5 0.5 collective-permute-start.12
  31.0 3.6 %collective-permute-done.14.refs_3_ = bf16[128,256]{1,0:T(8,128)(2,1)S(1)} collective-permute-done((bf16[128,256]{1,0:T(8,128)(2,1)S(1)}, bf16[128,256]{1,0:T(8,128)(2,1)S(1)}, u32[]{:S(2)}, u32[]{:S(2)}) %collective-permute-start.14) | collective-permute-done | bytes 65568 | tf_op jit(solution)/shard_map/ppermute | solution.py:234
  34.6 1.2 %collective-permute-done.13.refs_2_ = bf16[128,256]{1,0:T(8,128)(2,1)S(1)} collective-permute-done((bf16[128,256]{1,0:T(8,128)(2,1)S(1)}, bf16[128,256]{1,0:T(8,128)(2,1)S(1)}, u32[]{:S(2)}, u32[]{:S(2)}) %collective-permute-start.13) | collective-permute-done | bytes 65568 | tf_op jit(solution)/shard_map/ppermute | solution.py:234
  35.9 0.1 collective-permute-done.12.refs_1_
  35.9 0.5 collective-permute-start.16
  36.4 0.7 %collective-permute-done.17.refs_6_ = bf16[128,256]{1,0:T(8,128)(2,1)S(1)} collective-permute-done((bf16[128,256]{1,0:T(8,128)(2,1)S(1)}, bf16[128,256]{1,0:T(8,128)(2,1)S(1)}, u32[]{:S(2)}, u32[]{:S(2)}) %collective-permute-start.17) | collective-permute-done | bytes 65568 | tf_op jit(solution)/shard_map/ppermute | solution.py:228
  37.1 0.2 collective-permute-done.16.refs_5_
  37.3 0.8 %shard_map.103 = (bf16[128,256]{1,0:T(8,128)(2,1)S(1)}, f32[512,256]{1,0:T(8,128)S(1)}, bf16[512,256]{1,0:T(8,128)(2,1)S(1)}, f32[128,256]{1,0:T(8,128)S(1)}, bf...) custom-call(bf16[128,256]{1,0:T(8,128)(2,1)S(1)} %shard_map.100.refs_0_, ...), custom_call_target="tpu_custom_call" | custom-call | flops 1024 | bytes 1024 | tf_op jit(solution)/shard_map/pallas_call | solution.py:28
  38.1 0.4 collective-permute-start.20
  38.5 1.8 %collective-permute-start.21 = (bf16[128,256]{1,0:T(8,128)(2,1)S(1)}, bf16[128,256]{1,0:T(8,128)(2,1)S(1)}, u32[]{:S(2)}, u32[]{:S(2)}) collective-permute-start(bf16[128,256]{1,0:T(8,128)(2,1)S(1)} %get-tuple-element.39), channel_id=1, source_target_pairs={{0,3},{1,2},{2,1},{3,0},{4,7},{5,6},{6,5},{7,4},{8,11},{9,10},{10,... | collective-permute-start | bytes 196616 | tf_op jit(solution)/shard_map/ppermute | solution.py:231
  40.3 0.5 collective-permute-start.22
  40.8 1.2 %collective-permute-start.23 = (bf16[128,256]{1,0:T(8,128)(2,1)S(1)}, bf16[128,256]{1,0:T(8,128)(2,1)S(1)}, u32[]{:S(2)}, u32[]{:S(2)}) collective-permute-start(bf16[128,256]{1,0:T(8,128)(2,1)S(1)} %get-tuple-element.41), channel_id=1, source_target_pairs={{0,2},{1,3},{2,0},{3,1},{4,6},{5,7},{6,4},{7,5},{8,10},{9,11},{10,... | collective-permute-start | bytes 196616 | tf_op jit(solution)/shard_map/ppermute | solution.py:231
  42.0 0.4 shard_map.104
  42.4 1.9 %collective-permute-start.27 = (bf16[128,256]{1,0:T(8,128)(2,1)S(1)}, bf16[128,256]{1,0:T(8,128)(2,1)S(1)}, u32[]{:S(2)}, u32[]{:S(2)}) collective-permute-start(bf16[128,256]{1,0:T(8,128)(2,1)S(1)} %get-tuple-element.42), channel_id=1, source_target_pairs={{0,3},{1,2},{2,1},{3,0},{4,7},{5,6},{6,5},{7,4},{8,11},{9,10},{10,... | collective-permute-start | bytes 196616 | tf_op jit(solution)/shard_map/ppermute | solution.py:231
  44.2 0.5 collective-permute-start.28
  44.8 1.2 %collective-permute-start.29 = (bf16[128,256]{1,0:T(8,128)(2,1)S(1)}, bf16[128,256]{1,0:T(8,128)(2,1)S(1)}, u32[]{:S(2)}, u32[]{:S(2)}) collective-permute-start(bf16[128,256]{1,0:T(8,128)(2,1)S(1)} %get-tuple-element.44), channel_id=1, source_target_pairs={{0,2},{1,3},{2,0},{3,1},{4,6},{5,7},{6,4},{7,5},{8,10},{9,11},{10,... | collective-permute-start | bytes 196616 | tf_op jit(solution)/shard_map/ppermute | solution.py:231
  46.0 2.0 %collective-permute-start.26 = (bf16[128,256]{1,0:T(8,128)(2,1)S(1)}, bf16[128,256]{1,0:T(8,128)(2,1)S(1)}, u32[]{:S(2)}, u32[]{:S(2)}) collective-permute-start(bf16[128,256]{1,0:T(8,128)(2,1)S(1)} %shard_map.105.refs_0_), channel_id=1, source_target_pairs={{0,3},{1,2},{2,1},{3,0},{4,7},{5,6},{6,5},{7,4},{8,11},{9,10},{10,... | collective-permute-start | bytes 196616 | tf_op jit(solution)/shard_map/ppermute | solution.py:231
  48.0 0.5 collective-permute-start.25
  48.5 1.0 %collective-permute-start.24 = (bf16[128,256]{1,0:T(8,128)(2,1)S(1)}, bf16[128,256]{1,0:T(8,128)(2,1)S(1)}, u32[]{:S(2)}, u32[]{:S(2)}) collective-permute-start(bf16[128,256]{1,0:T(8,128)(2,1)S(1)} %shard_map.105.refs_0_), channel_id=1, source_target_pairs={{0,2},{1,3},{2,0},{3,1},{4,6},{5,7},{6,4},{7,5},{8,10},{9,11},{10,... | collective-permute-start | bytes 196616 | tf_op jit(solution)/shard_map/ppermute | solution.py:231
  49.5 0.4 collective-permute-done.29.refs_7_
  49.9 1.3 %collective-permute-done.26.refs_3_ = bf16[128,256]{1,0:T(8,128)(2,1)S(1)} collective-permute-done((bf16[128,256]{1,0:T(8,128)(2,1)S(1)}, bf16[128,256]{1,0:T(8,128)(2,1)S(1)}, u32[]{:S(2)}, u32[]{:S(2)}) %collective-permute-start.26) | collective-permute-done | bytes 65568 | tf_op jit(solution)/shard_map/ppermute | solution.py:231
  51.2 1.1 %collective-permute-done.25.refs_2_ = bf16[128,256]{1,0:T(8,128)(2,1)S(1)} collective-permute-done((bf16[128,256]{1,0:T(8,128)(2,1)S(1)}, bf16[128,256]{1,0:T(8,128)(2,1)S(1)}, u32[]{:S(2)}, u32[]{:S(2)}) %collective-permute-start.25) | collective-permute-done | bytes 65568 | tf_op jit(solution)/shard_map/ppermute | solution.py:231
  52.3 0.5 collective-permute-done.24.refs_1_
  52.8 0.9 %shard_map.106 = (f32[512,256]{1,0:T(8,128)}, bf16[128,256]{1,0:T(8,128)(2,1)}, bf16[128,256]{1,0:T(8,128)(2,1)}) custom-call(bf16[128,256]{1,0:T(8,128)(2,1)S(1)} %shard_map.105.refs_0_, bf16[128,256]{1,0:T(8,128)(2,1)S(1)} %collective-permute-done.24.refs_1_, bf16[128,256]{1,0:T(8,128)(2,1)S(1)} %collective-permute-done.25.refs_2_, ...), custom_call_target="tpu_custom_call" | custom-call | flops 1024 | bytes 1024 | tf_op jit(solution)/shard_map/pallas_call | solution.py:28
  (33 shorter events, 0.2 us)
Async XLA Ops:
  0.6 3.6 %copy-start.1 = (bf16[128,512]{1,0:T(8,128)(2,1)S(1)}, bf16[128,512]{1,0:T(8,128)(2,1)}, u32[]{:S(2)}) copy-start(bf16[128,512]{1,0:T(8,128)(2,1)} %refs_8_.1) | copy-start | bytes 393220
  2.2 6.3 %copy-start.2 = (bf16[128,512]{1,0:T(8,128)(2,1)S(1)}, bf16[128,512]{1,0:T(8,128)(2,1)}, u32[]{:S(2)}) copy-start(bf16[128,512]{1,0:T(8,128)(2,1)} %whole_ref.1) | copy-start | bytes 393220
  2.2 2.0 %collective-permute-start = (bf16[16,64,128]{2,1,0:T(8,128)(2,1)S(1)}, bf16[16,64,128]{2,1,0:T(8,128)(2,1)S(1)}, u32[]{:S(2)}, u32[]{:S(2)}) collective-permute-start(bf16[16,64,128]{2,1,0:T(8,128)(2,1)S(1)} %shard_map.95), channel_id=1, source_target_pairs={{0,16},{16,0},{1,17},{17,1},{2,18},{18,2},{3,19},{19,3},{4,20},{20... | collective-permute-start | bytes 786440 | tf_op jit(solution)/shard_map/ppermute | solution.py:228
  4.2 33.1 %copy-start = (bf16[512,512]{1,0:T(8,128)(2,1)S(1)}, bf16[512,512]{1,0:T(8,128)(2,1)}, u32[]{:S(2)}) copy-start(bf16[512,512]{1,0:T(8,128)(2,1)} %refs_9_.1) | copy-start | bytes 1572868
  4.2 33.1 %copy-start.3 = (f32[512]{0:T(512)S(1)}, f32[512]{0:T(512)}, u32[]{:S(2)}) copy-start(f32[512]{0:T(512)} %param.12) | copy-start | bytes 6148
  4.3 7.9 %collective-permute-start.1 = (bf16[512,128]{1,0:T(8,128)(2,1)S(1)}, bf16[512,128]{1,0:T(8,128)(2,1)S(1)}, u32[]{:S(2)}, u32[]{:S(2)}) collective-permute-start(bf16[512,128]{1,0:T(8,128)(2,1)S(1)} %get-tuple-element.27), channel_id=1, source_target_pairs={{0,3},{1,2},{2,1},{3,0},{4,7},{5,6},{6,5},{7,4},{8,11},{9,10},{10,... | collective-permute-start | bytes 393224 | tf_op jit(solution)/shard_map/ppermute | solution.py:231
  7.9 7.3 %collective-permute-start.2 = (bf16[512,128]{1,0:T(8,128)(2,1)S(1)}, bf16[512,128]{1,0:T(8,128)(2,1)S(1)}, u32[]{:S(2)}, u32[]{:S(2)}) collective-permute-start(bf16[512,128]{1,0:T(8,128)(2,1)S(1)} %get-tuple-element.28), channel_id=1, source_target_pairs={{0,1},{1,0},{2,3},{3,2},{4,5},{5,4},{6,7},{7,6},{8,9},{9,8},{10,11... | collective-permute-start | bytes 393224 | tf_op jit(solution)/shard_map/ppermute | solution.py:231
  8.4 7.2 %collective-permute-start.3 = (bf16[512,128]{1,0:T(8,128)(2,1)S(1)}, bf16[512,128]{1,0:T(8,128)(2,1)S(1)}, u32[]{:S(2)}, u32[]{:S(2)}) collective-permute-start(bf16[512,128]{1,0:T(8,128)(2,1)S(1)} %get-tuple-element.29), channel_id=1, source_target_pairs={{0,2},{1,3},{2,0},{3,1},{4,6},{5,7},{6,4},{7,5},{8,10},{9,11},{10,... | collective-permute-start | bytes 393224 | tf_op jit(solution)/shard_map/ppermute | solution.py:231
  8.5 7.1 %collective-permute-start.7 = (bf16[128,256]{1,0:T(8,128)(2,1)S(1)}, bf16[128,256]{1,0:T(8,128)(2,1)S(1)}, u32[]{:S(2)}, u32[]{:S(2)}) collective-permute-start(bf16[128,256]{1,0:T(8,128)(2,1)S(1)} %shard_map.97.refs_0_), channel_id=1, source_target_pairs={{0,8},{1,9},{2,10},{3,11},{4,12},{5,13},{6,14},{7,15},{8,0},{9,1},... | collective-permute-start | bytes 196616 | tf_op jit(solution)/shard_map/ppermute | solution.py:234
  12.2 4.8 %collective-permute-start.5 = (bf16[512,128]{1,0:T(8,128)(2,1)S(1)}, bf16[512,128]{1,0:T(8,128)(2,1)S(1)}, u32[]{:S(2)}, u32[]{:S(2)}) collective-permute-start(bf16[512,128]{1,0:T(8,128)(2,1)S(1)} %collective-permute-done.1.refs_1_), channel_id=1, source_target_pairs={{0,16},{16,0},{1,17},{17,1},{2,18},{18,2},{3,19},{19,3},{4,20},{20... | collective-permute-start | bytes 393224 | tf_op jit(solution)/shard_map/ppermute | solution.py:228
  15.1 1.9 %collective-permute-start.6 = (bf16[512,128]{1,0:T(8,128)(2,1)S(1)}, bf16[512,128]{1,0:T(8,128)(2,1)S(1)}, u32[]{:S(2)}, u32[]{:S(2)}) collective-permute-start(bf16[512,128]{1,0:T(8,128)(2,1)S(1)} %collective-permute-done.2.refs_2_), channel_id=1, source_target_pairs={{0,16},{16,0},{1,17},{17,1},{2,18},{18,2},{3,19},{19,3},{4,20},{20... | collective-permute-start | bytes 393224 | tf_op jit(solution)/shard_map/ppermute | solution.py:228
  15.1 1.4 %collective-permute-start.4 = (bf16[256,128]{1,0:T(8,128)(2,1)S(1)}, bf16[256,128]{1,0:T(8,128)(2,1)S(1)}, u32[]{:S(2)}, u32[]{:S(2)}) collective-permute-start(bf16[256,128]{1,0:T(8,128)(2,1)S(1)} %get-tuple-element.26.refs_0_), channel_id=1, source_target_pairs={{0,16},{16,0},{1,17},{17,1},{2,18},{18,2},{3,19},{19,3},{4,20},{20... | collective-permute-start | bytes 196616 | tf_op jit(solution)/shard_map/ppermute | solution.py:228
  15.7 1.3 %collective-permute-start.8 = (bf16[256,128]{1,0:T(8,128)(2,1)S(1)}, bf16[256,128]{1,0:T(8,128)(2,1)S(1)}, u32[]{:S(2)}, u32[]{:S(2)}) collective-permute-start(bf16[256,128]{1,0:T(8,128)(2,1)S(1)} %shard_map.98), channel_id=1, source_target_pairs={{0,16},{16,0},{1,17},{17,1},{2,18},{18,2},{3,19},{19,3},{4,20},{20... | collective-permute-start | bytes 196616 | tf_op jit(solution)/shard_map/ppermute | solution.py:228
  17.4 7.8 %collective-permute-start.9 = (bf16[128,256]{1,0:T(8,128)(2,1)S(1)}, bf16[128,256]{1,0:T(8,128)(2,1)S(1)}, u32[]{:S(2)}, u32[]{:S(2)}) collective-permute-start(bf16[128,256]{1,0:T(8,128)(2,1)S(1)} %get-tuple-element.32), channel_id=1, source_target_pairs={{0,8},{1,9},{2,10},{3,11},{4,12},{5,13},{6,14},{7,15},{8,0},{9,1},... | collective-permute-start | bytes 196616 | tf_op jit(solution)/shard_map/ppermute | solution.py:234
  20.1 6.8 %collective-permute-start.10 = (bf16[128,256]{1,0:T(8,128)(2,1)S(1)}, bf16[128,256]{1,0:T(8,128)(2,1)S(1)}, u32[]{:S(2)}, u32[]{:S(2)}) collective-permute-start(bf16[128,256]{1,0:T(8,128)(2,1)S(1)} %get-tuple-element.33), channel_id=1, source_target_pairs={{0,12},{1,13},{2,14},{3,15},{4,8},{5,9},{6,10},{7,11},{8,4},{9,5},... | collective-permute-start | bytes 196616 | tf_op jit(solution)/shard_map/ppermute | solution.py:234
  21.4 5.9 %collective-permute-start.11 = (bf16[128,256]{1,0:T(8,128)(2,1)S(1)}, bf16[128,256]{1,0:T(8,128)(2,1)S(1)}, u32[]{:S(2)}, u32[]{:S(2)}) collective-permute-start(bf16[128,256]{1,0:T(8,128)(2,1)S(1)} %get-tuple-element.34), channel_id=1, source_target_pairs={{0,4},{1,5},{2,6},{3,7},{4,0},{5,1},{6,2},{7,3},{8,12},{9,13},{10,... | collective-permute-start | bytes 196616 | tf_op jit(solution)/shard_map/ppermute | solution.py:234
  21.7 14.7 %collective-permute-start.19 = (bf16[256,256]{1,0:T(8,128)(2,1)S(1)}, bf16[256,256]{1,0:T(8,128)(2,1)S(1)}, u32[]{:S(2)}, u32[]{:S(2)}) collective-permute-start(bf16[256,256]{1,0:T(8,128)(2,1)S(1)} %shard_map.101.refs_0_), channel_id=1, source_target_pairs={{0,4},{1,5},{2,6},{3,7},{4,0},{5,1},{6,2},{7,3},{8,12},{9,13},{10,... | collective-permute-start | bytes 393224 | tf_op jit(solution)/shard_map/ppermute | solution.py:234
  27.4 7.3 %collective-permute-start.14 = (bf16[128,256]{1,0:T(8,128)(2,1)S(1)}, bf16[128,256]{1,0:T(8,128)(2,1)S(1)}, u32[]{:S(2)}, u32[]{:S(2)}) collective-permute-start(bf16[128,256]{1,0:T(8,128)(2,1)S(1)} %shard_map.100.refs_0_), channel_id=1, source_target_pairs={{0,8},{1,9},{2,10},{3,11},{4,12},{5,13},{6,14},{7,15},{8,0},{9,1},... | collective-permute-start | bytes 196616 | tf_op jit(solution)/shard_map/ppermute | solution.py:234
  29.5 6.4 %collective-permute-start.13 = (bf16[128,256]{1,0:T(8,128)(2,1)S(1)}, bf16[128,256]{1,0:T(8,128)(2,1)S(1)}, u32[]{:S(2)}, u32[]{:S(2)}) collective-permute-start(bf16[128,256]{1,0:T(8,128)(2,1)S(1)} %shard_map.100.refs_0_), channel_id=1, source_target_pairs={{0,12},{1,13},{2,14},{3,15},{4,8},{5,9},{6,10},{7,11},{8,4},{9,5},... | collective-permute-start | bytes 196616 | tf_op jit(solution)/shard_map/ppermute | solution.py:234
  30.5 5.4 %collective-permute-start.12 = (bf16[128,256]{1,0:T(8,128)(2,1)S(1)}, bf16[128,256]{1,0:T(8,128)(2,1)S(1)}, u32[]{:S(2)}, u32[]{:S(2)}) collective-permute-start(bf16[128,256]{1,0:T(8,128)(2,1)S(1)} %shard_map.100.refs_0_), channel_id=1, source_target_pairs={{0,4},{1,5},{2,6},{3,7},{4,0},{5,1},{6,2},{7,3},{8,12},{9,13},{10,... | collective-permute-start | bytes 196616 | tf_op jit(solution)/shard_map/ppermute | solution.py:234
  31.0 5.4 %collective-permute-start.15 = (bf16[128,256]{1,0:T(8,128)(2,1)S(1)}, bf16[128,256]{1,0:T(8,128)(2,1)S(1)}, u32[]{:S(2)}, u32[]{:S(2)}) collective-permute-start(bf16[128,256]{1,0:T(8,128)(2,1)S(1)} %shard_map.100.refs_0_), channel_id=1, source_target_pairs={{0,16},{16,0},{1,17},{17,1},{2,18},{18,2},{3,19},{19,3},{4,20},{20... | collective-permute-start | bytes 196616 | tf_op jit(solution)/shard_map/ppermute | solution.py:228
  34.6 1.8 %collective-permute-start.18 = (bf16[128,256]{1,0:T(8,128)(2,1)S(1)}, bf16[128,256]{1,0:T(8,128)(2,1)S(1)}, u32[]{:S(2)}, u32[]{:S(2)}) collective-permute-start(bf16[128,256]{1,0:T(8,128)(2,1)S(1)} %collective-permute-done.14.refs_3_), channel_id=1, source_target_pairs={{0,16},{16,0},{1,17},{17,1},{2,18},{18,2},{3,19},{19,3},{4,20},{20... | collective-permute-start | bytes 196616 | tf_op jit(solution)/shard_map/ppermute | solution.py:228
  35.9 1.3 %collective-permute-start.17 = (bf16[128,256]{1,0:T(8,128)(2,1)S(1)}, bf16[128,256]{1,0:T(8,128)(2,1)S(1)}, u32[]{:S(2)}, u32[]{:S(2)}) collective-permute-start(bf16[128,256]{1,0:T(8,128)(2,1)S(1)} %collective-permute-done.13.refs_2_), channel_id=1, source_target_pairs={{0,16},{16,0},{1,17},{17,1},{2,18},{18,2},{3,19},{19,3},{4,20},{20... | collective-permute-start | bytes 196616 | tf_op jit(solution)/shard_map/ppermute | solution.py:228
  35.9 1.4 %collective-permute-start.16 = (bf16[128,256]{1,0:T(8,128)(2,1)S(1)}, bf16[128,256]{1,0:T(8,128)(2,1)S(1)}, u32[]{:S(2)}, u32[]{:S(2)}) collective-permute-start(bf16[128,256]{1,0:T(8,128)(2,1)S(1)} %collective-permute-done.12.refs_1_), channel_id=1, source_target_pairs={{0,16},{16,0},{1,17},{17,1},{2,18},{18,2},{3,19},{19,3},{4,20},{20... | collective-permute-start | bytes 196616 | tf_op jit(solution)/shard_map/ppermute | solution.py:228
  38.1 3.9 %collective-permute-start.20 = (bf16[512,256]{1,0:T(8,128)(2,1)S(1)}, bf16[512,256]{1,0:T(8,128)(2,1)S(1)}, u32[]{:S(2)}, u32[]{:S(2)}) collective-permute-start(bf16[512,256]{1,0:T(8,128)(2,1)S(1)} %get-tuple-element.36), channel_id=1, source_target_pairs={{0,16},{16,0},{1,17},{17,1},{2,18},{18,2},{3,19},{19,3},{4,20},{20... | collective-permute-start | bytes 786440 | tf_op jit(solution)/shard_map/ppermute | solution.py:228
  38.5 6.2 %collective-permute-start.21 = (bf16[128,256]{1,0:T(8,128)(2,1)S(1)}, bf16[128,256]{1,0:T(8,128)(2,1)S(1)}, u32[]{:S(2)}, u32[]{:S(2)}) collective-permute-start(bf16[128,256]{1,0:T(8,128)(2,1)S(1)} %get-tuple-element.39), channel_id=1, source_target_pairs={{0,3},{1,2},{2,1},{3,0},{4,7},{5,6},{6,5},{7,4},{8,11},{9,10},{10,... | collective-permute-start | bytes 196616 | tf_op jit(solution)/shard_map/ppermute | solution.py:231
  40.3 5.6 %collective-permute-start.22 = (bf16[128,256]{1,0:T(8,128)(2,1)S(1)}, bf16[128,256]{1,0:T(8,128)(2,1)S(1)}, u32[]{:S(2)}, u32[]{:S(2)}) collective-permute-start(bf16[128,256]{1,0:T(8,128)(2,1)S(1)} %get-tuple-element.40), channel_id=1, source_target_pairs={{0,1},{1,0},{2,3},{3,2},{4,5},{5,4},{6,7},{7,6},{8,9},{9,8},{10,11... | collective-permute-start | bytes 196616 | tf_op jit(solution)/shard_map/ppermute | solution.py:231
  40.8 5.1 %collective-permute-start.23 = (bf16[128,256]{1,0:T(8,128)(2,1)S(1)}, bf16[128,256]{1,0:T(8,128)(2,1)S(1)}, u32[]{:S(2)}, u32[]{:S(2)}) collective-permute-start(bf16[128,256]{1,0:T(8,128)(2,1)S(1)} %get-tuple-element.41), channel_id=1, source_target_pairs={{0,2},{1,3},{2,0},{3,1},{4,6},{5,7},{6,4},{7,5},{8,10},{9,11},{10,... | collective-permute-start | bytes 196616 | tf_op jit(solution)/shard_map/ppermute | solution.py:231
  42.4 6.2 %collective-permute-start.27 = (bf16[128,256]{1,0:T(8,128)(2,1)S(1)}, bf16[128,256]{1,0:T(8,128)(2,1)S(1)}, u32[]{:S(2)}, u32[]{:S(2)}) collective-permute-start(bf16[128,256]{1,0:T(8,128)(2,1)S(1)} %get-tuple-element.42), channel_id=1, source_target_pairs={{0,3},{1,2},{2,1},{3,0},{4,7},{5,6},{6,5},{7,4},{8,11},{9,10},{10,... | collective-permute-start | bytes 196616 | tf_op jit(solution)/shard_map/ppermute | solution.py:231
  44.2 5.3 %collective-permute-start.28 = (bf16[128,256]{1,0:T(8,128)(2,1)S(1)}, bf16[128,256]{1,0:T(8,128)(2,1)S(1)}, u32[]{:S(2)}, u32[]{:S(2)}) collective-permute-start(bf16[128,256]{1,0:T(8,128)(2,1)S(1)} %get-tuple-element.43), channel_id=1, source_target_pairs={{0,1},{1,0},{2,3},{3,2},{4,5},{5,4},{6,7},{7,6},{8,9},{9,8},{10,11... | collective-permute-start | bytes 196616 | tf_op jit(solution)/shard_map/ppermute | solution.py:231
  44.8 5.2 %collective-permute-start.29 = (bf16[128,256]{1,0:T(8,128)(2,1)S(1)}, bf16[128,256]{1,0:T(8,128)(2,1)S(1)}, u32[]{:S(2)}, u32[]{:S(2)}) collective-permute-start(bf16[128,256]{1,0:T(8,128)(2,1)S(1)} %get-tuple-element.44), channel_id=1, source_target_pairs={{0,2},{1,3},{2,0},{3,1},{4,6},{5,7},{6,4},{7,5},{8,10},{9,11},{10,... | collective-permute-start | bytes 196616 | tf_op jit(solution)/shard_map/ppermute | solution.py:231
  46.0 5.2 %collective-permute-start.26 = (bf16[128,256]{1,0:T(8,128)(2,1)S(1)}, bf16[128,256]{1,0:T(8,128)(2,1)S(1)}, u32[]{:S(2)}, u32[]{:S(2)}) collective-permute-start(bf16[128,256]{1,0:T(8,128)(2,1)S(1)} %shard_map.105.refs_0_), channel_id=1, source_target_pairs={{0,3},{1,2},{2,1},{3,0},{4,7},{5,6},{6,5},{7,4},{8,11},{9,10},{10,... | collective-permute-start | bytes 196616 | tf_op jit(solution)/shard_map/ppermute | solution.py:231
  48.0 4.3 %collective-permute-start.25 = (bf16[128,256]{1,0:T(8,128)(2,1)S(1)}, bf16[128,256]{1,0:T(8,128)(2,1)S(1)}, u32[]{:S(2)}, u32[]{:S(2)}) collective-permute-start(bf16[128,256]{1,0:T(8,128)(2,1)S(1)} %shard_map.105.refs_0_), channel_id=1, source_target_pairs={{0,1},{1,0},{2,3},{3,2},{4,5},{5,4},{6,7},{7,6},{8,9},{9,8},{10,11... | collective-permute-start | bytes 196616 | tf_op jit(solution)/shard_map/ppermute | solution.py:231
  48.5 4.3 %collective-permute-start.24 = (bf16[128,256]{1,0:T(8,128)(2,1)S(1)}, bf16[128,256]{1,0:T(8,128)(2,1)S(1)}, u32[]{:S(2)}, u32[]{:S(2)}) collective-permute-start(bf16[128,256]{1,0:T(8,128)(2,1)S(1)} %shard_map.105.refs_0_), channel_id=1, source_target_pairs={{0,2},{1,3},{2,0},{3,1},{4,6},{5,7},{6,4},{7,5},{8,10},{9,11},{10,... | collective-permute-start | bytes 196616 | tf_op jit(solution)/shard_map/ppermute | solution.py:231

commit v5 on v4

--- a/solution.py
+++ b/solution.py
@@ -105,7 +105,7 @@
             outs[s][at : at + block] = piece
 
 
-def forward_kernel(group, outer, near, far, order, *refs):
+def forward_kernel(group, outer, near, far, *refs):
     own = [refs[near.index(s)] for s in range(group)]
     got = [refs[group + near.index(s)] for s in range(group)]
     features_ref, adjacency = refs[2 * group], refs[-outer - 2]
@@ -113,19 +113,19 @@
     rep, z, _ = place(group)
     block, width = features_ref.shape
     half, side = block // 2, width // 2
-    for i, t in enumerate(order):
-        at = pl.ds(pl.multiple_of(lax.bitwise_xor(z, t) * half, half), half)
+    for t in range(outer):
+        at = slice(t * half, (t + 1) * half)
         for s in range(group):
             columns = slice(s * block, (s + 1) * block)
-            adjacency[i, rows(rep, half), columns] = own[s][at, :]
-            adjacency[i, rows(1 - rep, half), columns] = got[s][at, :]
+            adjacency[t, rows(rep, half), columns] = own[s][at, :]
+            adjacency[t, rows(1 - rep, half), columns] = got[s][at, :]
     panel[:block, :] = features_ref[:, rows(rep, side)]
     for s in range(1, group):
         for i in range(side // block):
             start = outer * half + i * block
             panel[s * block : (s + 1) * block, i * block : (i + 1) * block] = own[s][start : start + block, :]
     for i, t in enumerate(far):
-        part = jnp.dot(adjacency[order.index(t)], panel[...], preferred_element_type=F32)
+        part = jnp.dot(adjacency[lax.bitwise_xor(z, t)], panel[...], preferred_element_type=F32)
         outs[i][...] = part.astype(outs[i].dtype)
 
 
@@ -150,15 +150,16 @@
     out[...] = (total * scale if scale is not None else total).astype(out.dtype)
 
 
-def dense_kernel(group, near, outer, place_of, *refs):
+def dense_kernel(group, near, far, place_of, *refs):
+    outer = len(far)
     own, got, slopes_ref = refs[:outer], refs[outer : 2 * outer], refs[2 * outer]
     weight_ref, bias_ref, active_ref, keep_ref, send_ref = refs[2 * outer + 1 : 2 * outer + 6]
     outs, (agg, grad, parts) = refs[2 * outer + 6 : -3], refs[-3:]
-    rep, _, q = place(group)
+    rep, z, q = place(group)
     block, side = own[0].shape
     mine, other = rows(rep, side), rows(1 - rep, side)
     for t in range(outer):
-        at = slice(t * block, (t + 1) * block)
+        at = rows(lax.bitwise_xor(z, far[t]), block)
         agg[at, mine] = own[t][...]
         agg[at, other] = got[t][...]
         pre = jnp.dot(agg[at, :], weight_ref[:, mine], preferred_element_type=F32) + bias_ref[:, mine]
@@ -249,7 +250,7 @@
     (last,) = call(top_kernel, [((cut_rows, block), BF16)], args=(mine[-1], got_slopes))
     others = [rep_swap(x) for x in (*mine[:-1], last)]
     adjacency, *parts = call(
-        functools.partial(forward_kernel, group, outer, near, far, far_back),
+        functools.partial(forward_kernel, group, outer, near, far),
         [((outer, block, group * block), BF16), ((block, half), F32)] + [((block, half), BF16)] * (outer - 1),
         scratch=(pltpu.VMEM((group * block, half), BF16),),
         args=(*mine, *others, features),
@@ -269,7 +270,7 @@
     aggs = [outer_swap(agg, t) if t else agg for t in far_back]
     tall = outer * block
     active, keep, send, *pieces = call(
-        functools.partial(dense_kernel, group, near, outer, [order.index(t) for t in far_back]),
+        functools.partial(dense_kernel, group, near, far_back, [order.index(t) for t in far_back]),
         [((block, half), BF16), ((tall, half), F32), ((tall, half), BF16), ((width // group, half), F32)]
         + [((width // group, half), BF16)] * (group - 1),
         scratch=(

time: 53.9 us -> 54 us (level)
  transfers between devices with their start and end apart: 30 -> 30, of which waited for: 16 -> 15; matrix products, arithmetic and copies ran while one was open for 0% -> 0% of each run, Pallas kernels for 4% -> 4%
where the time goes in v5:
time: 54 us; the launch traced here: 53.8 us
  starting transfers between devices  29.6 us (55%)
  waiting for transfers between devices  17.6 us (33%)
  Pallas kernels  5.81 us (11%)
  between operations  0.8 us (1%)
    ppermute x12, starting transfers between devices, inner_swap(): return lax.ppermute(x, 'dom', [(i, i ^ s) for i in range(domains)])  14.7 us
    ppermute x8, starting transfers between devices, outer_swap(): return lax.ppermute(x, 'dom', [(i, i ^ t * group) for i in range(domains)])  12.8 us
    ppermute x8, waiting for transfers between devices, outer_swap(): return lax.ppermute(x, 'dom', [(i, i ^ t * group) for i in range(domains)])  8.7 us
    ppermute x12, waiting for transfers between devices, inner_swap(): return lax.ppermute(x, 'dom', [(i, i ^ s) for i in range(domains)])  6.81 us
    pallas_call x2, Pallas kernels, combine(): pl.pallas_call(functools.partial(combine_kernel, mine), out_shape=jax.Sha...  3.02 us
    pallas_call x11, Pallas kernels, call(): pl.pallas_call(kernel, out_shape=[jax.ShapeDtypeStruct(shape, dtype) for...  2.78 us
    ppermute x10, waiting for transfers between devices, rep_swap(): return lax.ppermute(x, 'rep', [(0, 1), (1, 0)])  2.11 us
    ppermute x10, starting transfers between devices, rep_swap(): return lax.ppermute(x, 'rep', [(0, 1), (1, 0)])  2.03 us
  transfers between devices with their start and end apart: 30, of which 15 were waited for; matrix products, arithmetic and copies ran while one was open for 0% of the time, Pallas kernels for 4%

profile of v5, /device:TPU:0, one launch (start us, length us, event | category | flops | bytes accessed | tf_op | source)
XLA Modules:
  0.0 53.8 jit_solution(13674097520893691938)
XLA Ops:
  0.6 1.5 %shard_map.95 = bf16[16,64,128]{2,1,0:T(8,128)(2,1)S(1)} custom-call(s32[64]{0:T(128)} %bitcast.3, s32[64]{0:T(128)} %count_hbm.3, bf16[64,128,128]{2,1,0:T(8,128)(2,1)} %tiles_hbm.3), custom_call_target="tpu_custom_call" | custom-call | flops 1024 | bytes 1024 | tf_op jit(solution)/shard_map/pallas_call | solution.py:71
  2.2 0.5 collective-permute-start
  2.7 1.5 %shard_map.94.own_ref = bf16[16,64,128]{2,1,0:T(8,128)(2,1)S(1)} custom-call(s32[64]{0:T(128)} %bitcast.4, s32[64]{0:T(128)} %count_hbm.3, bf16[64,128,128]{2,1,0:T(8,128)(2,1)} %tiles_hbm.3), custom_call_target="tpu_custom_call" | custom-call | flops 1024 | bytes 1024 | tf_op jit(solution)/shard_map/pallas_call | solution.py:71
  4.3 0.1 shard_map.96
  4.3 3.5 %collective-permute-start.1 = (bf16[512,128]{1,0:T(8,128)(2,1)S(1)}, bf16[512,128]{1,0:T(8,128)(2,1)S(1)}, u32[]{:S(2)}, u32[]{:S(2)}) collective-permute-start(bf16[512,128]{1,0:T(8,128)(2,1)S(1)} %get-tuple-element.27), channel_id=1, source_target_pairs={{0,3},{1,2},{2,1},{3,0},{4,7},{5,6},{6,5},{7,4},{8,11},{9,10},{10,... | collective-permute-start | bytes 393224 | tf_op jit(solution)/shard_map/ppermute | solution.py:232
  7.9 0.5 collective-permute-start.2
  8.4 0.1 collective-permute-start.3
  8.5 3.1 %collective-permute-start.7 = (bf16[128,256]{1,0:T(8,128)(2,1)S(1)}, bf16[128,256]{1,0:T(8,128)(2,1)S(1)}, u32[]{:S(2)}, u32[]{:S(2)}) collective-permute-start(bf16[128,256]{1,0:T(8,128)(2,1)S(1)} %shard_map.97.refs_0_), channel_id=1, source_target_pairs={{0,8},{1,9},{2,10},{3,11},{4,12},{5,13},{6,14},{7,15},{8,0},{9,1},... | collective-permute-start | bytes 196616 | tf_op jit(solution)/shard_map/ppermute | solution.py:235
  11.6 0.6 %collective-permute-done.1.refs_1_ = bf16[512,128]{1,0:T(8,128)(2,1)S(1)} collective-permute-done((bf16[512,128]{1,0:T(8,128)(2,1)S(1)}, bf16[512,128]{1,0:T(8,128)(2,1)S(1)}, u32[]{:S(2)}, u32[]{:S(2)}) %collective-permute-start.1) | collective-permute-done | bytes 131104 | tf_op jit(solution)/shard_map/ppermute | solution.py:232
  12.2 2.9 %collective-permute-done.2.refs_2_ = bf16[512,128]{1,0:T(8,128)(2,1)S(1)} collective-permute-done((bf16[512,128]{1,0:T(8,128)(2,1)S(1)}, bf16[512,128]{1,0:T(8,128)(2,1)S(1)}, u32[]{:S(2)}, u32[]{:S(2)}) %collective-permute-start.2) | collective-permute-done | bytes 131104 | tf_op jit(solution)/shard_map/ppermute | solution.py:232
  15.1 0.5 collective-permute-start.4
  15.6 0.1 collective-permute-start.8
  15.7 0.8 %collective-permute-done.4.refs_4_ = bf16[256,128]{1,0:T(8,128)(2,1)S(1)} collective-permute-done((bf16[256,128]{1,0:T(8,128)(2,1)S(1)}, bf16[256,128]{1,0:T(8,128)(2,1)S(1)}, u32[]{:S(2)}, u32[]{:S(2)}) %collective-permute-start.4) | collective-permute-done | bytes 65568 | tf_op jit(solution)/shard_map/ppermute | solution.py:229
  16.6 0.4 collective-permute-done.8.refs_7_
  17.0 0.4 shard_map.99
  17.4 2.7 %collective-permute-start.9 = (bf16[128,256]{1,0:T(8,128)(2,1)S(1)}, bf16[128,256]{1,0:T(8,128)(2,1)S(1)}, u32[]{:S(2)}, u32[]{:S(2)}) collective-permute-start(bf16[128,256]{1,0:T(8,128)(2,1)S(1)} %get-tuple-element.32), channel_id=1, source_target_pairs={{0,8},{1,9},{2,10},{3,11},{4,12},{5,13},{6,14},{7,15},{8,0},{9,1},... | collective-permute-start | bytes 196616 | tf_op jit(solution)/shard_map/ppermute | solution.py:235
  20.0 1.3 %collective-permute-start.10 = (bf16[128,256]{1,0:T(8,128)(2,1)S(1)}, bf16[128,256]{1,0:T(8,128)(2,1)S(1)}, u32[]{:S(2)}, u32[]{:S(2)}) collective-permute-start(bf16[128,256]{1,0:T(8,128)(2,1)S(1)} %get-tuple-element.33), channel_id=1, source_target_pairs={{0,12},{1,13},{2,14},{3,15},{4,8},{5,9},{6,10},{7,11},{8,4},{9,5},... | collective-permute-start | bytes 196616 | tf_op jit(solution)/shard_map/ppermute | solution.py:235
  21.4 0.2 collective-permute-start.11
  21.6 1.9 %collective-permute-start.19 = (bf16[256,256]{1,0:T(8,128)(2,1)S(1)}, bf16[256,256]{1,0:T(8,128)(2,1)S(1)}, u32[]{:S(2)}, u32[]{:S(2)}) collective-permute-start(bf16[256,256]{1,0:T(8,128)(2,1)S(1)} %shard_map.101.refs_0_), channel_id=1, source_target_pairs={{0,4},{1,5},{2,6},{3,7},{4,0},{5,1},{6,2},{7,3},{8,12},{9,13},{10,... | collective-permute-start | bytes 393224 | tf_op jit(solution)/shard_map/ppermute | solution.py:235
  23.5 1.0 %collective-permute-done.9.refs_1_ = bf16[128,256]{1,0:T(8,128)(2,1)S(1)} collective-permute-done((bf16[128,256]{1,0:T(8,128)(2,1)S(1)}, bf16[128,256]{1,0:T(8,128)(2,1)S(1)}, u32[]{:S(2)}, u32[]{:S(2)}) %collective-permute-start.9) | collective-permute-done | bytes 65568 | tf_op jit(solution)/shard_map/ppermute | solution.py:235
  24.5 2.4 %collective-permute-done.10.refs_2_ = bf16[128,256]{1,0:T(8,128)(2,1)S(1)} collective-permute-done((bf16[128,256]{1,0:T(8,128)(2,1)S(1)}, bf16[128,256]{1,0:T(8,128)(2,1)S(1)}, u32[]{:S(2)}, u32[]{:S(2)}) %collective-permute-start.10) | collective-permute-done | bytes 65568 | tf_op jit(solution)/shard_map/ppermute | solution.py:235
  26.8 0.5 collective-permute-done.11.refs_3_
  27.4 2.1 %collective-permute-start.14 = (bf16[128,256]{1,0:T(8,128)(2,1)S(1)}, bf16[128,256]{1,0:T(8,128)(2,1)S(1)}, u32[]{:S(2)}, u32[]{:S(2)}) collective-permute-start(bf16[128,256]{1,0:T(8,128)(2,1)S(1)} %shard_map.100.refs_0_), channel_id=1, source_target_pairs={{0,8},{1,9},{2,10},{3,11},{4,12},{5,13},{6,14},{7,15},{8,0},{9,1},... | collective-permute-start | bytes 196616 | tf_op jit(solution)/shard_map/ppermute | solution.py:235
  29.5 1.0 %collective-permute-start.13 = (bf16[128,256]{1,0:T(8,128)(2,1)S(1)}, bf16[128,256]{1,0:T(8,128)(2,1)S(1)}, u32[]{:S(2)}, u32[]{:S(2)}) collective-permute-start(bf16[128,256]{1,0:T(8,128)(2,1)S(1)} %shard_map.100.refs_0_), channel_id=1, source_target_pairs={{0,12},{1,13},{2,14},{3,15},{4,8},{5,9},{6,10},{7,11},{8,4},{9,5},... | collective-permute-start | bytes 196616 | tf_op jit(solution)/shard_map/ppermute | solution.py:235
  30.5 0.5 collective-permute-start.12
  31.0 3.6 %collective-permute-done.14.refs_3_ = bf16[128,256]{1,0:T(8,128)(2,1)S(1)} collective-permute-done((bf16[128,256]{1,0:T(8,128)(2,1)S(1)}, bf16[128,256]{1,0:T(8,128)(2,1)S(1)}, u32[]{:S(2)}, u32[]{:S(2)}) %collective-permute-start.14) | collective-permute-done | bytes 65568 | tf_op jit(solution)/shard_map/ppermute | solution.py:235
  34.5 1.3 %collective-permute-done.13.refs_2_ = bf16[128,256]{1,0:T(8,128)(2,1)S(1)} collective-permute-done((bf16[128,256]{1,0:T(8,128)(2,1)S(1)}, bf16[128,256]{1,0:T(8,128)(2,1)S(1)}, u32[]{:S(2)}, u32[]{:S(2)}) %collective-permute-start.13) | collective-permute-done | bytes 65568 | tf_op jit(solution)/shard_map/ppermute | solution.py:235
  35.8 0.0 collective-permute-done.12.refs_1_
  35.9 0.5 collective-permute-start.16
  36.4 0.7 %collective-permute-done.17.refs_6_ = bf16[128,256]{1,0:T(8,128)(2,1)S(1)} collective-permute-done((bf16[128,256]{1,0:T(8,128)(2,1)S(1)}, bf16[128,256]{1,0:T(8,128)(2,1)S(1)}, u32[]{:S(2)}, u32[]{:S(2)}) %collective-permute-start.17) | collective-permute-done | bytes 65568 | tf_op jit(solution)/shard_map/ppermute | solution.py:229
  37.1 0.2 collective-permute-done.16.refs_5_
  37.3 0.9 %shard_map.103 = (bf16[128,256]{1,0:T(8,128)(2,1)S(1)}, f32[512,256]{1,0:T(8,128)S(1)}, bf16[512,256]{1,0:T(8,128)(2,1)S(1)}, f32[128,256]{1,0:T(8,128)S(1)}, bf...) custom-call(bf16[128,256]{1,0:T(8,128)(2,1)S(1)} %shard_map.100.refs_0_, ...), custom_call_target="tpu_custom_call" | custom-call | flops 1024 | bytes 1024 | tf_op jit(solution)/shard_map/pallas_call | solution.py:28
  38.2 0.4 collective-permute-start.20
  38.6 1.8 %collective-permute-start.21 = (bf16[128,256]{1,0:T(8,128)(2,1)S(1)}, bf16[128,256]{1,0:T(8,128)(2,1)S(1)}, u32[]{:S(2)}, u32[]{:S(2)}) collective-permute-start(bf16[128,256]{1,0:T(8,128)(2,1)S(1)} %get-tuple-element.39), channel_id=1, source_target_pairs={{0,3},{1,2},{2,1},{3,0},{4,7},{5,6},{6,5},{7,4},{8,11},{9,10},{10,... | collective-permute-start | bytes 196616 | tf_op jit(solution)/shard_map/ppermute | solution.py:232
  40.4 0.5 collective-permute-start.22
  40.9 1.2 %collective-permute-start.23 = (bf16[128,256]{1,0:T(8,128)(2,1)S(1)}, bf16[128,256]{1,0:T(8,128)(2,1)S(1)}, u32[]{:S(2)}, u32[]{:S(2)}) collective-permute-start(bf16[128,256]{1,0:T(8,128)(2,1)S(1)} %get-tuple-element.41), channel_id=1, source_target_pairs={{0,2},{1,3},{2,0},{3,1},{4,6},{5,7},{6,4},{7,5},{8,10},{9,11},{10,... | collective-permute-start | bytes 196616 | tf_op jit(solution)/shard_map/ppermute | solution.py:232
  42.1 0.4 shard_map.104
  42.5 1.8 %collective-permute-start.27 = (bf16[128,256]{1,0:T(8,128)(2,1)S(1)}, bf16[128,256]{1,0:T(8,128)(2,1)S(1)}, u32[]{:S(2)}, u32[]{:S(2)}) collective-permute-start(bf16[128,256]{1,0:T(8,128)(2,1)S(1)} %get-tuple-element.42), channel_id=1, source_target_pairs={{0,3},{1,2},{2,1},{3,0},{4,7},{5,6},{6,5},{7,4},{8,11},{9,10},{10,... | collective-permute-start | bytes 196616 | tf_op jit(solution)/shard_map/ppermute | solution.py:232
  44.3 0.6 %collective-permute-start.28 = (bf16[128,256]{1,0:T(8,128)(2,1)S(1)}, bf16[128,256]{1,0:T(8,128)(2,1)S(1)}, u32[]{:S(2)}, u32[]{:S(2)}) collective-permute-start(bf16[128,256]{1,0:T(8,128)(2,1)S(1)} %get-tuple-element.43), channel_id=1, source_target_pairs={{0,1},{1,0},{2,3},{3,2},{4,5},{5,4},{6,7},{7,6},{8,9},{9,8},{10,11... | collective-permute-start | bytes 196616 | tf_op jit(solution)/shard_map/ppermute | solution.py:232
  44.8 1.2 %collective-permute-start.29 = (bf16[128,256]{1,0:T(8,128)(2,1)S(1)}, bf16[128,256]{1,0:T(8,128)(2,1)S(1)}, u32[]{:S(2)}, u32[]{:S(2)}) collective-permute-start(bf16[128,256]{1,0:T(8,128)(2,1)S(1)} %get-tuple-element.44), channel_id=1, source_target_pairs={{0,2},{1,3},{2,0},{3,1},{4,6},{5,7},{6,4},{7,5},{8,10},{9,11},{10,... | collective-permute-start | bytes 196616 | tf_op jit(solution)/shard_map/ppermute | solution.py:232
  46.1 2.0 %collective-permute-start.26 = (bf16[128,256]{1,0:T(8,128)(2,1)S(1)}, bf16[128,256]{1,0:T(8,128)(2,1)S(1)}, u32[]{:S(2)}, u32[]{:S(2)}) collective-permute-start(bf16[128,256]{1,0:T(8,128)(2,1)S(1)} %shard_map.105.refs_0_), channel_id=1, source_target_pairs={{0,3},{1,2},{2,1},{3,0},{4,7},{5,6},{6,5},{7,4},{8,11},{9,10},{10,... | collective-permute-start | bytes 196616 | tf_op jit(solution)/shard_map/ppermute | solution.py:232
  48.1 0.5 collective-permute-start.25
  48.6 1.0 %collective-permute-start.24 = (bf16[128,256]{1,0:T(8,128)(2,1)S(1)}, bf16[128,256]{1,0:T(8,128)(2,1)S(1)}, u32[]{:S(2)}, u32[]{:S(2)}) collective-permute-start(bf16[128,256]{1,0:T(8,128)(2,1)S(1)} %shard_map.105.refs_0_), channel_id=1, source_target_pairs={{0,2},{1,3},{2,0},{3,1},{4,6},{5,7},{6,4},{7,5},{8,10},{9,11},{10,... | collective-permute-start | bytes 196616 | tf_op jit(solution)/shard_map/ppermute | solution.py:232
  49.6 0.4 collective-permute-done.29.refs_7_
  50.0 1.3 %collective-permute-done.26.refs_3_ = bf16[128,256]{1,0:T(8,128)(2,1)S(1)} collective-permute-done((bf16[128,256]{1,0:T(8,128)(2,1)S(1)}, bf16[128,256]{1,0:T(8,128)(2,1)S(1)}, u32[]{:S(2)}, u32[]{:S(2)}) %collective-permute-start.26) | collective-permute-done | bytes 65568 | tf_op jit(solution)/shard_map/ppermute | solution.py:232
  51.3 1.0 %collective-permute-done.25.refs_2_ = bf16[128,256]{1,0:T(8,128)(2,1)S(1)} collective-permute-done((bf16[128,256]{1,0:T(8,128)(2,1)S(1)}, bf16[128,256]{1,0:T(8,128)(2,1)S(1)}, u32[]{:S(2)}, u32[]{:S(2)}) %collective-permute-start.25) | collective-permute-done | bytes 65568 | tf_op jit(solution)/shard_map/ppermute | solution.py:232
  52.4 0.5 %collective-permute-done.24.refs_1_ = bf16[128,256]{1,0:T(8,128)(2,1)S(1)} collective-permute-done((bf16[128,256]{1,0:T(8,128)(2,1)S(1)}, bf16[128,256]{1,0:T(8,128)(2,1)S(1)}, u32[]{:S(2)}, u32[]{:S(2)}) %collective-permute-start.24) | collective-permute-done | bytes 65568 | tf_op jit(solution)/shard_map/ppermute | solution.py:232
  52.9 0.9 %shard_map.106 = (f32[512,256]{1,0:T(8,128)}, bf16[128,256]{1,0:T(8,128)(2,1)}, bf16[128,256]{1,0:T(8,128)(2,1)}) custom-call(bf16[128,256]{1,0:T(8,128)(2,1)S(1)} %shard_map.105.refs_0_, bf16[128,256]{1,0:T(8,128)(2,1)S(1)} %collective-permute-done.24.refs_1_, bf16[128,256]{1,0:T(8,128)(2,1)S(1)} %collective-permute-done.25.refs_2_, ...), custom_call_target="tpu_custom_call" | custom-call | flops 1024 | bytes 1024 | tf_op jit(solution)/shard_map/pallas_call | solution.py:28
  (33 shorter events, 0.2 us)
Async XLA Ops:
  0.6 3.6 %copy-start.1 = (bf16[128,512]{1,0:T(8,128)(2,1)S(1)}, bf16[128,512]{1,0:T(8,128)(2,1)}, u32[]{:S(2)}) copy-start(bf16[128,512]{1,0:T(8,128)(2,1)} %refs_8_.1) | copy-start | bytes 393220
  2.2 6.3 %copy-start.2 = (bf16[128,512]{1,0:T(8,128)(2,1)S(1)}, bf16[128,512]{1,0:T(8,128)(2,1)}, u32[]{:S(2)}) copy-start(bf16[128,512]{1,0:T(8,128)(2,1)} %whole_ref.1) | copy-start | bytes 393220
  2.2 2.0 %collective-permute-start = (bf16[16,64,128]{2,1,0:T(8,128)(2,1)S(1)}, bf16[16,64,128]{2,1,0:T(8,128)(2,1)S(1)}, u32[]{:S(2)}, u32[]{:S(2)}) collective-permute-start(bf16[16,64,128]{2,1,0:T(8,128)(2,1)S(1)} %shard_map.95), channel_id=1, source_target_pairs={{0,16},{16,0},{1,17},{17,1},{2,18},{18,2},{3,19},{19,3},{4,20},{20... | collective-permute-start | bytes 786440 | tf_op jit(solution)/shard_map/ppermute | solution.py:229
  4.2 33.1 %copy-start = (bf16[512,512]{1,0:T(8,128)(2,1)S(1)}, bf16[512,512]{1,0:T(8,128)(2,1)}, u32[]{:S(2)}) copy-start(bf16[512,512]{1,0:T(8,128)(2,1)} %refs_9_.1) | copy-start | bytes 1572868
  4.2 33.0 %copy-start.3 = (f32[512]{0:T(512)S(1)}, f32[512]{0:T(512)}, u32[]{:S(2)}) copy-start(f32[512]{0:T(512)} %param.12) | copy-start | bytes 6148
  4.3 7.9 %collective-permute-start.1 = (bf16[512,128]{1,0:T(8,128)(2,1)S(1)}, bf16[512,128]{1,0:T(8,128)(2,1)S(1)}, u32[]{:S(2)}, u32[]{:S(2)}) collective-permute-start(bf16[512,128]{1,0:T(8,128)(2,1)S(1)} %get-tuple-element.27), channel_id=1, source_target_pairs={{0,3},{1,2},{2,1},{3,0},{4,7},{5,6},{6,5},{7,4},{8,11},{9,10},{10,... | collective-permute-start | bytes 393224 | tf_op jit(solution)/shard_map/ppermute | solution.py:232
  7.9 7.3 %collective-permute-start.2 = (bf16[512,128]{1,0:T(8,128)(2,1)S(1)}, bf16[512,128]{1,0:T(8,128)(2,1)S(1)}, u32[]{:S(2)}, u32[]{:S(2)}) collective-permute-start(bf16[512,128]{1,0:T(8,128)(2,1)S(1)} %get-tuple-element.28), channel_id=1, source_target_pairs={{0,1},{1,0},{2,3},{3,2},{4,5},{5,4},{6,7},{7,6},{8,9},{9,8},{10,11... | collective-permute-start | bytes 393224 | tf_op jit(solution)/shard_map/ppermute | solution.py:232
  8.4 7.2 %collective-permute-start.3 = (bf16[512,128]{1,0:T(8,128)(2,1)S(1)}, bf16[512,128]{1,0:T(8,128)(2,1)S(1)}, u32[]{:S(2)}, u32[]{:S(2)}) collective-permute-start(bf16[512,128]{1,0:T(8,128)(2,1)S(1)} %get-tuple-element.29), channel_id=1, source_target_pairs={{0,2},{1,3},{2,0},{3,1},{4,6},{5,7},{6,4},{7,5},{8,10},{9,11},{10,... | collective-permute-start | bytes 393224 | tf_op jit(solution)/shard_map/ppermute | solution.py:232
  8.5 7.1 %collective-permute-start.7 = (bf16[128,256]{1,0:T(8,128)(2,1)S(1)}, bf16[128,256]{1,0:T(8,128)(2,1)S(1)}, u32[]{:S(2)}, u32[]{:S(2)}) collective-permute-start(bf16[128,256]{1,0:T(8,128)(2,1)S(1)} %shard_map.97.refs_0_), channel_id=1, source_target_pairs={{0,8},{1,9},{2,10},{3,11},{4,12},{5,13},{6,14},{7,15},{8,0},{9,1},... | collective-permute-start | bytes 196616 | tf_op jit(solution)/shard_map/ppermute | solution.py:235
  12.2 4.8 %collective-permute-start.5 = (bf16[512,128]{1,0:T(8,128)(2,1)S(1)}, bf16[512,128]{1,0:T(8,128)(2,1)S(1)}, u32[]{:S(2)}, u32[]{:S(2)}) collective-permute-start(bf16[512,128]{1,0:T(8,128)(2,1)S(1)} %collective-permute-done.1.refs_1_), channel_id=1, source_target_pairs={{0,16},{16,0},{1,17},{17,1},{2,18},{18,2},{3,19},{19,3},{4,20},{20... | collective-permute-start | bytes 393224 | tf_op jit(solution)/shard_map/ppermute | solution.py:229
  15.1 1.9 %collective-permute-start.6 = (bf16[512,128]{1,0:T(8,128)(2,1)S(1)}, bf16[512,128]{1,0:T(8,128)(2,1)S(1)}, u32[]{:S(2)}, u32[]{:S(2)}) collective-permute-start(bf16[512,128]{1,0:T(8,128)(2,1)S(1)} %collective-permute-done.2.refs_2_), channel_id=1, source_target_pairs={{0,16},{16,0},{1,17},{17,1},{2,18},{18,2},{3,19},{19,3},{4,20},{20... | collective-permute-start | bytes 393224 | tf_op jit(solution)/shard_map/ppermute | solution.py:229
  15.1 1.4 %collective-permute-start.4 = (bf16[256,128]{1,0:T(8,128)(2,1)S(1)}, bf16[256,128]{1,0:T(8,128)(2,1)S(1)}, u32[]{:S(2)}, u32[]{:S(2)}) collective-permute-start(bf16[256,128]{1,0:T(8,128)(2,1)S(1)} %get-tuple-element.26.refs_0_), channel_id=1, source_target_pairs={{0,16},{16,0},{1,17},{17,1},{2,18},{18,2},{3,19},{19,3},{4,20},{20... | collective-permute-start | bytes 196616 | tf_op jit(solution)/shard_map/ppermute | solution.py:229
  15.6 1.3 %collective-permute-start.8 = (bf16[256,128]{1,0:T(8,128)(2,1)S(1)}, bf16[256,128]{1,0:T(8,128)(2,1)S(1)}, u32[]{:S(2)}, u32[]{:S(2)}) collective-permute-start(bf16[256,128]{1,0:T(8,128)(2,1)S(1)} %shard_map.98), channel_id=1, source_target_pairs={{0,16},{16,0},{1,17},{17,1},{2,18},{18,2},{3,19},{19,3},{4,20},{20... | collective-permute-start | bytes 196616 | tf_op jit(solution)/shard_map/ppermute | solution.py:229
  17.4 7.1 %collective-permute-start.9 = (bf16[128,256]{1,0:T(8,128)(2,1)S(1)}, bf16[128,256]{1,0:T(8,128)(2,1)S(1)}, u32[]{:S(2)}, u32[]{:S(2)}) collective-permute-start(bf16[128,256]{1,0:T(8,128)(2,1)S(1)} %get-tuple-element.32), channel_id=1, source_target_pairs={{0,8},{1,9},{2,10},{3,11},{4,12},{5,13},{6,14},{7,15},{8,0},{9,1},... | collective-permute-start | bytes 196616 | tf_op jit(solution)/shard_map/ppermute | solution.py:235
  20.0 6.8 %collective-permute-start.10 = (bf16[128,256]{1,0:T(8,128)(2,1)S(1)}, bf16[128,256]{1,0:T(8,128)(2,1)S(1)}, u32[]{:S(2)}, u32[]{:S(2)}) collective-permute-start(bf16[128,256]{1,0:T(8,128)(2,1)S(1)} %get-tuple-element.33), channel_id=1, source_target_pairs={{0,12},{1,13},{2,14},{3,15},{4,8},{5,9},{6,10},{7,11},{8,4},{9,5},... | collective-permute-start | bytes 196616 | tf_op jit(solution)/shard_map/ppermute | solution.py:235
  21.4 5.9 %collective-permute-start.11 = (bf16[128,256]{1,0:T(8,128)(2,1)S(1)}, bf16[128,256]{1,0:T(8,128)(2,1)S(1)}, u32[]{:S(2)}, u32[]{:S(2)}) collective-permute-start(bf16[128,256]{1,0:T(8,128)(2,1)S(1)} %get-tuple-element.34), channel_id=1, source_target_pairs={{0,4},{1,5},{2,6},{3,7},{4,0},{5,1},{6,2},{7,3},{8,12},{9,13},{10,... | collective-permute-start | bytes 196616 | tf_op jit(solution)/shard_map/ppermute | solution.py:235
  21.6 14.7 %collective-permute-start.19 = (bf16[256,256]{1,0:T(8,128)(2,1)S(1)}, bf16[256,256]{1,0:T(8,128)(2,1)S(1)}, u32[]{:S(2)}, u32[]{:S(2)}) collective-permute-start(bf16[256,256]{1,0:T(8,128)(2,1)S(1)} %shard_map.101.refs_0_), channel_id=1, source_target_pairs={{0,4},{1,5},{2,6},{3,7},{4,0},{5,1},{6,2},{7,3},{8,12},{9,13},{10,... | collective-permute-start | bytes 393224 | tf_op jit(solution)/shard_map/ppermute | solution.py:235
  27.4 7.2 %collective-permute-start.14 = (bf16[128,256]{1,0:T(8,128)(2,1)S(1)}, bf16[128,256]{1,0:T(8,128)(2,1)S(1)}, u32[]{:S(2)}, u32[]{:S(2)}) collective-permute-start(bf16[128,256]{1,0:T(8,128)(2,1)S(1)} %shard_map.100.refs_0_), channel_id=1, source_target_pairs={{0,8},{1,9},{2,10},{3,11},{4,12},{5,13},{6,14},{7,15},{8,0},{9,1},... | collective-permute-start | bytes 196616 | tf_op jit(solution)/shard_map/ppermute | solution.py:235
  29.5 6.4 %collective-permute-start.13 = (bf16[128,256]{1,0:T(8,128)(2,1)S(1)}, bf16[128,256]{1,0:T(8,128)(2,1)S(1)}, u32[]{:S(2)}, u32[]{:S(2)}) collective-permute-start(bf16[128,256]{1,0:T(8,128)(2,1)S(1)} %shard_map.100.refs_0_), channel_id=1, source_target_pairs={{0,12},{1,13},{2,14},{3,15},{4,8},{5,9},{6,10},{7,11},{8,4},{9,5},... | collective-permute-start | bytes 196616 | tf_op jit(solution)/shard_map/ppermute | solution.py:235
  30.5 5.4 %collective-permute-start.12 = (bf16[128,256]{1,0:T(8,128)(2,1)S(1)}, bf16[128,256]{1,0:T(8,128)(2,1)S(1)}, u32[]{:S(2)}, u32[]{:S(2)}) collective-permute-start(bf16[128,256]{1,0:T(8,128)(2,1)S(1)} %shard_map.100.refs_0_), channel_id=1, source_target_pairs={{0,4},{1,5},{2,6},{3,7},{4,0},{5,1},{6,2},{7,3},{8,12},{9,13},{10,... | collective-permute-start | bytes 196616 | tf_op jit(solution)/shard_map/ppermute | solution.py:235
  31.0 5.4 %collective-permute-start.15 = (bf16[128,256]{1,0:T(8,128)(2,1)S(1)}, bf16[128,256]{1,0:T(8,128)(2,1)S(1)}, u32[]{:S(2)}, u32[]{:S(2)}) collective-permute-start(bf16[128,256]{1,0:T(8,128)(2,1)S(1)} %shard_map.100.refs_0_), channel_id=1, source_target_pairs={{0,16},{16,0},{1,17},{17,1},{2,18},{18,2},{3,19},{19,3},{4,20},{20... | collective-permute-start | bytes 196616 | tf_op jit(solution)/shard_map/ppermute | solution.py:229
  34.5 1.9 %collective-permute-start.18 = (bf16[128,256]{1,0:T(8,128)(2,1)S(1)}, bf16[128,256]{1,0:T(8,128)(2,1)S(1)}, u32[]{:S(2)}, u32[]{:S(2)}) collective-permute-start(bf16[128,256]{1,0:T(8,128)(2,1)S(1)} %collective-permute-done.14.refs_3_), channel_id=1, source_target_pairs={{0,16},{16,0},{1,17},{17,1},{2,18},{18,2},{3,19},{19,3},{4,20},{20... | collective-permute-start | bytes 196616 | tf_op jit(solution)/shard_map/ppermute | solution.py:229
  35.8 1.3 %collective-permute-start.17 = (bf16[128,256]{1,0:T(8,128)(2,1)S(1)}, bf16[128,256]{1,0:T(8,128)(2,1)S(1)}, u32[]{:S(2)}, u32[]{:S(2)}) collective-permute-start(bf16[128,256]{1,0:T(8,128)(2,1)S(1)} %collective-permute-done.13.refs_2_), channel_id=1, source_target_pairs={{0,16},{16,0},{1,17},{17,1},{2,18},{18,2},{3,19},{19,3},{4,20},{20... | collective-permute-start | bytes 196616 | tf_op jit(solution)/shard_map/ppermute | solution.py:229
  35.9 1.4 %collective-permute-start.16 = (bf16[128,256]{1,0:T(8,128)(2,1)S(1)}, bf16[128,256]{1,0:T(8,128)(2,1)S(1)}, u32[]{:S(2)}, u32[]{:S(2)}) collective-permute-start(bf16[128,256]{1,0:T(8,128)(2,1)S(1)} %collective-permute-done.12.refs_1_), channel_id=1, source_target_pairs={{0,16},{16,0},{1,17},{17,1},{2,18},{18,2},{3,19},{19,3},{4,20},{20... | collective-permute-start | bytes 196616 | tf_op jit(solution)/shard_map/ppermute | solution.py:229
  38.2 3.9 %collective-permute-start.20 = (bf16[512,256]{1,0:T(8,128)(2,1)S(1)}, bf16[512,256]{1,0:T(8,128)(2,1)S(1)}, u32[]{:S(2)}, u32[]{:S(2)}) collective-permute-start(bf16[512,256]{1,0:T(8,128)(2,1)S(1)} %get-tuple-element.36), channel_id=1, source_target_pairs={{0,16},{16,0},{1,17},{17,1},{2,18},{18,2},{3,19},{19,3},{4,20},{20... | collective-permute-start | bytes 786440 | tf_op jit(solution)/shard_map/ppermute | solution.py:229
  38.6 6.3 %collective-permute-start.21 = (bf16[128,256]{1,0:T(8,128)(2,1)S(1)}, bf16[128,256]{1,0:T(8,128)(2,1)S(1)}, u32[]{:S(2)}, u32[]{:S(2)}) collective-permute-start(bf16[128,256]{1,0:T(8,128)(2,1)S(1)} %get-tuple-element.39), channel_id=1, source_target_pairs={{0,3},{1,2},{2,1},{3,0},{4,7},{5,6},{6,5},{7,4},{8,11},{9,10},{10,... | collective-permute-start | bytes 196616 | tf_op jit(solution)/shard_map/ppermute | solution.py:232
  40.4 5.7 %collective-permute-start.22 = (bf16[128,256]{1,0:T(8,128)(2,1)S(1)}, bf16[128,256]{1,0:T(8,128)(2,1)S(1)}, u32[]{:S(2)}, u32[]{:S(2)}) collective-permute-start(bf16[128,256]{1,0:T(8,128)(2,1)S(1)} %get-tuple-element.40), channel_id=1, source_target_pairs={{0,1},{1,0},{2,3},{3,2},{4,5},{5,4},{6,7},{7,6},{8,9},{9,8},{10,11... | collective-permute-start | bytes 196616 | tf_op jit(solution)/shard_map/ppermute | solution.py:232
  40.9 5.1 %collective-permute-start.23 = (bf16[128,256]{1,0:T(8,128)(2,1)S(1)}, bf16[128,256]{1,0:T(8,128)(2,1)S(1)}, u32[]{:S(2)}, u32[]{:S(2)}) collective-permute-start(bf16[128,256]{1,0:T(8,128)(2,1)S(1)} %get-tuple-element.41), channel_id=1, source_target_pairs={{0,2},{1,3},{2,0},{3,1},{4,6},{5,7},{6,4},{7,5},{8,10},{9,11},{10,... | collective-permute-start | bytes 196616 | tf_op jit(solution)/shard_map/ppermute | solution.py:232
  42.5 6.2 %collective-permute-start.27 = (bf16[128,256]{1,0:T(8,128)(2,1)S(1)}, bf16[128,256]{1,0:T(8,128)(2,1)S(1)}, u32[]{:S(2)}, u32[]{:S(2)}) collective-permute-start(bf16[128,256]{1,0:T(8,128)(2,1)S(1)} %get-tuple-element.42), channel_id=1, source_target_pairs={{0,3},{1,2},{2,1},{3,0},{4,7},{5,6},{6,5},{7,4},{8,11},{9,10},{10,... | collective-permute-start | bytes 196616 | tf_op jit(solution)/shard_map/ppermute | solution.py:232
  44.3 5.4 %collective-permute-start.28 = (bf16[128,256]{1,0:T(8,128)(2,1)S(1)}, bf16[128,256]{1,0:T(8,128)(2,1)S(1)}, u32[]{:S(2)}, u32[]{:S(2)}) collective-permute-start(bf16[128,256]{1,0:T(8,128)(2,1)S(1)} %get-tuple-element.43), channel_id=1, source_target_pairs={{0,1},{1,0},{2,3},{3,2},{4,5},{5,4},{6,7},{7,6},{8,9},{9,8},{10,11... | collective-permute-start | bytes 196616 | tf_op jit(solution)/shard_map/ppermute | solution.py:232
  44.8 5.2 %collective-permute-start.29 = (bf16[128,256]{1,0:T(8,128)(2,1)S(1)}, bf16[128,256]{1,0:T(8,128)(2,1)S(1)}, u32[]{:S(2)}, u32[]{:S(2)}) collective-permute-start(bf16[128,256]{1,0:T(8,128)(2,1)S(1)} %get-tuple-element.44), channel_id=1, source_target_pairs={{0,2},{1,3},{2,0},{3,1},{4,6},{5,7},{6,4},{7,5},{8,10},{9,11},{10,... | collective-permute-start | bytes 196616 | tf_op jit(solution)/shard_map/ppermute | solution.py:232
  46.1 5.2 %collective-permute-start.26 = (bf16[128,256]{1,0:T(8,128)(2,1)S(1)}, bf16[128,256]{1,0:T(8,128)(2,1)S(1)}, u32[]{:S(2)}, u32[]{:S(2)}) collective-permute-start(bf16[128,256]{1,0:T(8,128)(2,1)S(1)} %shard_map.105.refs_0_), channel_id=1, source_target_pairs={{0,3},{1,2},{2,1},{3,0},{4,7},{5,6},{6,5},{7,4},{8,11},{9,10},{10,... | collective-permute-start | bytes 196616 | tf_op jit(solution)/shard_map/ppermute | solution.py:232
  48.1 4.3 %collective-permute-start.25 = (bf16[128,256]{1,0:T(8,128)(2,1)S(1)}, bf16[128,256]{1,0:T(8,128)(2,1)S(1)}, u32[]{:S(2)}, u32[]{:S(2)}) collective-permute-start(bf16[128,256]{1,0:T(8,128)(2,1)S(1)} %shard_map.105.refs_0_), channel_id=1, source_target_pairs={{0,1},{1,0},{2,3},{3,2},{4,5},{5,4},{6,7},{7,6},{8,9},{9,8},{10,11... | collective-permute-start | bytes 196616 | tf_op jit(solution)/shard_map/ppermute | solution.py:232
  48.6 4.3 %collective-permute-start.24 = (bf16[128,256]{1,0:T(8,128)(2,1)S(1)}, bf16[128,256]{1,0:T(8,128)(2,1)S(1)}, u32[]{:S(2)}, u32[]{:S(2)}) collective-permute-start(bf16[128,256]{1,0:T(8,128)(2,1)S(1)} %shard_map.105.refs_0_), channel_id=1, source_target_pairs={{0,2},{1,3},{2,0},{3,1},{4,6},{5,7},{6,4},{7,5},{8,10},{9,11},{10,... | collective-permute-start | bytes 196616 | tf_op jit(solution)/shard_map/ppermute | solution.py:232

commit v6 on v5

--- a/solution.py
+++ b/solution.py
@@ -220,10 +220,9 @@
     half = width // 2
     nodes = domains * block
 
-    near = [0, group - 1, *range(1, group - 1)]
-    far = [0, *range(outer // 2, outer), *range(1, outer // 2)]
-
-    near_back, far_back = [0, *near[:0:-1]], [0, *far[:0:-1]]
+    near, near_back = [0, group - 1, *range(1, group - 1)], [0, *range(group - 2, 0, -1), group - 1]
+    blocks_near = [0, 1, *range(group - 1, 1, -1)]
+    far, far_back = [0, *range(outer - 1, 0, -1)], [0, *range(2, 0, -1), *range(3, outer)]
 
     def rep_swap(x):
         return lax.ppermute(x, "rep", [(0, 1), (1, 0)])
@@ -282,13 +281,13 @@
     )
     pieces = [inner_swap(pieces[i], s) if s else pieces[i] for i, s in enumerate(near)]
     back = call(
-        functools.partial(backward_kernel, group, near),
+        functools.partial(backward_kernel, group, blocks_near),
         [((block, half), F32)] + [((block, half), BF16)] * (group - 1),
         scratch=(pltpu.VMEM((tall, half), BF16),),
         args=(adjacency, keep, rep_swap(send)),
     )
     back_own = back[0]
-    back = [inner_swap(back[i], s) if s else back[i] for i, s in enumerate(near)]
+    back = [inner_swap(back[i], s) if s else back[i] for i, s in enumerate(blocks_near)]
     (piece,) = call(
         functools.partial(late_sum_kernel, 1.0 / math.sqrt(nodes)),
         [((width // group, half), BF16)],

time: 54 us -> 53 us (0.981)
  waiting for transfers between devices: 17.6 us -> 16.8 us
    ppermute x8, waiting for transfers between devices: 8.7 us -> 7.73 us  [outer_swap(): return lax.ppermute(x, 'dom', [(i, i ^ t * group) for i in range(domains)])]
    ppermute x10, starting transfers between devices: 2.03 us -> 1.39 us  [rep_swap(): return lax.ppermute(x, 'rep', [(0, 1), (1, 0)])]
  transfers between devices with their start and end apart: 30 -> 30, of which waited for: 15 -> 16; matrix products, arithmetic and copies ran while one was open for 0% -> 0% of each run, Pallas kernels for 4% -> 4%
where the time goes in v6:
time: 53 us; the launch traced here: 52.9 us
  starting transfers between devices  29.4 us (55%)
  waiting for transfers between devices  16.8 us (32%)
  Pallas kernels  5.81 us (11%)
  between operations  0.8 us (2%)
    ppermute x12, starting transfers between devices, inner_swap(): return lax.ppermute(x, 'dom', [(i, i ^ s) for i in range(domains)])  14.8 us
    ppermute x8, starting transfers between devices, outer_swap(): return lax.ppermute(x, 'dom', [(i, i ^ t * group) for i in range(domains)])  13.3 us
    ppermute x8, waiting for transfers between devices, outer_swap(): return lax.ppermute(x, 'dom', [(i, i ^ t * group) for i in range(domains)])  7.73 us
    ppermute x12, waiting for transfers between devices, inner_swap(): return lax.ppermute(x, 'dom', [(i, i ^ s) for i in range(domains)])  6.65 us
    pallas_call x2, Pallas kernels, combine(): pl.pallas_call(functools.partial(combine_kernel, mine), out_shape=jax.Sha...  3.04 us
    pallas_call x11, Pallas kernels, call(): pl.pallas_call(kernel, out_shape=[jax.ShapeDtypeStruct(shape, dtype) for...  2.77 us
    ppermute x10, waiting for transfers between devices, rep_swap(): return lax.ppermute(x, 'rep', [(0, 1), (1, 0)])  2.46 us
    ppermute x10, starting transfers between devices, rep_swap(): return lax.ppermute(x, 'rep', [(0, 1), (1, 0)])  1.39 us
  transfers between devices with their start and end apart: 30, of which 16 were waited for; matrix products, arithmetic and copies ran while one was open for 0% of the time, Pallas kernels for 4%

profile of v6, /device:TPU:0, one launch (start us, length us, event | category | flops | bytes accessed | tf_op | source)
XLA Modules:
  0.0 52.9 jit_solution(13235903584431255518)
XLA Ops:
  0.6 1.5 %shard_map.95 = bf16[16,64,128]{2,1,0:T(8,128)(2,1)S(1)} custom-call(s32[64]{0:T(128)} %bitcast.3, s32[64]{0:T(128)} %count_hbm.3, bf16[64,128,128]{2,1,0:T(8,128)(2,1)} %tiles_hbm.3), custom_call_target="tpu_custom_call" | custom-call | flops 1024 | bytes 1024 | tf_op jit(solution)/shard_map/pallas_call | solution.py:71
  2.2 0.0 copy-start.2
  2.2 0.5 collective-permute-start
  2.7 1.5 %shard_map.94.own_ref = bf16[16,64,128]{2,1,0:T(8,128)(2,1)S(1)} custom-call(s32[64]{0:T(128)} %bitcast.4, s32[64]{0:T(128)} %count_hbm.3, bf16[64,128,128]{2,1,0:T(8,128)(2,1)} %tiles_hbm.3), custom_call_target="tpu_custom_call" | custom-call | flops 1024 | bytes 1024 | tf_op jit(solution)/shard_map/pallas_call | solution.py:71
  4.2 0.0 copy-start.3
  4.3 0.1 shard_map.96
  4.3 3.5 %collective-permute-start.1 = (bf16[512,128]{1,0:T(8,128)(2,1)S(1)}, bf16[512,128]{1,0:T(8,128)(2,1)S(1)}, u32[]{:S(2)}, u32[]{:S(2)}) collective-permute-start(bf16[512,128]{1,0:T(8,128)(2,1)S(1)} %get-tuple-element.27), channel_id=1, source_target_pairs={{0,3},{1,2},{2,1},{3,0},{4,7},{5,6},{6,5},{7,4},{8,11},{9,10},{10,... | collective-permute-start | bytes 393224 | tf_op jit(solution)/shard_map/ppermute | solution.py:231
  7.9 0.5 %collective-permute-start.2 = (bf16[512,128]{1,0:T(8,128)(2,1)S(1)}, bf16[512,128]{1,0:T(8,128)(2,1)S(1)}, u32[]{:S(2)}, u32[]{:S(2)}) collective-permute-start(bf16[512,128]{1,0:T(8,128)(2,1)S(1)} %get-tuple-element.28), channel_id=1, source_target_pairs={{0,1},{1,0},{2,3},{3,2},{4,5},{5,4},{6,7},{7,6},{8,9},{9,8},{10,11... | collective-permute-start | bytes 393224 | tf_op jit(solution)/shard_map/ppermute | solution.py:231
  8.4 0.1 collective-permute-start.3
  8.5 3.1 %collective-permute-start.7 = (bf16[128,256]{1,0:T(8,128)(2,1)S(1)}, bf16[128,256]{1,0:T(8,128)(2,1)S(1)}, u32[]{:S(2)}, u32[]{:S(2)}) collective-permute-start(bf16[128,256]{1,0:T(8,128)(2,1)S(1)} %shard_map.97.refs_0_), channel_id=1, source_target_pairs={{0,8},{1,9},{2,10},{3,11},{4,12},{5,13},{6,14},{7,15},{8,0},{9,1},... | collective-permute-start | bytes 196616 | tf_op jit(solution)/shard_map/ppermute | solution.py:234
  11.6 0.6 %collective-permute-done.1.refs_1_ = bf16[512,128]{1,0:T(8,128)(2,1)S(1)} collective-permute-done((bf16[512,128]{1,0:T(8,128)(2,1)S(1)}, bf16[512,128]{1,0:T(8,128)(2,1)S(1)}, u32[]{:S(2)}, u32[]{:S(2)}) %collective-permute-start.1) | collective-permute-done | bytes 131104 | tf_op jit(solution)/shard_map/ppermute | solution.py:231
  12.2 2.9 %collective-permute-done.2.refs_2_ = bf16[512,128]{1,0:T(8,128)(2,1)S(1)} collective-permute-done((bf16[512,128]{1,0:T(8,128)(2,1)S(1)}, bf16[512,128]{1,0:T(8,128)(2,1)S(1)}, u32[]{:S(2)}, u32[]{:S(2)}) %collective-permute-start.2) | collective-permute-done | bytes 131104 | tf_op jit(solution)/shard_map/ppermute | solution.py:231
  15.1 0.5 collective-permute-start.4
  15.7 0.1 collective-permute-start.8
  15.7 0.8 %collective-permute-done.4.refs_4_ = bf16[256,128]{1,0:T(8,128)(2,1)S(1)} collective-permute-done((bf16[256,128]{1,0:T(8,128)(2,1)S(1)}, bf16[256,128]{1,0:T(8,128)(2,1)S(1)}, u32[]{:S(2)}, u32[]{:S(2)}) %collective-permute-start.4) | collective-permute-done | bytes 65568 | tf_op jit(solution)/shard_map/ppermute | solution.py:228
  16.6 0.4 collective-permute-done.8.refs_7_
  17.0 0.4 shard_map.99
  17.4 3.6 %collective-permute-start.9 = (bf16[128,256]{1,0:T(8,128)(2,1)S(1)}, bf16[128,256]{1,0:T(8,128)(2,1)S(1)}, u32[]{:S(2)}, u32[]{:S(2)}) collective-permute-start(bf16[128,256]{1,0:T(8,128)(2,1)S(1)} %get-tuple-element.32), channel_id=1, source_target_pairs={{0,12},{1,13},{2,14},{3,15},{4,8},{5,9},{6,10},{7,11},{8,4},{9,5},... | collective-permute-start | bytes 196616 | tf_op jit(solution)/shard_map/ppermute | solution.py:234
  21.1 0.8 %collective-permute-start.11 = (bf16[128,256]{1,0:T(8,128)(2,1)S(1)}, bf16[128,256]{1,0:T(8,128)(2,1)S(1)}, u32[]{:S(2)}, u32[]{:S(2)}) collective-permute-start(bf16[128,256]{1,0:T(8,128)(2,1)S(1)} %get-tuple-element.34), channel_id=1, source_target_pairs={{0,4},{1,5},{2,6},{3,7},{4,0},{5,1},{6,2},{7,3},{8,12},{9,13},{10,... | collective-permute-start | bytes 196616 | tf_op jit(solution)/shard_map/ppermute | solution.py:234
  21.9 1.3 %collective-permute-start.19 = (bf16[256,256]{1,0:T(8,128)(2,1)S(1)}, bf16[256,256]{1,0:T(8,128)(2,1)S(1)}, u32[]{:S(2)}, u32[]{:S(2)}) collective-permute-start(bf16[256,256]{1,0:T(8,128)(2,1)S(1)} %shard_map.101.refs_0_), channel_id=1, source_target_pairs={{0,4},{1,5},{2,6},{3,7},{4,0},{5,1},{6,2},{7,3},{8,12},{9,13},{10,... | collective-permute-start | bytes 393224 | tf_op jit(solution)/shard_map/ppermute | solution.py:234
  23.2 0.6 %collective-permute-done.9.refs_1_ = bf16[128,256]{1,0:T(8,128)(2,1)S(1)} collective-permute-done((bf16[128,256]{1,0:T(8,128)(2,1)S(1)}, bf16[128,256]{1,0:T(8,128)(2,1)S(1)}, u32[]{:S(2)}, u32[]{:S(2)}) %collective-permute-start.9) | collective-permute-done | bytes 65568 | tf_op jit(solution)/shard_map/ppermute | solution.py:234
  23.8 3.3 %collective-permute-done.10.refs_2_ = bf16[128,256]{1,0:T(8,128)(2,1)S(1)} collective-permute-done((bf16[128,256]{1,0:T(8,128)(2,1)S(1)}, bf16[128,256]{1,0:T(8,128)(2,1)S(1)}, u32[]{:S(2)}, u32[]{:S(2)}) %collective-permute-start.10) | collective-permute-done | bytes 65568 | tf_op jit(solution)/shard_map/ppermute | solution.py:234
  27.0 0.3 collective-permute-done.11.refs_3_
  27.4 2.4 %collective-permute-start.14 = (bf16[128,256]{1,0:T(8,128)(2,1)S(1)}, bf16[128,256]{1,0:T(8,128)(2,1)S(1)}, u32[]{:S(2)}, u32[]{:S(2)}) collective-permute-start(bf16[128,256]{1,0:T(8,128)(2,1)S(1)} %shard_map.100.refs_0_), channel_id=1, source_target_pairs={{0,12},{1,13},{2,14},{3,15},{4,8},{5,9},{6,10},{7,11},{8,4},{9,5},... | collective-permute-start | bytes 196616 | tf_op jit(solution)/shard_map/ppermute | solution.py:234
  29.8 2.0 %collective-permute-start.12 = (bf16[128,256]{1,0:T(8,128)(2,1)S(1)}, bf16[128,256]{1,0:T(8,128)(2,1)S(1)}, u32[]{:S(2)}, u32[]{:S(2)}) collective-permute-start(bf16[128,256]{1,0:T(8,128)(2,1)S(1)} %shard_map.100.refs_0_), channel_id=1, source_target_pairs={{0,8},{1,9},{2,10},{3,11},{4,12},{5,13},{6,14},{7,15},{8,0},{9,1},... | collective-permute-start | bytes 196616 | tf_op jit(solution)/shard_map/ppermute | solution.py:234
  31.9 2.2 %collective-permute-done.14.refs_3_ = bf16[128,256]{1,0:T(8,128)(2,1)S(1)} collective-permute-done((bf16[128,256]{1,0:T(8,128)(2,1)S(1)}, bf16[128,256]{1,0:T(8,128)(2,1)S(1)}, u32[]{:S(2)}, u32[]{:S(2)}) %collective-permute-start.14) | collective-permute-done | bytes 65568 | tf_op jit(solution)/shard_map/ppermute | solution.py:234
  34.1 0.4 collective-permute-done.13.refs_2_
  34.5 0.1 collective-permute-start.17
  34.6 0.8 %collective-permute-done.12.refs_1_ = bf16[128,256]{1,0:T(8,128)(2,1)S(1)} collective-permute-done((bf16[128,256]{1,0:T(8,128)(2,1)S(1)}, bf16[128,256]{1,0:T(8,128)(2,1)S(1)}, u32[]{:S(2)}, u32[]{:S(2)}) %collective-permute-start.12) | collective-permute-done | bytes 65568 | tf_op jit(solution)/shard_map/ppermute | solution.py:234
  35.5 0.3 collective-permute-done.17.refs_6_
  35.8 0.9 %collective-permute-done.16.refs_5_ = bf16[128,256]{1,0:T(8,128)(2,1)S(1)} collective-permute-done((bf16[128,256]{1,0:T(8,128)(2,1)S(1)}, bf16[128,256]{1,0:T(8,128)(2,1)S(1)}, u32[]{:S(2)}, u32[]{:S(2)}) %collective-permute-start.16) | collective-permute-done | bytes 65568 | tf_op jit(solution)/shard_map/ppermute | solution.py:228
  36.7 0.9 %shard_map.103 = (bf16[128,256]{1,0:T(8,128)(2,1)S(1)}, f32[512,256]{1,0:T(8,128)S(1)}, bf16[512,256]{1,0:T(8,128)(2,1)S(1)}, f32[128,256]{1,0:T(8,128)S(1)}, bf...) custom-call(bf16[128,256]{1,0:T(8,128)(2,1)S(1)} %shard_map.100.refs_0_, ...), custom_call_target="tpu_custom_call" | custom-call | flops 1024 | bytes 1024 | tf_op jit(solution)/shard_map/pallas_call | solution.py:28
  37.6 0.2 collective-permute-start.20
  37.8 1.8 %collective-permute-start.21 = (bf16[128,256]{1,0:T(8,128)(2,1)S(1)}, bf16[128,256]{1,0:T(8,128)(2,1)S(1)}, u32[]{:S(2)}, u32[]{:S(2)}) collective-permute-start(bf16[128,256]{1,0:T(8,128)(2,1)S(1)} %get-tuple-element.39), channel_id=1, source_target_pairs={{0,3},{1,2},{2,1},{3,0},{4,7},{5,6},{6,5},{7,4},{8,11},{9,10},{10,... | collective-permute-start | bytes 196616 | tf_op jit(solution)/shard_map/ppermute | solution.py:231
  39.6 0.5 %collective-permute-start.22 = (bf16[128,256]{1,0:T(8,128)(2,1)S(1)}, bf16[128,256]{1,0:T(8,128)(2,1)S(1)}, u32[]{:S(2)}, u32[]{:S(2)}) collective-permute-start(bf16[128,256]{1,0:T(8,128)(2,1)S(1)} %get-tuple-element.40), channel_id=1, source_target_pairs={{0,1},{1,0},{2,3},{3,2},{4,5},{5,4},{6,7},{7,6},{8,9},{9,8},{10,11... | collective-permute-start | bytes 196616 | tf_op jit(solution)/shard_map/ppermute | solution.py:231
  40.2 1.2 %collective-permute-start.23 = (bf16[128,256]{1,0:T(8,128)(2,1)S(1)}, bf16[128,256]{1,0:T(8,128)(2,1)S(1)}, u32[]{:S(2)}, u32[]{:S(2)}) collective-permute-start(bf16[128,256]{1,0:T(8,128)(2,1)S(1)} %get-tuple-element.41), channel_id=1, source_target_pairs={{0,2},{1,3},{2,0},{3,1},{4,6},{5,7},{6,4},{7,5},{8,10},{9,11},{10,... | collective-permute-start | bytes 196616 | tf_op jit(solution)/shard_map/ppermute | solution.py:231
  41.3 0.4 shard_map.104
  41.7 1.6 %collective-permute-start.27 = (bf16[128,256]{1,0:T(8,128)(2,1)S(1)}, bf16[128,256]{1,0:T(8,128)(2,1)S(1)}, u32[]{:S(2)}, u32[]{:S(2)}) collective-permute-start(bf16[128,256]{1,0:T(8,128)(2,1)S(1)} %get-tuple-element.42), channel_id=1, source_target_pairs={{0,1},{1,0},{2,3},{3,2},{4,5},{5,4},{6,7},{7,6},{8,9},{9,8},{10,11... | collective-permute-start | bytes 196616 | tf_op jit(solution)/shard_map/ppermute | solution.py:231
  43.3 0.8 %collective-permute-start.28 = (bf16[128,256]{1,0:T(8,128)(2,1)S(1)}, bf16[128,256]{1,0:T(8,128)(2,1)S(1)}, u32[]{:S(2)}, u32[]{:S(2)}) collective-permute-start(bf16[128,256]{1,0:T(8,128)(2,1)S(1)} %get-tuple-element.43), channel_id=1, source_target_pairs={{0,3},{1,2},{2,1},{3,0},{4,7},{5,6},{6,5},{7,4},{8,11},{9,10},{10,... | collective-permute-start | bytes 196616 | tf_op jit(solution)/shard_map/ppermute | solution.py:231
  44.1 1.2 %collective-permute-start.29 = (bf16[128,256]{1,0:T(8,128)(2,1)S(1)}, bf16[128,256]{1,0:T(8,128)(2,1)S(1)}, u32[]{:S(2)}, u32[]{:S(2)}) collective-permute-start(bf16[128,256]{1,0:T(8,128)(2,1)S(1)} %get-tuple-element.44), channel_id=1, source_target_pairs={{0,2},{1,3},{2,0},{3,1},{4,6},{5,7},{6,4},{7,5},{8,10},{9,11},{10,... | collective-permute-start | bytes 196616 | tf_op jit(solution)/shard_map/ppermute | solution.py:231
  45.3 1.8 %collective-permute-start.26 = (bf16[128,256]{1,0:T(8,128)(2,1)S(1)}, bf16[128,256]{1,0:T(8,128)(2,1)S(1)}, u32[]{:S(2)}, u32[]{:S(2)}) collective-permute-start(bf16[128,256]{1,0:T(8,128)(2,1)S(1)} %shard_map.105.refs_0_), channel_id=1, source_target_pairs={{0,3},{1,2},{2,1},{3,0},{4,7},{5,6},{6,5},{7,4},{8,11},{9,10},{10,... | collective-permute-start | bytes 196616 | tf_op jit(solution)/shard_map/ppermute | solution.py:231
  47.2 0.5 %collective-permute-start.25 = (bf16[128,256]{1,0:T(8,128)(2,1)S(1)}, bf16[128,256]{1,0:T(8,128)(2,1)S(1)}, u32[]{:S(2)}, u32[]{:S(2)}) collective-permute-start(bf16[128,256]{1,0:T(8,128)(2,1)S(1)} %shard_map.105.refs_0_), channel_id=1, source_target_pairs={{0,1},{1,0},{2,3},{3,2},{4,5},{5,4},{6,7},{7,6},{8,9},{9,8},{10,11... | collective-permute-start | bytes 196616 | tf_op jit(solution)/shard_map/ppermute | solution.py:231
  47.7 1.2 %collective-permute-start.24 = (bf16[128,256]{1,0:T(8,128)(2,1)S(1)}, bf16[128,256]{1,0:T(8,128)(2,1)S(1)}, u32[]{:S(2)}, u32[]{:S(2)}) collective-permute-start(bf16[128,256]{1,0:T(8,128)(2,1)S(1)} %shard_map.105.refs_0_), channel_id=1, source_target_pairs={{0,2},{1,3},{2,0},{3,1},{4,6},{5,7},{6,4},{7,5},{8,10},{9,11},{10,... | collective-permute-start | bytes 196616 | tf_op jit(solution)/shard_map/ppermute | solution.py:231
  48.9 0.3 collective-permute-done.28.refs_6_
  49.1 1.9 %collective-permute-done.29.refs_7_ = bf16[128,256]{1,0:T(8,128)(2,1)S(1)} collective-permute-done((bf16[128,256]{1,0:T(8,128)(2,1)S(1)}, bf16[128,256]{1,0:T(8,128)(2,1)S(1)}, u32[]{:S(2)}, u32[]{:S(2)}) %collective-permute-start.29) | collective-permute-done | bytes 65568 | tf_op jit(solution)/shard_map/ppermute | solution.py:231
  51.0 0.4 collective-permute-done.25.refs_2_
  51.4 0.5 %collective-permute-done.24.refs_1_ = bf16[128,256]{1,0:T(8,128)(2,1)S(1)} collective-permute-done((bf16[128,256]{1,0:T(8,128)(2,1)S(1)}, bf16[128,256]{1,0:T(8,128)(2,1)S(1)}, u32[]{:S(2)}, u32[]{:S(2)}) %collective-permute-start.24) | collective-permute-done | bytes 65568 | tf_op jit(solution)/shard_map/ppermute | solution.py:231
  52.0 0.9 %shard_map.106 = (f32[512,256]{1,0:T(8,128)}, bf16[128,256]{1,0:T(8,128)(2,1)}, bf16[128,256]{1,0:T(8,128)(2,1)}) custom-call(bf16[128,256]{1,0:T(8,128)(2,1)S(1)} %shard_map.105.refs_0_, bf16[128,256]{1,0:T(8,128)(2,1)S(1)} %collective-permute-done.24.refs_1_, bf16[128,256]{1,0:T(8,128)(2,1)S(1)} %collective-permute-done.25.refs_2_, ...), custom_call_target="tpu_custom_call" | custom-call | flops 1024 | bytes 1024 | tf_op jit(solution)/shard_map/pallas_call | solution.py:28
  (33 shorter events, 0.2 us)
Async XLA Ops:
  0.6 3.6 %copy-start.1 = (bf16[128,512]{1,0:T(8,128)(2,1)S(1)}, bf16[128,512]{1,0:T(8,128)(2,1)}, u32[]{:S(2)}) copy-start(bf16[128,512]{1,0:T(8,128)(2,1)} %refs_8_.1) | copy-start | bytes 393220
  2.2 6.3 %copy-start.2 = (bf16[128,512]{1,0:T(8,128)(2,1)S(1)}, bf16[128,512]{1,0:T(8,128)(2,1)}, u32[]{:S(2)}) copy-start(bf16[128,512]{1,0:T(8,128)(2,1)} %whole_ref.1) | copy-start | bytes 393220
  2.2 2.0 %collective-permute-start = (bf16[16,64,128]{2,1,0:T(8,128)(2,1)S(1)}, bf16[16,64,128]{2,1,0:T(8,128)(2,1)S(1)}, u32[]{:S(2)}, u32[]{:S(2)}) collective-permute-start(bf16[16,64,128]{2,1,0:T(8,128)(2,1)S(1)} %shard_map.95), channel_id=1, source_target_pairs={{0,16},{16,0},{1,17},{17,1},{2,18},{18,2},{3,19},{19,3},{4,20},{20... | collective-permute-start | bytes 786440 | tf_op jit(solution)/shard_map/ppermute | solution.py:228
  4.2 32.5 %copy-start = (bf16[512,512]{1,0:T(8,128)(2,1)S(1)}, bf16[512,512]{1,0:T(8,128)(2,1)}, u32[]{:S(2)}) copy-start(bf16[512,512]{1,0:T(8,128)(2,1)} %refs_9_.1) | copy-start | bytes 1572868
  4.2 32.5 %copy-start.3 = (f32[512]{0:T(512)S(1)}, f32[512]{0:T(512)}, u32[]{:S(2)}) copy-start(f32[512]{0:T(512)} %param.12) | copy-start | bytes 6148
  4.3 7.9 %collective-permute-start.1 = (bf16[512,128]{1,0:T(8,128)(2,1)S(1)}, bf16[512,128]{1,0:T(8,128)(2,1)S(1)}, u32[]{:S(2)}, u32[]{:S(2)}) collective-permute-start(bf16[512,128]{1,0:T(8,128)(2,1)S(1)} %get-tuple-element.27), channel_id=1, source_target_pairs={{0,3},{1,2},{2,1},{3,0},{4,7},{5,6},{6,5},{7,4},{8,11},{9,10},{10,... | collective-permute-start | bytes 393224 | tf_op jit(solution)/shard_map/ppermute | solution.py:231
  7.9 7.3 %collective-permute-start.2 = (bf16[512,128]{1,0:T(8,128)(2,1)S(1)}, bf16[512,128]{1,0:T(8,128)(2,1)S(1)}, u32[]{:S(2)}, u32[]{:S(2)}) collective-permute-start(bf16[512,128]{1,0:T(8,128)(2,1)S(1)} %get-tuple-element.28), channel_id=1, source_target_pairs={{0,1},{1,0},{2,3},{3,2},{4,5},{5,4},{6,7},{7,6},{8,9},{9,8},{10,11... | collective-permute-start | bytes 393224 | tf_op jit(solution)/shard_map/ppermute | solution.py:231
  8.4 7.2 %collective-permute-start.3 = (bf16[512,128]{1,0:T(8,128)(2,1)S(1)}, bf16[512,128]{1,0:T(8,128)(2,1)S(1)}, u32[]{:S(2)}, u32[]{:S(2)}) collective-permute-start(bf16[512,128]{1,0:T(8,128)(2,1)S(1)} %get-tuple-element.29), channel_id=1, source_target_pairs={{0,2},{1,3},{2,0},{3,1},{4,6},{5,7},{6,4},{7,5},{8,10},{9,11},{10,... | collective-permute-start | bytes 393224 | tf_op jit(solution)/shard_map/ppermute | solution.py:231
  8.5 7.1 %collective-permute-start.7 = (bf16[128,256]{1,0:T(8,128)(2,1)S(1)}, bf16[128,256]{1,0:T(8,128)(2,1)S(1)}, u32[]{:S(2)}, u32[]{:S(2)}) collective-permute-start(bf16[128,256]{1,0:T(8,128)(2,1)S(1)} %shard_map.97.refs_0_), channel_id=1, source_target_pairs={{0,8},{1,9},{2,10},{3,11},{4,12},{5,13},{6,14},{7,15},{8,0},{9,1},... | collective-permute-start | bytes 196616 | tf_op jit(solution)/shard_map/ppermute | solution.py:234
  12.2 4.8 %collective-permute-start.5 = (bf16[512,128]{1,0:T(8,128)(2,1)S(1)}, bf16[512,128]{1,0:T(8,128)(2,1)S(1)}, u32[]{:S(2)}, u32[]{:S(2)}) collective-permute-start(bf16[512,128]{1,0:T(8,128)(2,1)S(1)} %collective-permute-done.1.refs_1_), channel_id=1, source_target_pairs={{0,16},{16,0},{1,17},{17,1},{2,18},{18,2},{3,19},{19,3},{4,20},{20... | collective-permute-start | bytes 393224 | tf_op jit(solution)/shard_map/ppermute | solution.py:228
  15.1 1.9 %collective-permute-start.6 = (bf16[512,128]{1,0:T(8,128)(2,1)S(1)}, bf16[512,128]{1,0:T(8,128)(2,1)S(1)}, u32[]{:S(2)}, u32[]{:S(2)}) collective-permute-start(bf16[512,128]{1,0:T(8,128)(2,1)S(1)} %collective-permute-done.2.refs_2_), channel_id=1, source_target_pairs={{0,16},{16,0},{1,17},{17,1},{2,18},{18,2},{3,19},{19,3},{4,20},{20... | collective-permute-start | bytes 393224 | tf_op jit(solution)/shard_map/ppermute | solution.py:228
  15.1 1.4 %collective-permute-start.4 = (bf16[256,128]{1,0:T(8,128)(2,1)S(1)}, bf16[256,128]{1,0:T(8,128)(2,1)S(1)}, u32[]{:S(2)}, u32[]{:S(2)}) collective-permute-start(bf16[256,128]{1,0:T(8,128)(2,1)S(1)} %get-tuple-element.26.refs_0_), channel_id=1, source_target_pairs={{0,16},{16,0},{1,17},{17,1},{2,18},{18,2},{3,19},{19,3},{4,20},{20... | collective-permute-start | bytes 196616 | tf_op jit(solution)/shard_map/ppermute | solution.py:228
  15.7 1.3 %collective-permute-start.8 = (bf16[256,128]{1,0:T(8,128)(2,1)S(1)}, bf16[256,128]{1,0:T(8,128)(2,1)S(1)}, u32[]{:S(2)}, u32[]{:S(2)}) collective-permute-start(bf16[256,128]{1,0:T(8,128)(2,1)S(1)} %shard_map.98), channel_id=1, source_target_pairs={{0,16},{16,0},{1,17},{17,1},{2,18},{18,2},{3,19},{19,3},{4,20},{20... | collective-permute-start | bytes 196616 | tf_op jit(solution)/shard_map/ppermute | solution.py:228
  17.4 6.4 %collective-permute-start.9 = (bf16[128,256]{1,0:T(8,128)(2,1)S(1)}, bf16[128,256]{1,0:T(8,128)(2,1)S(1)}, u32[]{:S(2)}, u32[]{:S(2)}) collective-permute-start(bf16[128,256]{1,0:T(8,128)(2,1)S(1)} %get-tuple-element.32), channel_id=1, source_target_pairs={{0,12},{1,13},{2,14},{3,15},{4,8},{5,9},{6,10},{7,11},{8,4},{9,5},... | collective-permute-start | bytes 196616 | tf_op jit(solution)/shard_map/ppermute | solution.py:234
  21.1 6.0 %collective-permute-start.10 = (bf16[128,256]{1,0:T(8,128)(2,1)S(1)}, bf16[128,256]{1,0:T(8,128)(2,1)S(1)}, u32[]{:S(2)}, u32[]{:S(2)}) collective-permute-start(bf16[128,256]{1,0:T(8,128)(2,1)S(1)} %get-tuple-element.33), channel_id=1, source_target_pairs={{0,8},{1,9},{2,10},{3,11},{4,12},{5,13},{6,14},{7,15},{8,0},{9,1},... | collective-permute-start | bytes 196616 | tf_op jit(solution)/shard_map/ppermute | solution.py:234
  21.1 6.3 %collective-permute-start.11 = (bf16[128,256]{1,0:T(8,128)(2,1)S(1)}, bf16[128,256]{1,0:T(8,128)(2,1)S(1)}, u32[]{:S(2)}, u32[]{:S(2)}) collective-permute-start(bf16[128,256]{1,0:T(8,128)(2,1)S(1)} %get-tuple-element.34), channel_id=1, source_target_pairs={{0,4},{1,5},{2,6},{3,7},{4,0},{5,1},{6,2},{7,3},{8,12},{9,13},{10,... | collective-permute-start | bytes 196616 | tf_op jit(solution)/shard_map/ppermute | solution.py:234
  21.9 13.6 %collective-permute-start.19 = (bf16[256,256]{1,0:T(8,128)(2,1)S(1)}, bf16[256,256]{1,0:T(8,128)(2,1)S(1)}, u32[]{:S(2)}, u32[]{:S(2)}) collective-permute-start(bf16[256,256]{1,0:T(8,128)(2,1)S(1)} %shard_map.101.refs_0_), channel_id=1, source_target_pairs={{0,4},{1,5},{2,6},{3,7},{4,0},{5,1},{6,2},{7,3},{8,12},{9,13},{10,... | collective-permute-start | bytes 393224 | tf_op jit(solution)/shard_map/ppermute | solution.py:234
  27.4 6.7 %collective-permute-start.14 = (bf16[128,256]{1,0:T(8,128)(2,1)S(1)}, bf16[128,256]{1,0:T(8,128)(2,1)S(1)}, u32[]{:S(2)}, u32[]{:S(2)}) collective-permute-start(bf16[128,256]{1,0:T(8,128)(2,1)S(1)} %shard_map.100.refs_0_), channel_id=1, source_target_pairs={{0,12},{1,13},{2,14},{3,15},{4,8},{5,9},{6,10},{7,11},{8,4},{9,5},... | collective-permute-start | bytes 196616 | tf_op jit(solution)/shard_map/ppermute | solution.py:234
  29.8 4.7 %collective-permute-start.13 = (bf16[128,256]{1,0:T(8,128)(2,1)S(1)}, bf16[128,256]{1,0:T(8,128)(2,1)S(1)}, u32[]{:S(2)}, u32[]{:S(2)}) collective-permute-start(bf16[128,256]{1,0:T(8,128)(2,1)S(1)} %shard_map.100.refs_0_), channel_id=1, source_target_pairs={{0,4},{1,5},{2,6},{3,7},{4,0},{5,1},{6,2},{7,3},{8,12},{9,13},{10,... | collective-permute-start | bytes 196616 | tf_op jit(solution)/shard_map/ppermute | solution.py:234
  29.8 5.6 %collective-permute-start.12 = (bf16[128,256]{1,0:T(8,128)(2,1)S(1)}, bf16[128,256]{1,0:T(8,128)(2,1)S(1)}, u32[]{:S(2)}, u32[]{:S(2)}) collective-permute-start(bf16[128,256]{1,0:T(8,128)(2,1)S(1)} %shard_map.100.refs_0_), channel_id=1, source_target_pairs={{0,8},{1,9},{2,10},{3,11},{4,12},{5,13},{6,14},{7,15},{8,0},{9,1},... | collective-permute-start | bytes 196616 | tf_op jit(solution)/shard_map/ppermute | solution.py:234
  31.9 3.6 %collective-permute-start.15 = (bf16[128,256]{1,0:T(8,128)(2,1)S(1)}, bf16[128,256]{1,0:T(8,128)(2,1)S(1)}, u32[]{:S(2)}, u32[]{:S(2)}) collective-permute-start(bf16[128,256]{1,0:T(8,128)(2,1)S(1)} %shard_map.100.refs_0_), channel_id=1, source_target_pairs={{0,16},{16,0},{1,17},{17,1},{2,18},{18,2},{3,19},{19,3},{4,20},{20... | collective-permute-start | bytes 196616 | tf_op jit(solution)/shard_map/ppermute | solution.py:228
  34.1 1.4 %collective-permute-start.18 = (bf16[128,256]{1,0:T(8,128)(2,1)S(1)}, bf16[128,256]{1,0:T(8,128)(2,1)S(1)}, u32[]{:S(2)}, u32[]{:S(2)}) collective-permute-start(bf16[128,256]{1,0:T(8,128)(2,1)S(1)} %collective-permute-done.14.refs_3_), channel_id=1, source_target_pairs={{0,16},{16,0},{1,17},{17,1},{2,18},{18,2},{3,19},{19,3},{4,20},{20... | collective-permute-start | bytes 196616 | tf_op jit(solution)/shard_map/ppermute | solution.py:228
  34.5 1.3 %collective-permute-start.17 = (bf16[128,256]{1,0:T(8,128)(2,1)S(1)}, bf16[128,256]{1,0:T(8,128)(2,1)S(1)}, u32[]{:S(2)}, u32[]{:S(2)}) collective-permute-start(bf16[128,256]{1,0:T(8,128)(2,1)S(1)} %collective-permute-done.13.refs_2_), channel_id=1, source_target_pairs={{0,16},{16,0},{1,17},{17,1},{2,18},{18,2},{3,19},{19,3},{4,20},{20... | collective-permute-start | bytes 196616 | tf_op jit(solution)/shard_map/ppermute | solution.py:228
  35.5 1.3 %collective-permute-start.16 = (bf16[128,256]{1,0:T(8,128)(2,1)S(1)}, bf16[128,256]{1,0:T(8,128)(2,1)S(1)}, u32[]{:S(2)}, u32[]{:S(2)}) collective-permute-start(bf16[128,256]{1,0:T(8,128)(2,1)S(1)} %collective-permute-done.12.refs_1_), channel_id=1, source_target_pairs={{0,16},{16,0},{1,17},{17,1},{2,18},{18,2},{3,19},{19,3},{4,20},{20... | collective-permute-start | bytes 196616 | tf_op jit(solution)/shard_map/ppermute | solution.py:228
  37.6 3.7 %collective-permute-start.20 = (bf16[512,256]{1,0:T(8,128)(2,1)S(1)}, bf16[512,256]{1,0:T(8,128)(2,1)S(1)}, u32[]{:S(2)}, u32[]{:S(2)}) collective-permute-start(bf16[512,256]{1,0:T(8,128)(2,1)S(1)} %get-tuple-element.36), channel_id=1, source_target_pairs={{0,16},{16,0},{1,17},{17,1},{2,18},{18,2},{3,19},{19,3},{4,20},{20... | collective-permute-start | bytes 786440 | tf_op jit(solution)/shard_map/ppermute | solution.py:228
  37.8 6.2 %collective-permute-start.21 = (bf16[128,256]{1,0:T(8,128)(2,1)S(1)}, bf16[128,256]{1,0:T(8,128)(2,1)S(1)}, u32[]{:S(2)}, u32[]{:S(2)}) collective-permute-start(bf16[128,256]{1,0:T(8,128)(2,1)S(1)} %get-tuple-element.39), channel_id=1, source_target_pairs={{0,3},{1,2},{2,1},{3,0},{4,7},{5,6},{6,5},{7,4},{8,11},{9,10},{10,... | collective-permute-start | bytes 196616 | tf_op jit(solution)/shard_map/ppermute | solution.py:231
  39.6 5.6 %collective-permute-start.22 = (bf16[128,256]{1,0:T(8,128)(2,1)S(1)}, bf16[128,256]{1,0:T(8,128)(2,1)S(1)}, u32[]{:S(2)}, u32[]{:S(2)}) collective-permute-start(bf16[128,256]{1,0:T(8,128)(2,1)S(1)} %get-tuple-element.40), channel_id=1, source_target_pairs={{0,1},{1,0},{2,3},{3,2},{4,5},{5,4},{6,7},{7,6},{8,9},{9,8},{10,11... | collective-permute-start | bytes 196616 | tf_op jit(solution)/shard_map/ppermute | solution.py:231
  40.2 5.1 %collective-permute-start.23 = (bf16[128,256]{1,0:T(8,128)(2,1)S(1)}, bf16[128,256]{1,0:T(8,128)(2,1)S(1)}, u32[]{:S(2)}, u32[]{:S(2)}) collective-permute-start(bf16[128,256]{1,0:T(8,128)(2,1)S(1)} %get-tuple-element.41), channel_id=1, source_target_pairs={{0,2},{1,3},{2,0},{3,1},{4,6},{5,7},{6,4},{7,5},{8,10},{9,11},{10,... | collective-permute-start | bytes 196616 | tf_op jit(solution)/shard_map/ppermute | solution.py:231
  41.7 6.0 %collective-permute-start.27 = (bf16[128,256]{1,0:T(8,128)(2,1)S(1)}, bf16[128,256]{1,0:T(8,128)(2,1)S(1)}, u32[]{:S(2)}, u32[]{:S(2)}) collective-permute-start(bf16[128,256]{1,0:T(8,128)(2,1)S(1)} %get-tuple-element.42), channel_id=1, source_target_pairs={{0,1},{1,0},{2,3},{3,2},{4,5},{5,4},{6,7},{7,6},{8,9},{9,8},{10,11... | collective-permute-start | bytes 196616 | tf_op jit(solution)/shard_map/ppermute | solution.py:231
  43.3 5.9 %collective-permute-start.28 = (bf16[128,256]{1,0:T(8,128)(2,1)S(1)}, bf16[128,256]{1,0:T(8,128)(2,1)S(1)}, u32[]{:S(2)}, u32[]{:S(2)}) collective-permute-start(bf16[128,256]{1,0:T(8,128)(2,1)S(1)} %get-tuple-element.43), channel_id=1, source_target_pairs={{0,3},{1,2},{2,1},{3,0},{4,7},{5,6},{6,5},{7,4},{8,11},{9,10},{10,... | collective-permute-start | bytes 196616 | tf_op jit(solution)/shard_map/ppermute | solution.py:231
  44.1 6.9 %collective-permute-start.29 = (bf16[128,256]{1,0:T(8,128)(2,1)S(1)}, bf16[128,256]{1,0:T(8,128)(2,1)S(1)}, u32[]{:S(2)}, u32[]{:S(2)}) collective-permute-start(bf16[128,256]{1,0:T(8,128)(2,1)S(1)} %get-tuple-element.44), channel_id=1, source_target_pairs={{0,2},{1,3},{2,0},{3,1},{4,6},{5,7},{6,4},{7,5},{8,10},{9,11},{10,... | collective-permute-start | bytes 196616 | tf_op jit(solution)/shard_map/ppermute | solution.py:231
  45.3 5.7 %collective-permute-start.26 = (bf16[128,256]{1,0:T(8,128)(2,1)S(1)}, bf16[128,256]{1,0:T(8,128)(2,1)S(1)}, u32[]{:S(2)}, u32[]{:S(2)}) collective-permute-start(bf16[128,256]{1,0:T(8,128)(2,1)S(1)} %shard_map.105.refs_0_), channel_id=1, source_target_pairs={{0,3},{1,2},{2,1},{3,0},{4,7},{5,6},{6,5},{7,4},{8,11},{9,10},{10,... | collective-permute-start | bytes 196616 | tf_op jit(solution)/shard_map/ppermute | solution.py:231
  47.2 4.3 %collective-permute-start.25 = (bf16[128,256]{1,0:T(8,128)(2,1)S(1)}, bf16[128,256]{1,0:T(8,128)(2,1)S(1)}, u32[]{:S(2)}, u32[]{:S(2)}) collective-permute-start(bf16[128,256]{1,0:T(8,128)(2,1)S(1)} %shard_map.105.refs_0_), channel_id=1, source_target_pairs={{0,1},{1,0},{2,3},{3,2},{4,5},{5,4},{6,7},{7,6},{8,9},{9,8},{10,11... | collective-permute-start | bytes 196616 | tf_op jit(solution)/shard_map/ppermute | solution.py:231
  47.7 4.3 %collective-permute-start.24 = (bf16[128,256]{1,0:T(8,128)(2,1)S(1)}, bf16[128,256]{1,0:T(8,128)(2,1)S(1)}, u32[]{:S(2)}, u32[]{:S(2)}) collective-permute-start(bf16[128,256]{1,0:T(8,128)(2,1)S(1)} %shard_map.105.refs_0_), channel_id=1, source_target_pairs={{0,2},{1,3},{2,0},{3,1},{4,6},{5,7},{6,4},{7,5},{8,10},{9,11},{10,... | collective-permute-start | bytes 196616 | tf_op jit(solution)/shard_map/ppermute | solution.py:231

commit v7 on v6

--- a/solution.py
+++ b/solution.py
@@ -105,27 +105,42 @@
             outs[s][at : at + block] = piece
 
 
-def forward_kernel(group, outer, near, far, *refs):
-    own = [refs[near.index(s)] for s in range(group)]
-    got = [refs[group + near.index(s)] for s in range(group)]
-    features_ref, adjacency = refs[2 * group], refs[-outer - 2]
-    outs, panel = refs[-outer - 1 : -1], refs[-1]
-    rep, z, _ = place(group)
+def begin_kernel(outer, *refs):
+    number = (len(refs) - 4) // 2
+    own, got, features_ref = refs[:number], refs[number : 2 * number], refs[2 * number]
+    adjacency, partial, panel = refs[2 * number + 1 :]
+    rep, _, _ = place(number + 1)
     block, width = features_ref.shape
     half, side = block // 2, width // 2
+    panel[:block, :] = features_ref[:, rows(rep, side)]
+    for k in range(number):
+        columns = slice(k * block, (k + 1) * block)
+        for t in range(outer):
+            at = slice(t * half, (t + 1) * half)
+            adjacency[t, rows(rep, half), columns] = own[k][at, :]
+            adjacency[t, rows(1 - rep, half), columns] = got[k][at, :]
+        for i in range(side // block if k else 0):
+            start = outer * half + i * block
+            panel[columns, i * block : (i + 1) * block] = own[k][start : start + block, :]
+    for t in range(outer):
+        partial[t] = jnp.dot(adjacency[t], panel[...], preferred_element_type=F32)
+
+
+def forward_kernel(group, far, own_ref, got_ref, partial, adjacency, *refs):
+    outs, panel = refs[:-1], refs[-1]
+    rep, z, _ = place(group)
+    outer, block, side = partial.shape
+    half = block // 2
     for t in range(outer):
         at = slice(t * half, (t + 1) * half)
-        for s in range(group):
-            columns = slice(s * block, (s + 1) * block)
-            adjacency[t, rows(rep, half), columns] = own[s][at, :]
-            adjacency[t, rows(1 - rep, half), columns] = got[s][at, :]
-    panel[:block, :] = features_ref[:, rows(rep, side)]
-    for s in range(1, group):
-        for i in range(side // block):
-            start = outer * half + i * block
-            panel[s * block : (s + 1) * block, i * block : (i + 1) * block] = own[s][start : start + block, :]
+        adjacency[t, rows(rep, half), :] = own_ref[at, :]
+        adjacency[t, rows(1 - rep, half), :] = got_ref[at, :]
+    for i in range(side // block):
+        start = outer * half + i * block
+        panel[:, i * block : (i + 1) * block] = own_ref[start : start + block, :]
     for i, t in enumerate(far):
-        part = jnp.dot(adjacency[lax.bitwise_xor(z, t)], panel[...], preferred_element_type=F32)
+        b = lax.bitwise_xor(z, t)
+        part = partial[b] + jnp.dot(adjacency[b], panel[...], preferred_element_type=F32)
         outs[i][...] = part.astype(outs[i].dtype)
 
 
@@ -179,13 +194,15 @@
         ref[...] = row_grad.astype(ref.dtype)
 
 
-def backward_kernel(group, near, adjacency, keep_ref, got_ref, *refs):
+def backward_kernel(near, held, first, final, keep_ref, got_ref, *refs):
     outs, grad = refs[:-1], refs[-1]
-    outer, block, columns = adjacency.shape
+    outer, block, _ = final.shape
     grad[...] = (keep_ref[...] + got_ref[...].astype(F32)).astype(BF16)
     for i, s in enumerate(near):
+        k = held.index(s)
+        strip = final[...] if s == held[-1] else first[:, :, k * block : (k + 1) * block]
         total = lax.dot_general(
-            adjacency[...].reshape(outer * block, columns)[:, s * block : (s + 1) * block],
+            strip.reshape(outer * block, block),
             grad[...],
             (((0,), (0,)), ((), ())),
             preferred_element_type=F32,
@@ -248,11 +265,17 @@
     mine = [inner_swap(cut[i], s) if s else cut[i] for i, s in enumerate(near)]
     (last,) = call(top_kernel, [((cut_rows, block), BF16)], args=(mine[-1], got_slopes))
     others = [rep_swap(x) for x in (*mine[:-1], last)]
-    adjacency, *parts = call(
-        functools.partial(forward_kernel, group, outer, near, far),
-        [((outer, block, group * block), BF16), ((block, half), F32)] + [((block, half), BF16)] * (outer - 1),
-        scratch=(pltpu.VMEM((group * block, half), BF16),),
-        args=(*mine, *others, features),
+    first, partial = call(
+        functools.partial(begin_kernel, outer),
+        [((outer, block, (group - 1) * block), BF16), ((outer, block, half), F32)],
+        scratch=(pltpu.VMEM(((group - 1) * block, half), BF16),),
+        args=(*mine[:-1], *others[:-1], features),
+    )
+    final, *parts = call(
+        functools.partial(forward_kernel, group, far),
+        [((outer, block, block), BF16), ((block, half), F32)] + [((block, half), BF16)] * (outer - 1),
+        scratch=(pltpu.VMEM((block, half), BF16),),
+        args=(mine[-1], others[-1], partial),
     )
     own_part = parts[0]
     parts = [outer_swap(parts[i], t) if t else parts[i] for i, t in enumerate(far)]
@@ -281,10 +304,10 @@
     )
     pieces = [inner_swap(pieces[i], s) if s else pieces[i] for i, s in enumerate(near)]
     back = call(
-        functools.partial(backward_kernel, group, blocks_near),
+        functools.partial(backward_kernel, blocks_near, near),
         [((block, half), F32)] + [((block, half), BF16)] * (group - 1),
         scratch=(pltpu.VMEM((tall, half), BF16),),
-        args=(adjacency, keep, rep_swap(send)),
+        args=(first, final, keep, rep_swap(send)),
     )
     back_own = back[0]
     back = [inner_swap(back[i], s) if s else back[i] for i, s in enumerate(blocks_near)]

time: 53 us -> 52.9 us (level)
    pallas_call x11 -> x12, Pallas kernels: 2.77 us -> 2.93 us  [call(): pl.pallas_call(kernel, out_shape=[jax.ShapeDtypeStruct(shape, dtype) for...]
  transfers between devices with their start and end apart: 30 -> 30, of which waited for: 16 -> 15; matrix products, arithmetic and copies ran while one was open for 0% -> 0% of each run, Pallas kernels for 4% -> 4%
where the time goes in v7:
time: 52.9 us; the launch traced here: 52.7 us
  starting transfers between devices  29.3 us (55%)
  waiting for transfers between devices  16.5 us (31%)
  Pallas kernels  5.98 us (11%)
  between operations  0.8 us (2%)
    ppermute x12, starting transfers between devices, inner_swap(): return lax.ppermute(x, 'dom', [(i, i ^ s) for i in range(domains)])  14.8 us
    ppermute x8, starting transfers between devices, outer_swap(): return lax.ppermute(x, 'dom', [(i, i ^ t * group) for i in range(domains)])  13.3 us
    ppermute x8, waiting for transfers between devices, outer_swap(): return lax.ppermute(x, 'dom', [(i, i ^ t * group) for i in range(domains)])  7.79 us
    ppermute x12, waiting for transfers between devices, inner_swap(): return lax.ppermute(x, 'dom', [(i, i ^ s) for i in range(domains)])  6.64 us
    pallas_call x2, Pallas kernels, combine(): pl.pallas_call(functools.partial(combine_kernel, mine), out_shape=jax.Sha...  3.05 us
    pallas_call x12, Pallas kernels, call(): pl.pallas_call(kernel, out_shape=[jax.ShapeDtypeStruct(shape, dtype) for...  2.93 us
    ppermute x10, waiting for transfers between devices, rep_swap(): return lax.ppermute(x, 'rep', [(0, 1), (1, 0)])  2.09 us
    ppermute x10, starting transfers between devices, rep_swap(): return lax.ppermute(x, 'rep', [(0, 1), (1, 0)])  1.31 us
  transfers between devices with their start and end apart: 30, of which 15 were waited for; matrix products, arithmetic and copies ran while one was open for 0% of the time, Pallas kernels for 4%

profile of v7, /device:TPU:0, one launch (start us, length us, event | category | flops | bytes accessed | tf_op | source)
XLA Modules:
  0.0 52.7 jit_solution(3487466901984371305)
XLA Ops:
  0.6 1.5 %shard_map.95 = bf16[16,64,128]{2,1,0:T(8,128)(2,1)S(1)} custom-call(s32[64]{0:T(128)} %bitcast.3, s32[64]{0:T(128)} %count_hbm.3, bf16[64,128,128]{2,1,0:T(8,128)(2,1)} %tiles_hbm.3), custom_call_target="tpu_custom_call" | custom-call | flops 1024 | bytes 1024 | tf_op jit(solution)/shard_map/pallas_call | solution.py:71
  2.2 0.5 collective-permute-start
  2.7 1.5 %shard_map.94.own_ref = bf16[16,64,128]{2,1,0:T(8,128)(2,1)S(1)} custom-call(s32[64]{0:T(128)} %bitcast.4, s32[64]{0:T(128)} %count_hbm.3, bf16[64,128,128]{2,1,0:T(8,128)(2,1)} %tiles_hbm.3), custom_call_target="tpu_custom_call" | custom-call | flops 1024 | bytes 1024 | tf_op jit(solution)/shard_map/pallas_call | solution.py:71
  4.2 0.0 copy-start
  4.2 0.0 copy-start.3
  4.3 0.1 shard_map.96
  4.4 3.5 %collective-permute-start.1 = (bf16[512,128]{1,0:T(8,128)(2,1)S(1)}, bf16[512,128]{1,0:T(8,128)(2,1)S(1)}, u32[]{:S(2)}, u32[]{:S(2)}) collective-permute-start(bf16[512,128]{1,0:T(8,128)(2,1)S(1)} %get-tuple-element.29), channel_id=1, source_target_pairs={{0,3},{1,2},{2,1},{3,0},{4,7},{5,6},{6,5},{7,4},{8,11},{9,10},{10,... | collective-permute-start | bytes 393224 | tf_op jit(solution)/shard_map/ppermute | solution.py:248
  7.9 0.5 %collective-permute-start.2 = (bf16[512,128]{1,0:T(8,128)(2,1)S(1)}, bf16[512,128]{1,0:T(8,128)(2,1)S(1)}, u32[]{:S(2)}, u32[]{:S(2)}) collective-permute-start(bf16[512,128]{1,0:T(8,128)(2,1)S(1)} %get-tuple-element.30), channel_id=1, source_target_pairs={{0,1},{1,0},{2,3},{3,2},{4,5},{5,4},{6,7},{7,6},{8,9},{9,8},{10,11... | collective-permute-start | bytes 393224 | tf_op jit(solution)/shard_map/ppermute | solution.py:248
  8.4 0.1 collective-permute-start.6
  8.5 3.0 %collective-permute-start.7 = (bf16[128,256]{1,0:T(8,128)(2,1)S(1)}, bf16[128,256]{1,0:T(8,128)(2,1)S(1)}, u32[]{:S(2)}, u32[]{:S(2)}) collective-permute-start(bf16[128,256]{1,0:T(8,128)(2,1)S(1)} %shard_map.98.refs_0_), channel_id=1, source_target_pairs={{0,8},{1,9},{2,10},{3,11},{4,12},{5,13},{6,14},{7,15},{8,0},{9,1},... | collective-permute-start | bytes 196616 | tf_op jit(solution)/shard_map/ppermute | solution.py:251
  11.6 0.7 %collective-permute-done.1.refs_1_ = bf16[512,128]{1,0:T(8,128)(2,1)S(1)} collective-permute-done((bf16[512,128]{1,0:T(8,128)(2,1)S(1)}, bf16[512,128]{1,0:T(8,128)(2,1)S(1)}, u32[]{:S(2)}, u32[]{:S(2)}) %collective-permute-start.1) | collective-permute-done | bytes 131104 | tf_op jit(solution)/shard_map/ppermute | solution.py:248
  12.2 2.9 %collective-permute-done.2.refs_2_ = bf16[512,128]{1,0:T(8,128)(2,1)S(1)} collective-permute-done((bf16[512,128]{1,0:T(8,128)(2,1)S(1)}, bf16[512,128]{1,0:T(8,128)(2,1)S(1)}, u32[]{:S(2)}, u32[]{:S(2)}) %collective-permute-start.2) | collective-permute-done | bytes 131104 | tf_op jit(solution)/shard_map/ppermute | solution.py:248
  15.1 0.5 collective-permute-start.3
  15.6 0.1 collective-permute-start.8
  15.7 0.8 %collective-permute-done.3.refs_3_ = bf16[256,128]{1,0:T(8,128)(2,1)S(1)} collective-permute-done((bf16[256,128]{1,0:T(8,128)(2,1)S(1)}, bf16[256,128]{1,0:T(8,128)(2,1)S(1)}, u32[]{:S(2)}, u32[]{:S(2)}) %collective-permute-start.3) | collective-permute-done | bytes 65568 | tf_op jit(solution)/shard_map/ppermute | solution.py:245
  16.6 0.4 shard_map.97
  16.9 0.0 collective-permute-done.8.got_ref
  17.0 0.2 shard_map.100
  17.2 3.7 %collective-permute-start.9 = (bf16[128,256]{1,0:T(8,128)(2,1)S(1)}, bf16[128,256]{1,0:T(8,128)(2,1)S(1)}, u32[]{:S(2)}, u32[]{:S(2)}) collective-permute-start(bf16[128,256]{1,0:T(8,128)(2,1)S(1)} %get-tuple-element.36), channel_id=1, source_target_pairs={{0,12},{1,13},{2,14},{3,15},{4,8},{5,9},{6,10},{7,11},{8,4},{9,5},... | collective-permute-start | bytes 196616 | tf_op jit(solution)/shard_map/ppermute | solution.py:251
  20.9 0.8 %collective-permute-start.11 = (bf16[128,256]{1,0:T(8,128)(2,1)S(1)}, bf16[128,256]{1,0:T(8,128)(2,1)S(1)}, u32[]{:S(2)}, u32[]{:S(2)}) collective-permute-start(bf16[128,256]{1,0:T(8,128)(2,1)S(1)} %get-tuple-element.38), channel_id=1, source_target_pairs={{0,4},{1,5},{2,6},{3,7},{4,0},{5,1},{6,2},{7,3},{8,12},{9,13},{10,... | collective-permute-start | bytes 196616 | tf_op jit(solution)/shard_map/ppermute | solution.py:251
  21.7 1.3 %collective-permute-start.19 = (bf16[256,256]{1,0:T(8,128)(2,1)S(1)}, bf16[256,256]{1,0:T(8,128)(2,1)S(1)}, u32[]{:S(2)}, u32[]{:S(2)}) collective-permute-start(bf16[256,256]{1,0:T(8,128)(2,1)S(1)} %shard_map.102.refs_0_), channel_id=1, source_target_pairs={{0,4},{1,5},{2,6},{3,7},{4,0},{5,1},{6,2},{7,3},{8,12},{9,13},{10,... | collective-permute-start | bytes 393224 | tf_op jit(solution)/shard_map/ppermute | solution.py:251
  23.0 0.7 %collective-permute-done.9.refs_1_ = bf16[128,256]{1,0:T(8,128)(2,1)S(1)} collective-permute-done((bf16[128,256]{1,0:T(8,128)(2,1)S(1)}, bf16[128,256]{1,0:T(8,128)(2,1)S(1)}, u32[]{:S(2)}, u32[]{:S(2)}) %collective-permute-start.9) | collective-permute-done | bytes 65568 | tf_op jit(solution)/shard_map/ppermute | solution.py:251
  23.7 3.2 %collective-permute-done.10.refs_2_ = bf16[128,256]{1,0:T(8,128)(2,1)S(1)} collective-permute-done((bf16[128,256]{1,0:T(8,128)(2,1)S(1)}, bf16[128,256]{1,0:T(8,128)(2,1)S(1)}, u32[]{:S(2)}, u32[]{:S(2)}) %collective-permute-start.10) | collective-permute-done | bytes 65568 | tf_op jit(solution)/shard_map/ppermute | solution.py:251
  26.9 0.3 collective-permute-done.11.refs_3_
  27.3 2.3 %collective-permute-start.14 = (bf16[128,256]{1,0:T(8,128)(2,1)S(1)}, bf16[128,256]{1,0:T(8,128)(2,1)S(1)}, u32[]{:S(2)}, u32[]{:S(2)}) collective-permute-start(bf16[128,256]{1,0:T(8,128)(2,1)S(1)} %shard_map.101.refs_0_), channel_id=1, source_target_pairs={{0,12},{1,13},{2,14},{3,15},{4,8},{5,9},{6,10},{7,11},{8,4},{9,5},... | collective-permute-start | bytes 196616 | tf_op jit(solution)/shard_map/ppermute | solution.py:251
  29.6 2.2 %collective-permute-start.12 = (bf16[128,256]{1,0:T(8,128)(2,1)S(1)}, bf16[128,256]{1,0:T(8,128)(2,1)S(1)}, u32[]{:S(2)}, u32[]{:S(2)}) collective-permute-start(bf16[128,256]{1,0:T(8,128)(2,1)S(1)} %shard_map.101.refs_0_), channel_id=1, source_target_pairs={{0,8},{1,9},{2,10},{3,11},{4,12},{5,13},{6,14},{7,15},{8,0},{9,1},... | collective-permute-start | bytes 196616 | tf_op jit(solution)/shard_map/ppermute | solution.py:251
  31.7 1.9 %collective-permute-done.14.refs_3_ = bf16[128,256]{1,0:T(8,128)(2,1)S(1)} collective-permute-done((bf16[128,256]{1,0:T(8,128)(2,1)S(1)}, bf16[128,256]{1,0:T(8,128)(2,1)S(1)}, u32[]{:S(2)}, u32[]{:S(2)}) %collective-permute-start.14) | collective-permute-done | bytes 65568 | tf_op jit(solution)/shard_map/ppermute | solution.py:251
  33.7 1.0 %collective-permute-done.13.refs_2_ = bf16[128,256]{1,0:T(8,128)(2,1)S(1)} collective-permute-done((bf16[128,256]{1,0:T(8,128)(2,1)S(1)}, bf16[128,256]{1,0:T(8,128)(2,1)S(1)}, u32[]{:S(2)}, u32[]{:S(2)}) %collective-permute-start.13) | collective-permute-done | bytes 65568 | tf_op jit(solution)/shard_map/ppermute | solution.py:251
  34.7 0.6 %collective-permute-done.12.refs_1_ = bf16[128,256]{1,0:T(8,128)(2,1)S(1)} collective-permute-done((bf16[128,256]{1,0:T(8,128)(2,1)S(1)}, bf16[128,256]{1,0:T(8,128)(2,1)S(1)}, u32[]{:S(2)}, u32[]{:S(2)}) %collective-permute-start.12) | collective-permute-done | bytes 65568 | tf_op jit(solution)/shard_map/ppermute | solution.py:251
  35.3 0.6 %collective-permute-done.17.refs_6_ = bf16[128,256]{1,0:T(8,128)(2,1)S(1)} collective-permute-done((bf16[128,256]{1,0:T(8,128)(2,1)S(1)}, bf16[128,256]{1,0:T(8,128)(2,1)S(1)}, u32[]{:S(2)}, u32[]{:S(2)}) %collective-permute-start.17) | collective-permute-done | bytes 65568 | tf_op jit(solution)/shard_map/ppermute | solution.py:245
  35.9 0.6 %collective-permute-done.16.refs_5_ = bf16[128,256]{1,0:T(8,128)(2,1)S(1)} collective-permute-done((bf16[128,256]{1,0:T(8,128)(2,1)S(1)}, bf16[128,256]{1,0:T(8,128)(2,1)S(1)}, u32[]{:S(2)}, u32[]{:S(2)}) %collective-permute-start.16) | collective-permute-done | bytes 65568 | tf_op jit(solution)/shard_map/ppermute | solution.py:245
  36.5 0.9 %shard_map.104 = (bf16[128,256]{1,0:T(8,128)(2,1)S(1)}, f32[512,256]{1,0:T(8,128)S(1)}, bf16[512,256]{1,0:T(8,128)(2,1)S(1)}, f32[128,256]{1,0:T(8,128)S(1)}, bf...) custom-call(bf16[128,256]{1,0:T(8,128)(2,1)S(1)} %shard_map.101.refs_0_, ...), custom_call_target="tpu_custom_call" | custom-call | flops 1024 | bytes 1024 | tf_op jit(solution)/shard_map/pallas_call | solution.py:28
  37.4 0.2 collective-permute-start.20
  37.6 1.8 %collective-permute-start.21 = (bf16[128,256]{1,0:T(8,128)(2,1)S(1)}, bf16[128,256]{1,0:T(8,128)(2,1)S(1)}, u32[]{:S(2)}, u32[]{:S(2)}) collective-permute-start(bf16[128,256]{1,0:T(8,128)(2,1)S(1)} %get-tuple-element.43), channel_id=1, source_target_pairs={{0,3},{1,2},{2,1},{3,0},{4,7},{5,6},{6,5},{7,4},{8,11},{9,10},{10,... | collective-permute-start | bytes 196616 | tf_op jit(solution)/shard_map/ppermute | solution.py:248
  39.4 0.5 collective-permute-start.22
  40.0 1.2 %collective-permute-start.23 = (bf16[128,256]{1,0:T(8,128)(2,1)S(1)}, bf16[128,256]{1,0:T(8,128)(2,1)S(1)}, u32[]{:S(2)}, u32[]{:S(2)}) collective-permute-start(bf16[128,256]{1,0:T(8,128)(2,1)S(1)} %get-tuple-element.45), channel_id=1, source_target_pairs={{0,2},{1,3},{2,0},{3,1},{4,6},{5,7},{6,4},{7,5},{8,10},{9,11},{10,... | collective-permute-start | bytes 196616 | tf_op jit(solution)/shard_map/ppermute | solution.py:248
  41.1 0.4 shard_map.105
  41.5 1.5 %collective-permute-start.27 = (bf16[128,256]{1,0:T(8,128)(2,1)S(1)}, bf16[128,256]{1,0:T(8,128)(2,1)S(1)}, u32[]{:S(2)}, u32[]{:S(2)}) collective-permute-start(bf16[128,256]{1,0:T(8,128)(2,1)S(1)} %get-tuple-element.46), channel_id=1, source_target_pairs={{0,1},{1,0},{2,3},{3,2},{4,5},{5,4},{6,7},{7,6},{8,9},{9,8},{10,11... | collective-permute-start | bytes 196616 | tf_op jit(solution)/shard_map/ppermute | solution.py:248
  43.1 0.8 %collective-permute-start.28 = (bf16[128,256]{1,0:T(8,128)(2,1)S(1)}, bf16[128,256]{1,0:T(8,128)(2,1)S(1)}, u32[]{:S(2)}, u32[]{:S(2)}) collective-permute-start(bf16[128,256]{1,0:T(8,128)(2,1)S(1)} %get-tuple-element.47), channel_id=1, source_target_pairs={{0,3},{1,2},{2,1},{3,0},{4,7},{5,6},{6,5},{7,4},{8,11},{9,10},{10,... | collective-permute-start | bytes 196616 | tf_op jit(solution)/shard_map/ppermute | solution.py:248
  43.9 1.2 %collective-permute-start.29 = (bf16[128,256]{1,0:T(8,128)(2,1)S(1)}, bf16[128,256]{1,0:T(8,128)(2,1)S(1)}, u32[]{:S(2)}, u32[]{:S(2)}) collective-permute-start(bf16[128,256]{1,0:T(8,128)(2,1)S(1)} %get-tuple-element.48), channel_id=1, source_target_pairs={{0,2},{1,3},{2,0},{3,1},{4,6},{5,7},{6,4},{7,5},{8,10},{9,11},{10,... | collective-permute-start | bytes 196616 | tf_op jit(solution)/shard_map/ppermute | solution.py:248
  45.1 1.9 %collective-permute-start.26 = (bf16[128,256]{1,0:T(8,128)(2,1)S(1)}, bf16[128,256]{1,0:T(8,128)(2,1)S(1)}, u32[]{:S(2)}, u32[]{:S(2)}) collective-permute-start(bf16[128,256]{1,0:T(8,128)(2,1)S(1)} %shard_map.106.refs_0_), channel_id=1, source_target_pairs={{0,3},{1,2},{2,1},{3,0},{4,7},{5,6},{6,5},{7,4},{8,11},{9,10},{10,... | collective-permute-start | bytes 196616 | tf_op jit(solution)/shard_map/ppermute | solution.py:248
  47.0 0.5 collective-permute-start.25
  47.5 1.2 %collective-permute-start.24 = (bf16[128,256]{1,0:T(8,128)(2,1)S(1)}, bf16[128,256]{1,0:T(8,128)(2,1)S(1)}, u32[]{:S(2)}, u32[]{:S(2)}) collective-permute-start(bf16[128,256]{1,0:T(8,128)(2,1)S(1)} %shard_map.106.refs_0_), channel_id=1, source_target_pairs={{0,2},{1,3},{2,0},{3,1},{4,6},{5,7},{6,4},{7,5},{8,10},{9,11},{10,... | collective-permute-start | bytes 196616 | tf_op jit(solution)/shard_map/ppermute | solution.py:248
  48.7 0.2 collective-permute-done.28.refs_6_
  48.9 1.9 %collective-permute-done.29.refs_7_ = bf16[128,256]{1,0:T(8,128)(2,1)S(1)} collective-permute-done((bf16[128,256]{1,0:T(8,128)(2,1)S(1)}, bf16[128,256]{1,0:T(8,128)(2,1)S(1)}, u32[]{:S(2)}, u32[]{:S(2)}) %collective-permute-start.29) | collective-permute-done | bytes 65568 | tf_op jit(solution)/shard_map/ppermute | solution.py:248
  50.8 0.4 collective-permute-done.25.refs_2_
  51.3 0.5 collective-permute-done.24.refs_1_
  51.8 0.9 %shard_map.107 = (f32[512,256]{1,0:T(8,128)}, bf16[128,256]{1,0:T(8,128)(2,1)}, bf16[128,256]{1,0:T(8,128)(2,1)}) custom-call(bf16[128,256]{1,0:T(8,128)(2,1)S(1)} %shard_map.106.refs_0_, bf16[128,256]{1,0:T(8,128)(2,1)S(1)} %collective-permute-done.24.refs_1_, bf16[128,256]{1,0:T(8,128)(2,1)S(1)} %collective-permute-done.25.refs_2_, ...), custom_call_target="tpu_custom_call" | custom-call | flops 1024 | bytes 1024 | tf_op jit(solution)/shard_map/pallas_call | solution.py:28
  (34 shorter events, 0.2 us)
Async XLA Ops:
  0.6 3.6 %copy-start.1 = (bf16[128,512]{1,0:T(8,128)(2,1)S(1)}, bf16[128,512]{1,0:T(8,128)(2,1)}, u32[]{:S(2)}) copy-start(bf16[128,512]{1,0:T(8,128)(2,1)} %refs_6_.1) | copy-start | bytes 393220
  2.2 6.3 %copy-start.2 = (bf16[128,512]{1,0:T(8,128)(2,1)S(1)}, bf16[128,512]{1,0:T(8,128)(2,1)}, u32[]{:S(2)}) copy-start(bf16[128,512]{1,0:T(8,128)(2,1)} %whole_ref.1) | copy-start | bytes 393220
  2.2 2.0 %collective-permute-start = (bf16[16,64,128]{2,1,0:T(8,128)(2,1)S(1)}, bf16[16,64,128]{2,1,0:T(8,128)(2,1)S(1)}, u32[]{:S(2)}, u32[]{:S(2)}) collective-permute-start(bf16[16,64,128]{2,1,0:T(8,128)(2,1)S(1)} %shard_map.95), channel_id=1, source_target_pairs={{0,16},{16,0},{1,17},{17,1},{2,18},{18,2},{3,19},{19,3},{4,20},{20... | collective-permute-start | bytes 786440 | tf_op jit(solution)/shard_map/ppermute | solution.py:245
  4.2 32.3 %copy-start = (bf16[512,512]{1,0:T(8,128)(2,1)S(1)}, bf16[512,512]{1,0:T(8,128)(2,1)}, u32[]{:S(2)}) copy-start(bf16[512,512]{1,0:T(8,128)(2,1)} %refs_9_.1) | copy-start | bytes 1572868
  4.2 32.3 %copy-start.3 = (f32[512]{0:T(512)S(1)}, f32[512]{0:T(512)}, u32[]{:S(2)}) copy-start(f32[512]{0:T(512)} %param.12) | copy-start | bytes 6148
  4.4 7.9 %collective-permute-start.1 = (bf16[512,128]{1,0:T(8,128)(2,1)S(1)}, bf16[512,128]{1,0:T(8,128)(2,1)S(1)}, u32[]{:S(2)}, u32[]{:S(2)}) collective-permute-start(bf16[512,128]{1,0:T(8,128)(2,1)S(1)} %get-tuple-element.29), channel_id=1, source_target_pairs={{0,3},{1,2},{2,1},{3,0},{4,7},{5,6},{6,5},{7,4},{8,11},{9,10},{10,... | collective-permute-start | bytes 393224 | tf_op jit(solution)/shard_map/ppermute | solution.py:248
  7.9 7.2 %collective-permute-start.2 = (bf16[512,128]{1,0:T(8,128)(2,1)S(1)}, bf16[512,128]{1,0:T(8,128)(2,1)S(1)}, u32[]{:S(2)}, u32[]{:S(2)}) collective-permute-start(bf16[512,128]{1,0:T(8,128)(2,1)S(1)} %get-tuple-element.30), channel_id=1, source_target_pairs={{0,1},{1,0},{2,3},{3,2},{4,5},{5,4},{6,7},{7,6},{8,9},{9,8},{10,11... | collective-permute-start | bytes 393224 | tf_op jit(solution)/shard_map/ppermute | solution.py:248
  8.4 7.2 %collective-permute-start.6 = (bf16[512,128]{1,0:T(8,128)(2,1)S(1)}, bf16[512,128]{1,0:T(8,128)(2,1)S(1)}, u32[]{:S(2)}, u32[]{:S(2)}) collective-permute-start(bf16[512,128]{1,0:T(8,128)(2,1)S(1)} %get-tuple-element.32), channel_id=1, source_target_pairs={{0,2},{1,3},{2,0},{3,1},{4,6},{5,7},{6,4},{7,5},{8,10},{9,11},{10,... | collective-permute-start | bytes 393224 | tf_op jit(solution)/shard_map/ppermute | solution.py:248
  8.5 7.1 %collective-permute-start.7 = (bf16[128,256]{1,0:T(8,128)(2,1)S(1)}, bf16[128,256]{1,0:T(8,128)(2,1)S(1)}, u32[]{:S(2)}, u32[]{:S(2)}) collective-permute-start(bf16[128,256]{1,0:T(8,128)(2,1)S(1)} %shard_map.98.refs_0_), channel_id=1, source_target_pairs={{0,8},{1,9},{2,10},{3,11},{4,12},{5,13},{6,14},{7,15},{8,0},{9,1},... | collective-permute-start | bytes 196616 | tf_op jit(solution)/shard_map/ppermute | solution.py:251
  12.2 4.3 %collective-permute-start.4 = (bf16[512,128]{1,0:T(8,128)(2,1)S(1)}, bf16[512,128]{1,0:T(8,128)(2,1)S(1)}, u32[]{:S(2)}, u32[]{:S(2)}) collective-permute-start(bf16[512,128]{1,0:T(8,128)(2,1)S(1)} %collective-permute-done.1.refs_1_), channel_id=1, source_target_pairs={{0,16},{16,0},{1,17},{17,1},{2,18},{18,2},{3,19},{19,3},{4,20},{20... | collective-permute-start | bytes 393224 | tf_op jit(solution)/shard_map/ppermute | solution.py:245
  15.1 1.4 %collective-permute-start.5 = (bf16[512,128]{1,0:T(8,128)(2,1)S(1)}, bf16[512,128]{1,0:T(8,128)(2,1)S(1)}, u32[]{:S(2)}, u32[]{:S(2)}) collective-permute-start(bf16[512,128]{1,0:T(8,128)(2,1)S(1)} %collective-permute-done.2.refs_2_), channel_id=1, source_target_pairs={{0,16},{16,0},{1,17},{17,1},{2,18},{18,2},{3,19},{19,3},{4,20},{20... | collective-permute-start | bytes 393224 | tf_op jit(solution)/shard_map/ppermute | solution.py:245
  15.1 1.4 %collective-permute-start.3 = (bf16[256,128]{1,0:T(8,128)(2,1)S(1)}, bf16[256,128]{1,0:T(8,128)(2,1)S(1)}, u32[]{:S(2)}, u32[]{:S(2)}) collective-permute-start(bf16[256,128]{1,0:T(8,128)(2,1)S(1)} %get-tuple-element.28.refs_0_), channel_id=1, source_target_pairs={{0,16},{16,0},{1,17},{17,1},{2,18},{18,2},{3,19},{19,3},{4,20},{20... | collective-permute-start | bytes 196616 | tf_op jit(solution)/shard_map/ppermute | solution.py:245
  15.6 1.3 %collective-permute-start.8 = (bf16[256,128]{1,0:T(8,128)(2,1)S(1)}, bf16[256,128]{1,0:T(8,128)(2,1)S(1)}, u32[]{:S(2)}, u32[]{:S(2)}) collective-permute-start(bf16[256,128]{1,0:T(8,128)(2,1)S(1)} %shard_map.99), channel_id=1, source_target_pairs={{0,16},{16,0},{1,17},{17,1},{2,18},{18,2},{3,19},{19,3},{4,20},{20... | collective-permute-start | bytes 196616 | tf_op jit(solution)/shard_map/ppermute | solution.py:245
  17.2 6.5 %collective-permute-start.9 = (bf16[128,256]{1,0:T(8,128)(2,1)S(1)}, bf16[128,256]{1,0:T(8,128)(2,1)S(1)}, u32[]{:S(2)}, u32[]{:S(2)}) collective-permute-start(bf16[128,256]{1,0:T(8,128)(2,1)S(1)} %get-tuple-element.36), channel_id=1, source_target_pairs={{0,12},{1,13},{2,14},{3,15},{4,8},{5,9},{6,10},{7,11},{8,4},{9,5},... | collective-permute-start | bytes 196616 | tf_op jit(solution)/shard_map/ppermute | solution.py:251
  20.9 6.0 %collective-permute-start.10 = (bf16[128,256]{1,0:T(8,128)(2,1)S(1)}, bf16[128,256]{1,0:T(8,128)(2,1)S(1)}, u32[]{:S(2)}, u32[]{:S(2)}) collective-permute-start(bf16[128,256]{1,0:T(8,128)(2,1)S(1)} %get-tuple-element.37), channel_id=1, source_target_pairs={{0,8},{1,9},{2,10},{3,11},{4,12},{5,13},{6,14},{7,15},{8,0},{9,1},... | collective-permute-start | bytes 196616 | tf_op jit(solution)/shard_map/ppermute | solution.py:251
  20.9 6.4 %collective-permute-start.11 = (bf16[128,256]{1,0:T(8,128)(2,1)S(1)}, bf16[128,256]{1,0:T(8,128)(2,1)S(1)}, u32[]{:S(2)}, u32[]{:S(2)}) collective-permute-start(bf16[128,256]{1,0:T(8,128)(2,1)S(1)} %get-tuple-element.38), channel_id=1, source_target_pairs={{0,4},{1,5},{2,6},{3,7},{4,0},{5,1},{6,2},{7,3},{8,12},{9,13},{10,... | collective-permute-start | bytes 196616 | tf_op jit(solution)/shard_map/ppermute | solution.py:251
  21.7 13.6 %collective-permute-start.19 = (bf16[256,256]{1,0:T(8,128)(2,1)S(1)}, bf16[256,256]{1,0:T(8,128)(2,1)S(1)}, u32[]{:S(2)}, u32[]{:S(2)}) collective-permute-start(bf16[256,256]{1,0:T(8,128)(2,1)S(1)} %shard_map.102.refs_0_), channel_id=1, source_target_pairs={{0,4},{1,5},{2,6},{3,7},{4,0},{5,1},{6,2},{7,3},{8,12},{9,13},{10,... | collective-permute-start | bytes 393224 | tf_op jit(solution)/shard_map/ppermute | solution.py:251
  27.3 6.4 %collective-permute-start.14 = (bf16[128,256]{1,0:T(8,128)(2,1)S(1)}, bf16[128,256]{1,0:T(8,128)(2,1)S(1)}, u32[]{:S(2)}, u32[]{:S(2)}) collective-permute-start(bf16[128,256]{1,0:T(8,128)(2,1)S(1)} %shard_map.101.refs_0_), channel_id=1, source_target_pairs={{0,12},{1,13},{2,14},{3,15},{4,8},{5,9},{6,10},{7,11},{8,4},{9,5},... | collective-permute-start | bytes 196616 | tf_op jit(solution)/shard_map/ppermute | solution.py:251
  29.6 5.1 %collective-permute-start.13 = (bf16[128,256]{1,0:T(8,128)(2,1)S(1)}, bf16[128,256]{1,0:T(8,128)(2,1)S(1)}, u32[]{:S(2)}, u32[]{:S(2)}) collective-permute-start(bf16[128,256]{1,0:T(8,128)(2,1)S(1)} %shard_map.101.refs_0_), channel_id=1, source_target_pairs={{0,4},{1,5},{2,6},{3,7},{4,0},{5,1},{6,2},{7,3},{8,12},{9,13},{10,... | collective-permute-start | bytes 196616 | tf_op jit(solution)/shard_map/ppermute | solution.py:251
  29.6 5.7 %collective-permute-start.12 = (bf16[128,256]{1,0:T(8,128)(2,1)S(1)}, bf16[128,256]{1,0:T(8,128)(2,1)S(1)}, u32[]{:S(2)}, u32[]{:S(2)}) collective-permute-start(bf16[128,256]{1,0:T(8,128)(2,1)S(1)} %shard_map.101.refs_0_), channel_id=1, source_target_pairs={{0,8},{1,9},{2,10},{3,11},{4,12},{5,13},{6,14},{7,15},{8,0},{9,1},... | collective-permute-start | bytes 196616 | tf_op jit(solution)/shard_map/ppermute | solution.py:251
  31.7 3.6 %collective-permute-start.15 = (bf16[128,256]{1,0:T(8,128)(2,1)S(1)}, bf16[128,256]{1,0:T(8,128)(2,1)S(1)}, u32[]{:S(2)}, u32[]{:S(2)}) collective-permute-start(bf16[128,256]{1,0:T(8,128)(2,1)S(1)} %shard_map.101.refs_0_), channel_id=1, source_target_pairs={{0,16},{16,0},{1,17},{17,1},{2,18},{18,2},{3,19},{19,3},{4,20},{20... | collective-permute-start | bytes 196616 | tf_op jit(solution)/shard_map/ppermute | solution.py:245
  33.7 1.6 %collective-permute-start.18 = (bf16[128,256]{1,0:T(8,128)(2,1)S(1)}, bf16[128,256]{1,0:T(8,128)(2,1)S(1)}, u32[]{:S(2)}, u32[]{:S(2)}) collective-permute-start(bf16[128,256]{1,0:T(8,128)(2,1)S(1)} %collective-permute-done.14.refs_3_), channel_id=1, source_target_pairs={{0,16},{16,0},{1,17},{17,1},{2,18},{18,2},{3,19},{19,3},{4,20},{20... | collective-permute-start | bytes 196616 | tf_op jit(solution)/shard_map/ppermute | solution.py:245
  34.6 1.3 %collective-permute-start.17 = (bf16[128,256]{1,0:T(8,128)(2,1)S(1)}, bf16[128,256]{1,0:T(8,128)(2,1)S(1)}, u32[]{:S(2)}, u32[]{:S(2)}) collective-permute-start(bf16[128,256]{1,0:T(8,128)(2,1)S(1)} %collective-permute-done.13.refs_2_), channel_id=1, source_target_pairs={{0,16},{16,0},{1,17},{17,1},{2,18},{18,2},{3,19},{19,3},{4,20},{20... | collective-permute-start | bytes 196616 | tf_op jit(solution)/shard_map/ppermute | solution.py:245
  35.3 1.3 %collective-permute-start.16 = (bf16[128,256]{1,0:T(8,128)(2,1)S(1)}, bf16[128,256]{1,0:T(8,128)(2,1)S(1)}, u32[]{:S(2)}, u32[]{:S(2)}) collective-permute-start(bf16[128,256]{1,0:T(8,128)(2,1)S(1)} %collective-permute-done.12.refs_1_), channel_id=1, source_target_pairs={{0,16},{16,0},{1,17},{17,1},{2,18},{18,2},{3,19},{19,3},{4,20},{20... | collective-permute-start | bytes 196616 | tf_op jit(solution)/shard_map/ppermute | solution.py:245
  37.4 3.7 %collective-permute-start.20 = (bf16[512,256]{1,0:T(8,128)(2,1)S(1)}, bf16[512,256]{1,0:T(8,128)(2,1)S(1)}, u32[]{:S(2)}, u32[]{:S(2)}) collective-permute-start(bf16[512,256]{1,0:T(8,128)(2,1)S(1)} %get-tuple-element.40), channel_id=1, source_target_pairs={{0,16},{16,0},{1,17},{17,1},{2,18},{18,2},{3,19},{19,3},{4,20},{20... | collective-permute-start | bytes 786440 | tf_op jit(solution)/shard_map/ppermute | solution.py:245
  37.6 6.3 %collective-permute-start.21 = (bf16[128,256]{1,0:T(8,128)(2,1)S(1)}, bf16[128,256]{1,0:T(8,128)(2,1)S(1)}, u32[]{:S(2)}, u32[]{:S(2)}) collective-permute-start(bf16[128,256]{1,0:T(8,128)(2,1)S(1)} %get-tuple-element.43), channel_id=1, source_target_pairs={{0,3},{1,2},{2,1},{3,0},{4,7},{5,6},{6,5},{7,4},{8,11},{9,10},{10,... | collective-permute-start | bytes 196616 | tf_op jit(solution)/shard_map/ppermute | solution.py:248
  39.4 5.6 %collective-permute-start.22 = (bf16[128,256]{1,0:T(8,128)(2,1)S(1)}, bf16[128,256]{1,0:T(8,128)(2,1)S(1)}, u32[]{:S(2)}, u32[]{:S(2)}) collective-permute-start(bf16[128,256]{1,0:T(8,128)(2,1)S(1)} %get-tuple-element.44), channel_id=1, source_target_pairs={{0,1},{1,0},{2,3},{3,2},{4,5},{5,4},{6,7},{7,6},{8,9},{9,8},{10,11... | collective-permute-start | bytes 196616 | tf_op jit(solution)/shard_map/ppermute | solution.py:248
  40.0 5.1 %collective-permute-start.23 = (bf16[128,256]{1,0:T(8,128)(2,1)S(1)}, bf16[128,256]{1,0:T(8,128)(2,1)S(1)}, u32[]{:S(2)}, u32[]{:S(2)}) collective-permute-start(bf16[128,256]{1,0:T(8,128)(2,1)S(1)} %get-tuple-element.45), channel_id=1, source_target_pairs={{0,2},{1,3},{2,0},{3,1},{4,6},{5,7},{6,4},{7,5},{8,10},{9,11},{10,... | collective-permute-start | bytes 196616 | tf_op jit(solution)/shard_map/ppermute | solution.py:248
  41.5 6.0 %collective-permute-start.27 = (bf16[128,256]{1,0:T(8,128)(2,1)S(1)}, bf16[128,256]{1,0:T(8,128)(2,1)S(1)}, u32[]{:S(2)}, u32[]{:S(2)}) collective-permute-start(bf16[128,256]{1,0:T(8,128)(2,1)S(1)} %get-tuple-element.46), channel_id=1, source_target_pairs={{0,1},{1,0},{2,3},{3,2},{4,5},{5,4},{6,7},{7,6},{8,9},{9,8},{10,11... | collective-permute-start | bytes 196616 | tf_op jit(solution)/shard_map/ppermute | solution.py:248
  43.1 5.9 %collective-permute-start.28 = (bf16[128,256]{1,0:T(8,128)(2,1)S(1)}, bf16[128,256]{1,0:T(8,128)(2,1)S(1)}, u32[]{:S(2)}, u32[]{:S(2)}) collective-permute-start(bf16[128,256]{1,0:T(8,128)(2,1)S(1)} %get-tuple-element.47), channel_id=1, source_target_pairs={{0,3},{1,2},{2,1},{3,0},{4,7},{5,6},{6,5},{7,4},{8,11},{9,10},{10,... | collective-permute-start | bytes 196616 | tf_op jit(solution)/shard_map/ppermute | solution.py:248
  43.9 6.9 %collective-permute-start.29 = (bf16[128,256]{1,0:T(8,128)(2,1)S(1)}, bf16[128,256]{1,0:T(8,128)(2,1)S(1)}, u32[]{:S(2)}, u32[]{:S(2)}) collective-permute-start(bf16[128,256]{1,0:T(8,128)(2,1)S(1)} %get-tuple-element.48), channel_id=1, source_target_pairs={{0,2},{1,3},{2,0},{3,1},{4,6},{5,7},{6,4},{7,5},{8,10},{9,11},{10,... | collective-permute-start | bytes 196616 | tf_op jit(solution)/shard_map/ppermute | solution.py:248
  45.1 5.7 %collective-permute-start.26 = (bf16[128,256]{1,0:T(8,128)(2,1)S(1)}, bf16[128,256]{1,0:T(8,128)(2,1)S(1)}, u32[]{:S(2)}, u32[]{:S(2)}) collective-permute-start(bf16[128,256]{1,0:T(8,128)(2,1)S(1)} %shard_map.106.refs_0_), channel_id=1, source_target_pairs={{0,3},{1,2},{2,1},{3,0},{4,7},{5,6},{6,5},{7,4},{8,11},{9,10},{10,... | collective-permute-start | bytes 196616 | tf_op jit(solution)/shard_map/ppermute | solution.py:248
  47.0 4.3 %collective-permute-start.25 = (bf16[128,256]{1,0:T(8,128)(2,1)S(1)}, bf16[128,256]{1,0:T(8,128)(2,1)S(1)}, u32[]{:S(2)}, u32[]{:S(2)}) collective-permute-start(bf16[128,256]{1,0:T(8,128)(2,1)S(1)} %shard_map.106.refs_0_), channel_id=1, source_target_pairs={{0,1},{1,0},{2,3},{3,2},{4,5},{5,4},{6,7},{7,6},{8,9},{9,8},{10,11... | collective-permute-start | bytes 196616 | tf_op jit(solution)/shard_map/ppermute | solution.py:248
  47.5 4.3 %collective-permute-start.24 = (bf16[128,256]{1,0:T(8,128)(2,1)S(1)}, bf16[128,256]{1,0:T(8,128)(2,1)S(1)}, u32[]{:S(2)}, u32[]{:S(2)}) collective-permute-start(bf16[128,256]{1,0:T(8,128)(2,1)S(1)} %shard_map.106.refs_0_), channel_id=1, source_target_pairs={{0,2},{1,3},{2,0},{3,1},{4,6},{5,7},{6,4},{7,5},{8,10},{9,11},{10,... | collective-permute-start | bytes 196616 | tf_op jit(solution)/shard_map/ppermute | solution.py:248
